TPU v7x, 512 devices: a whole 4x8x8 slice. The times are simulated.
512 devices in a mesh: dp: 32 (over z, x), tensor: 16 (over y, core).
Axes of the slice: x: 4, y: 8, z: 8, core: 2. Of those that a mesh axis runs over, the one named last changes fastest.
Arguments:
- tokens: bfloat16 [16384, 8192], P('dp', 'tensor'), may hold values from -6 to 6
- key_value_weight: bfloat16 [8192, 2048], P('tensor'), may hold values from -0.0625 to 0.0625
- adapter_down_weight: bfloat16 [96, 64, 8192], P('dp', None, 'tensor'), may hold values from -0.0625 to 0.0625
- adapter_up_weight: bfloat16 [96, 64, 2048], P('dp', None, 'tensor'), may hold values from -0.75 to 0.75
- cotangent: bfloat16 [16384, 2048], P('dp', 'tensor'), may hold values from -3 to 3
- sequence_adapter_index: int32 [512], replicated, may hold values from 0 to 95, as said below
- adapter_storage_row: int32 [96], replicated, may hold values from 0 to 95, as said below
Outputs:
- key_value_output: bfloat16 [16384, 2048], P('dp', 'tensor')
- token_gradient: bfloat16 [16384, 8192], P('dp', 'tensor')
- grad_down: float32 [96, 64, 8192], P('dp', None, 'tensor')
- grad_up: float32 [96, 64, 2048], P('dp', None, 'tensor')
Inputs may be any that keep to these rules, and one draw needn't show every extreme that they name: Each value appears once: adapter a is held at row adapter_storage_row[a] of adapter_down_weight, adapter_up_weight, grad_down and grad_up, on index adapter_storage_row[a] // 3 of dp. `sequence_adapter_index`: the 16 sequences i that share one value of i // 16 use adapters held on 16 different indices of dp.
All inputs are finite; a program needn't handle non-finite values.
Results may differ from a plain program's by a relative error of at most 0.02.
Values may be sent and summed in bfloat16 or wider, within the bound.
No kernel may reach another device: no remote copies, remote signals or barrier semaphores. Data moves between devices by JAX's collectives and lax.ppermute only.
A program may use at most 64 MiB of HBM per device.

v0:
```python
import jax
import jax.numpy as jnp
from jax import lax
from jax.sharding import PartitionSpec as P

adapter_scale = 0.25


def gathered_total(value, axis):
    return lax.all_gather(value, axis).astype(jnp.float32).sum(0)


def cut_along(value, dim, length):
    before, after = (value.shape[:dim], value.shape[dim + 1 :])
    return jnp.moveaxis(value.reshape(*before, length, -1, *after), dim, 0)


def sent_and_summed(value, axis, dim):
    pieces = cut_along(value, dim, lax.axis_size(axis))
    arrived = lax.all_to_all(pieces, axis, split_axis=0, concat_axis=0, tiled=True)
    return arrived.astype(jnp.float32).sum(axis=0)


def on_device(
    tokens,
    key_value_weight,
    adapter_down_weight,
    adapter_up_weight,
    cotangent,
    sequence_adapter_index,
    adapter_storage_row,
):
    dp_count = lax.axis_size("dp")
    my_index = lax.axis_index("dp")
    resident_adapters = adapter_down_weight.shape[0]
    rank_span = adapter_down_weight.shape[1]
    block_span = adapter_down_weight.shape[2]
    output_block = adapter_up_weight.shape[2]
    token_row_matrix = tokens.shape[0]
    adapters = adapter_storage_row.shape[0]
    seq_local = sequence_adapter_index.shape[0] // dp_count
    seq_length = token_row_matrix // seq_local
    adapter_codes = jnp.arange(adapters, dtype=jnp.int32)
    matches = sequence_adapter_index[:, None] == adapter_codes[None, :]
    seq_rows = jnp.sum(jnp.where(matches, adapter_storage_row[None, :], 0), axis=1)
    my_rows = lax.dynamic_slice_in_dim(seq_rows, my_index * seq_local, seq_local)
    my_owners = my_rows // resident_adapters
    owner_codes = jnp.arange(dp_count, dtype=jnp.int32)
    from_owner = (my_owners[:, None] == owner_codes[None, :]).astype(jnp.bfloat16)
    reader_rows = seq_rows.reshape(dp_count, seq_local)
    local_codes = jnp.arange(resident_adapters, dtype=jnp.int32) + my_index * resident_adapters
    wanted = (reader_rows[:, :, None] == local_codes[None, None, :]).astype(jnp.float32)
    serve_table = jnp.sum(wanted, axis=1).astype(jnp.bfloat16)
    usage_count = jnp.sum(wanted, axis=(0, 1))
    inverse_use = 1.0 / jnp.maximum(usage_count, 1.0)
    down_flattened = adapter_down_weight.reshape(resident_adapters, rank_span * block_span)
    up_flattened = adapter_up_weight.reshape(resident_adapters, rank_span * output_block)
    send_down = jnp.dot(serve_table, down_flattened, preferred_element_type=jnp.float32).astype(
        jnp.bfloat16
    )
    send_up = jnp.dot(serve_table, up_flattened, preferred_element_type=jnp.float32).astype(
        jnp.bfloat16
    )
    came_down, came_up = (
        lax.all_to_all(send_down, "dp", split_axis=0, concat_axis=0, tiled=True),
        lax.all_to_all(send_up, "dp", split_axis=0, concat_axis=0, tiled=True),
    )
    got_down = jnp.dot(from_owner, came_down, preferred_element_type=jnp.float32)
    got_up = jnp.dot(from_owner, came_up, preferred_element_type=jnp.float32)
    storage_down = got_down.astype(jnp.bfloat16).reshape(seq_local, rank_span, block_span)
    storage_up = got_up.astype(jnp.bfloat16).reshape(seq_local, rank_span, output_block)
    token_sequences = tokens.reshape(seq_local, seq_length, block_span)
    cot_seqs = cotangent.reshape(seq_local, seq_length, output_block)
    inner_part = jnp.einsum(
        "jby,jcy->jbc", token_sequences, storage_down, preferred_element_type=jnp.float32
    )
    back_part = jnp.einsum("slo,sro->slr", cot_seqs, storage_up, preferred_element_type=jnp.float32)
    joined = gathered_total(
        jnp.concatenate([inner_part, back_part], axis=2).astype(jnp.bfloat16), "tensor"
    ).astype(jnp.float32)
    middle_round = joined[:, :, :rank_span].astype(jnp.bfloat16)
    backward_round = joined[:, :, rank_span:].astype(jnp.bfloat16)
    partial_value = jnp.dot(tokens, key_value_weight, preferred_element_type=jnp.float32)
    frozen_backbone = sent_and_summed(partial_value.astype(jnp.bfloat16), "tensor", 1)
    adapter_output = jnp.einsum(
        "ivq,iqg->ivg", middle_round, storage_up, preferred_element_type=jnp.float32
    )
    key_value_output = (
        frozen_backbone + adapter_scale * adapter_output.reshape(token_row_matrix, output_block)
    ).astype(jnp.bfloat16)
    base_gradient = lax.dot_general(
        lax.all_gather(cotangent, "tensor", axis=1, tiled=True),
        key_value_weight,
        (((1,), (1,)), ((), ())),
        preferred_element_type=jnp.float32,
    )
    adapter_gradient = jnp.einsum(
        "cun,cny->cuy", backward_round, storage_down, preferred_element_type=jnp.float32
    )
    token_gradient = (
        base_gradient + adapter_scale * adapter_gradient.reshape(token_row_matrix, block_span)
    ).astype(jnp.bfloat16)
    down_term = (
        adapter_scale
        * jnp.einsum(
            "cfj,cfh->cjh", backward_round, token_sequences, preferred_element_type=jnp.float32
        )
    ).astype(jnp.bfloat16)
    up_term = (
        adapter_scale
        * jnp.einsum("slr,slo->sro", middle_round, cot_seqs, preferred_element_type=jnp.float32)
    ).astype(jnp.bfloat16)
    to_owner = from_owner.T
    ship_down = jnp.dot(
        to_owner, down_term.reshape(seq_local, -1), preferred_element_type=jnp.float32
    ).astype(jnp.bfloat16)
    ship_up = jnp.dot(
        to_owner, up_term.reshape(seq_local, -1), preferred_element_type=jnp.float32
    ).astype(jnp.bfloat16)
    back_down, back_up = (
        lax.all_to_all(ship_down, "dp", split_axis=0, concat_axis=0, tiled=True),
        lax.all_to_all(ship_up, "dp", split_axis=0, concat_axis=0, tiled=True),
    )
    serve_turned = serve_table.T
    grad_down = (
        jnp.dot(serve_turned, back_down, preferred_element_type=jnp.float32) * inverse_use[:, None]
    )
    grad_up = (
        jnp.dot(serve_turned, back_up, preferred_element_type=jnp.float32) * inverse_use[:, None]
    )
    grad_down = grad_down.reshape(resident_adapters, rank_span, block_span)
    grad_up = grad_up.reshape(resident_adapters, rank_span, output_block)
    return (key_value_output, token_gradient, grad_down, grad_up)


def solution(mesh):
    in_specs = (
        P("dp", "tensor"),
        P("tensor", None),
        P("dp", None, "tensor"),
        P("dp", None, "tensor"),
        P("dp", "tensor"),
        P(),
        P(),
    )
    out_specs = (
        P("dp", "tensor"),
        P("dp", "tensor"),
        P("dp", None, "tensor"),
        P("dp", None, "tensor"),
    )
    return jax.shard_map(
        on_device, mesh=mesh, in_specs=in_specs, out_specs=out_specs, check_vma=False
    )
```

profile of v0, /device:TPU:24, one launch (start us, length us, event | category | flops | bytes accessed | tf_op | source)
XLA Modules:
  0.0 297.3 jit_solution(2475872210258353637)
XLA Ops:
  7.2 0.0 copy-start
  7.2 1.0 select_reduce_fusion
  8.2 0.1 eq.47
  8.2 0.1 copy.22
  8.3 0.2 convert_reduce_fusion.1
  8.5 1.2 fusion.2
  9.7 0.5 broadcast.29
  10.2 1.0 reduce.1
  11.2 1.2 reshape.109
  12.4 13.2 %all-to-all-start.2 = ((bf16[32,2,4096]{2,1,0:T(2,128)(2,1)}), bf16[32,2,4096]{2,1,0:T(2,128)(2,1)S(1)}, u32[]{:S(2)}, u32[]{:S(2)}) async-start(bf16[32,2,4096]{2,1,0:T(2,128)(2,1)} %reshape.109), calls=%async_computation.2 | async-start | bytes 1048576 | tf_op jit(solution)/shard_map/all_to_all | solution.py:66
  25.6 0.2 copy.32
  25.7 2.1 fusion
  27.8 4.6 %reduce.2 = bf16[32,32768]{1,0:T(8,128)(2,1)} reduce(bf16[32,1,32768]{2,0,1:T(8,128)(2,1)} %fusion, bf16[]{:T(256)} %broadcast.29), dimensions={1}, to_apply=%copy.23.reduce_sub_computation | reduce | bytes 4194306 | tf_op jit(solution)/shard_map/all_to_all | solution.py:65
  32.4 4.5 %reshape.111 = bf16[32,2,16384]{2,1,0:T(2,128)(2,1)} reshape(bf16[32,32768]{1,0:T(8,128)(2,1)} %reduce.2) | data formatting | bytes 4194304
  36.9 6.4 %all-to-all-done.2 = bf16[32,2,4096]{2,1,0:T(2,128)(2,1)S(1)} async-done(((bf16[32,2,4096]{2,1,0:T(2,128)(2,1)}), bf16[32,2,4096]{2,1,0:T(2,128)(2,1)S(1)}, u32[]{:S(2)}, u32[]{:S(2)}) %all-to-all-start.2) | async-done | bytes 524320 | tf_op jit(solution)/shard_map/all_to_all | solution.py:66
  43.3 4.8 %all-to-all-start.1 = ((bf16[32,2,16384]{2,1,0:T(2,128)(2,1)}), bf16[32,2,16384]{2,1,0:T(2,128)(2,1)}, u32[]{:S(2)}, u32[]{:S(2)}) async-start(bf16[32,2,16384]{2,1,0:T(2,128)(2,1)} %reshape.111), calls=%async_computation.1 | async-start | bytes 4194304 | tf_op jit(solution)/shard_map/all_to_all | solution.py:65
  48.1 0.0 copy-start.3
  48.1 0.0 all-gather.3.cloned.1.call-start
  48.2 0.1 and_select_fusion
  48.2 3.6 %reshape.110 = bf16[32,1,8192]{2,1,0:T(2,128)(2,1)S(1)} reshape(bf16[32,2,4096]{2,1,0:T(2,128)(2,1)} %copy-done.1) | data formatting | bytes 1048576
  51.9 0.7 fusion.11
  52.5 0.1 copy.35
  52.6 0.9 fusion.12
  53.5 43.8 %all-to-all-done.1 = bf16[32,2,16384]{2,1,0:T(2,128)(2,1)} async-done(((bf16[32,2,16384]{2,1,0:T(2,128)(2,1)}), bf16[32,2,16384]{2,1,0:T(2,128)(2,1)}, u32[]{:S(2)}, u32[]{:S(2)}) %all-to-all-start.1) | async-done | bytes 2097184 | tf_op jit(solution)/shard_map/all_to_all | solution.py:65
  97.3 10.5 %reshape.112 = bf16[32,1,32768]{2,1,0:T(2,128)(2,1)} reshape(bf16[32,2,16384]{2,1,0:T(2,128)(2,1)} %all-to-all-done.1) | data formatting | bytes 4194304
  107.8 4.6 %convolution_convert_fusion.2 = bf16[16,32768]{1,0:T(8,128)(2,1)S(1)} fusion(bf16[32,1,32768]{2,1,0:T(2,128)(2,1)} %reshape.112, s32[16]{0:T(128)S(1)} %and_select_fusion), kind=kOutput, calls=%fused_computation.4 | convolution fusion | flops 34079232 | bytes 3145792 | tf_op jit(solution)/shard_map/dot_general | solution.py:68
  112.3 0.3 copy.33
  112.7 0.4 fusion.14
  113.1 0.2 copy-done.4
  113.2 0.8 pad_maximum_fusion
  114.0 0.0 all-gather.3.cloned.1.call-update
  114.0 2.3 fusion.8
  116.3 1.8 copy.67
  118.2 7.3 %all-to-all-start = ((bf16[16,512,128]{2,1,0:T(8,128)(2,1)}), bf16[16,512,128]{2,1,0:T(8,128)(2,1)}, u32[]{:S(2)}, u32[]{:S(2)}) async-start(bf16[16,512,128]{2,1,0:T(8,128)(2,1)} %bitcast.89), calls=%async_computation | async-start | bytes 4194304 | tf_op jit(solution)/shard_map/all_to_all | solution.py:20
  125.5 54.0 %all-gather.3.cloned.1.call-done = bf16[16,16,32,128]{3,2,1,0:T(8,128)(2,1)} async-done(((bf16[1,16,32,128]{3,2,1,0:T(8,128)(2,1)}), bf16[16,16,32,128]{3,2,1,0:T(8,128)(2,1)}) %all-gather.3.cloned.1.call-update) | async-done | bytes 2097168 | tf_op jit(solution)/shard_map/all_gather | solution.py:10
  179.5 1.9 reduce
  181.4 1.2 fusion.10
  182.6 1.2 fusion.3
  183.8 2.7 reduce.4
  186.5 2.2 reshape.115
  188.7 0.0 all-to-all-done
  188.8 11.6 %all-to-all-start.4 = ((bf16[32,2,4096]{2,1,0:T(2,128)(2,1)}), bf16[32,2,4096]{2,1,0:T(2,128)(2,1)}, u32[]{:S(2)}, u32[]{:S(2)}) async-start(bf16[32,2,4096]{2,1,0:T(2,128)(2,1)} %reshape.115), calls=%async_computation.4 | async-start | bytes 1048576 | tf_op jit(solution)/shard_map/all_to_all | solution.py:122
  200.4 0.0 all-gather.5.cloned.1.call-start
  200.4 0.7 all-gather.5.cloned.1.call-update
  201.1 1.9 multiply_convert_fusion
  203.0 0.6 copy.36
  203.6 2.2 fusion.1
  205.7 4.5 %reduce.3 = bf16[32,32768]{1,0:T(8,128)(2,1)} reduce(bf16[32,1,32768]{2,0,1:T(8,128)(2,1)} %fusion.1, bf16[]{:T(256)} %broadcast.29), dimensions={1}, to_apply=%copy.25.reduce_sub_computation | reduce | bytes 4194306 | tf_op jit(solution)/shard_map/all_to_all | solution.py:121
  210.3 4.5 %reshape.113 = bf16[32,2,16384]{2,1,0:T(2,128)(2,1)} reshape(bf16[32,32768]{1,0:T(8,128)(2,1)} %reduce.3) | data formatting | bytes 4194304
  214.8 3.8 %all-to-all-done.4 = bf16[32,2,4096]{2,1,0:T(2,128)(2,1)} async-done(((bf16[32,2,4096]{2,1,0:T(2,128)(2,1)}), bf16[32,2,4096]{2,1,0:T(2,128)(2,1)}, u32[]{:S(2)}, u32[]{:S(2)}) %all-to-all-start.4) | async-done | bytes 524320 | tf_op jit(solution)/shard_map/all_to_all | solution.py:122
  218.6 6.0 %all-to-all-start.3 = ((bf16[32,2,16384]{2,1,0:T(2,128)(2,1)}), bf16[32,2,16384]{2,1,0:T(2,128)(2,1)}, u32[]{:S(2)}, u32[]{:S(2)}) async-start(bf16[32,2,16384]{2,1,0:T(2,128)(2,1)} %reshape.113), calls=%async_computation.3 | async-start | bytes 4194304 | tf_op jit(solution)/shard_map/all_to_all | solution.py:121
  224.6 1.9 convert_reduce_fusion
  226.6 0.2 convolution_multiply_fusion.4
  226.8 0.7 fusion.21
  227.5 1.3 convolution_multiply_fusion.2
  228.8 16.4 %all-gather.5.cloned.1.call-done = bf16[512,2048]{1,0:T(8,128)(2,1)} async-done(((bf16[512,128]{1,0:T(8,128)(2,1)}), bf16[512,2048]{1,0:T(8,128)(2,1)}) %all-gather.5.cloned.1.call-update) | async-done | bytes 2097168 | tf_op jit(solution)/shard_map/all_gather | solution.py:92
  245.2 3.9 %fusion.9 = bf16[512,512]{1,0:T(8,128)(2,1)} fusion(f32[512,512]{1,0:T(8,128)} %bitcast.101, bf16[512,2048]{1,0:T(8,128)(2,1)} %all-gather.5.cloned.1.call-done, bf16[512,2048]{1,0:T(8,128)(2,1)S(1)} %copy-done), kind=kOutput, calls=%fused_computation.23 | convolution fusion | flops 1074266112 | bytes 5767168 | tf_op jit(solution)/shard_map/dot_general | solution.py:91
  249.1 3.6 %reshape.116 = bf16[32,1,8192]{2,1,0:T(2,128)(2,1)S(1)} reshape(bf16[32,2,4096]{2,1,0:T(2,128)(2,1)} %all-to-all-done.4) | data formatting | bytes 1048576
  252.8 0.7 fusion.13
  253.4 0.6 copy.69
  254.1 20.5 %all-to-all-done.3 = bf16[32,2,16384]{2,1,0:T(2,128)(2,1)} async-done(((bf16[32,2,16384]{2,1,0:T(2,128)(2,1)}), bf16[32,2,16384]{2,1,0:T(2,128)(2,1)}, u32[]{:S(2)}, u32[]{:S(2)}) %all-to-all-start.3) | async-done | bytes 2097184 | tf_op jit(solution)/shard_map/all_to_all | solution.py:121
  274.6 10.5 %reshape.114 = bf16[32,1,32768]{2,1,0:T(2,128)(2,1)} reshape(bf16[32,2,16384]{2,1,0:T(2,128)(2,1)} %all-to-all-done.3) | data formatting | bytes 4194304
  285.0 4.5 %convolution_multiply_fusion = f32[3,32768]{1,0:T(4,128)S(1)} fusion(bf16[32,3]{0,1:T(4,128)(2,1)S(1)} %get-tuple-element.5, bf16[32,1,32768]{2,1,0:T(2,128)(2,1)} %reshape.114, f32[3]{0:T(128)S(1)} %maximum_divide_fusion), kind=kOutput, calls=%fused_computation.5 | convolution fusion | flops 6389760 | bytes 2490572 | tf_op jit(solution)/shard_map/dot_general | solution.py:126
  289.6 0.9 copy.68
  (11 shorter events, 0.0 us)
Async XLA Ops:
  7.2 106.9 %copy-start = (bf16[512,2048]{1,0:T(8,128)(2,1)S(1)}, bf16[512,2048]{1,0:T(8,128)(2,1)}, u32[]{:S(2)}) copy-start(bf16[512,2048]{1,0:T(8,128)(2,1)} %param.8) | copy-start | bytes 6291460
  7.2 18.4 %copy-start.5 = (bf16[3,64,512]{2,1,0:T(8,128)(2,1)S(1)}, bf16[3,64,512]{2,1,0:T(8,128)(2,1)}, u32[]{:S(2)}) copy-start(bf16[3,64,512]{2,1,0:T(8,128)(2,1)} %param.9) | copy-start | bytes 589828
  12.4 30.9 %all-to-all-start.2 = ((bf16[32,2,4096]{2,1,0:T(2,128)(2,1)}), bf16[32,2,4096]{2,1,0:T(2,128)(2,1)S(1)}, u32[]{:S(2)}, u32[]{:S(2)}) async-start(bf16[32,2,4096]{2,1,0:T(2,128)(2,1)} %reshape.109), calls=%async_computation.2 | async-start | bytes 1048576 | tf_op jit(solution)/shard_map/all_to_all | solution.py:66
  43.3 4.9 %copy-start.1 = (bf16[32,2,4096]{2,1,0:T(2,128)(2,1)}, bf16[32,2,4096]{2,1,0:T(2,128)(2,1)S(1)}, u32[]{:S(2)}) copy-start(bf16[32,2,4096]{2,1,0:T(2,128)(2,1)S(1)} %all-to-all-done.2) | copy-start | bytes 1572868
  43.3 54.0 %all-to-all-start.1 = ((bf16[32,2,16384]{2,1,0:T(2,128)(2,1)}), bf16[32,2,16384]{2,1,0:T(2,128)(2,1)}, u32[]{:S(2)}, u32[]{:S(2)}) async-start(bf16[32,2,16384]{2,1,0:T(2,128)(2,1)} %reshape.111), calls=%async_computation.1 | async-start | bytes 4194304 | tf_op jit(solution)/shard_map/all_to_all | solution.py:65
  48.1 4.5 %copy-start.3 = (bf16[512,128]{1,0:T(8,128)(2,1)S(1)}, bf16[512,128]{1,0:T(8,128)(2,1)}, u32[]{:S(2)}) copy-start(bf16[512,128]{1,0:T(8,128)(2,1)} %param.11) | copy-start | bytes 393220
  48.1 131.4 %all-gather.3.cloned.1.call-start = ((), (), s32[]{:S(2)}) async-start(), calls=%async_computation.5 | async-start | bytes 2228224 | tf_op jit(solution)/shard_map/all_gather | solution.py:10
  107.8 4.9 %copy-start.2 = (bf16[512,512]{1,0:T(8,128)(2,1)S(1)}, bf16[512,512]{1,0:T(8,128)(2,1)}, u32[]{:S(2)}) copy-start(bf16[512,512]{1,0:T(8,128)(2,1)} %param.7) | copy-start | bytes 1572868
  112.3 0.9 copy-start.4
  118.2 70.6 %all-to-all-start = ((bf16[16,512,128]{2,1,0:T(8,128)(2,1)}), bf16[16,512,128]{2,1,0:T(8,128)(2,1)}, u32[]{:S(2)}, u32[]{:S(2)}) async-start(bf16[16,512,128]{2,1,0:T(8,128)(2,1)} %bitcast.89), calls=%async_computation | async-start | bytes 4194304 | tf_op jit(solution)/shard_map/all_to_all | solution.py:20
  188.8 29.8 %all-to-all-start.4 = ((bf16[32,2,4096]{2,1,0:T(2,128)(2,1)}), bf16[32,2,4096]{2,1,0:T(2,128)(2,1)}, u32[]{:S(2)}, u32[]{:S(2)}) async-start(bf16[32,2,4096]{2,1,0:T(2,128)(2,1)} %reshape.115), calls=%async_computation.4 | async-start | bytes 1048576 | tf_op jit(solution)/shard_map/all_to_all | solution.py:122
  200.4 44.8 %all-gather.5.cloned.1.call-start = ((), (), s32[]{:S(2)}) async-start(), calls=%async_computation.6 | async-start | bytes 2228224 | tf_op jit(solution)/shard_map/all_gather | solution.py:92
  218.6 56.0 %all-to-all-start.3 = ((bf16[32,2,16384]{2,1,0:T(2,128)(2,1)}), bf16[32,2,16384]{2,1,0:T(2,128)(2,1)}, u32[]{:S(2)}, u32[]{:S(2)}) async-start(bf16[32,2,16384]{2,1,0:T(2,128)(2,1)} %reshape.113), calls=%async_computation.3 | async-start | bytes 4194304 | tf_op jit(solution)/shard_map/all_to_all | solution.py:121
Sparse Core Ops, SparseCore 0:
  114.2 65.3 all-gather.2
  203.3 41.8 all-gather.4
where the time goes:
time: 299 us; the launch traced here: 297 us
  waiting for transfers between devices  146 us (49%)
  local copies, waits for them, and re-layouts  45.9 us (15%)
  starting transfers between devices  43 us (14%)
  matrix products  29.1 us (10%)
  other arithmetic  19.4 us (6%)
  between operations  14.2 us (5%)
    all_gather x1, waiting for transfers between devices, gathered_total(): return lax.all_gather(value, axis).astype(jnp.float32).sum(0)  54 us
    all_to_all x1, waiting for transfers between devices, on_device(): lax.all_to_all(send_down, 'dp', split_axis=0, concat_axis=0, tiled=True)  43.8 us
    unnamed x26, local copies, waits for them, and re-layouts  43.4 us
    all_to_all x1, waiting for transfers between devices, on_device(): lax.all_to_all(ship_down, 'dp', split_axis=0, concat_axis=0, tiled=True)  20.5 us
    all_gather x1, waiting for transfers between devices, on_device(): lax.all_gather(cotangent, 'tensor', axis=1, tiled=True)  16.4 us
    all_to_all x1, starting transfers between devices, on_device(): lax.all_to_all(send_up, 'dp', split_axis=0, concat_axis=0, tiled=True)  13.2 us
    all_to_all x1, starting transfers between devices, on_device(): lax.all_to_all(ship_up, 'dp', split_axis=0, concat_axis=0, tiled=True)  11.6 us
    all_to_all x1, starting transfers between devices, sent_and_summed(): lax.all_to_all(pieces, axis, split_axis=0, concat_axis=0, tiled=True)  7.34 us
  transfers between devices with their start and end apart: 7, of which 6 were waited for; matrix products, arithmetic and copies ran while one was open for 19% of the time, Pallas kernels for 0%

commit v1 on v0

v1 whole, which is shorter than its diff:
```python
import functools

import jax
import jax.numpy as jnp
from jax import lax
from jax.experimental import pallas as pl
from jax.experimental.pallas import tpu as pltpu
from jax.sharding import PartitionSpec as P

adapter_scale = 0.25
f32 = jnp.float32
bf16 = jnp.bfloat16
SMEM = pl.BlockSpec(memory_space=pltpu.SMEM)
VMEM = pl.BlockSpec(memory_space=pltpu.VMEM)
VMEM_LIMIT = 40 * 1024 * 1024


def local_call(body, out_shape, specs, scratch=(), flops=0, moved=0):
    multiple = isinstance(out_shape, (tuple, list))
    return pl.pallas_call(
        body,
        out_shape=out_shape,
        in_specs=specs,
        out_specs=(VMEM,) * len(out_shape) if multiple else VMEM,
        scratch_shapes=list(scratch),
        compiler_params=pltpu.CompilerParams(vmem_limit_bytes=VMEM_LIMIT),
        cost_estimate=pl.CostEstimate(flops=flops, bytes_accessed=moved, transcendentals=0),
    )


def owner_of(first, index_ref, storage_ref, held, j):
    return storage_ref[index_ref[first + j]] // held


def spread_body(held, first_ref, index_ref, storage_ref, rows_ref, out_ref):
    slots, length, width = out_ref.shape
    out_ref[...] = jnp.zeros_like(out_ref)
    first = first_ref[0]
    for j in range(rows_ref.shape[0] // length):
        owner = owner_of(first, index_ref, storage_ref, held, j)
        out_ref[owner] = rows_ref[j * length : (j + 1) * length, :]


def projection_body(core_ref, tokens_ref, weight_ref, own_ref, send_ref):
    blocks, rows, width = own_ref.shape
    core = core_ref[0]
    tokens = tokens_ref[...]
    for b in range(blocks):
        part = jnp.dot(
            tokens,
            weight_ref[:, b * 2 * width : (b + 1) * 2 * width],
            preferred_element_type=f32,
        ).astype(bf16)
        low, high = part[:, :width], part[:, width:]

        @pl.when(core == 0)
        def _():
            own_ref[b] = low
            send_ref[b] = high

        @pl.when(core != 0)
        def _():
            own_ref[b] = high
            send_ref[b] = low


def rank_body(pick_ref, rows_ref, adapter_ref, out_ref):
    slots, length, width = rows_ref.shape
    held, rank, _ = adapter_ref.shape
    half = slots // 2
    flat = rows_ref[...].reshape(slots * length, width)
    dims = (((1,), (1,)), ((), ()))
    totals = [
        lax.dot_general(flat, adapter_ref[a], dims, preferred_element_type=f32) for a in range(held)
    ]
    chosen = []
    for s in range(slots):
        at = slice(s * length, (s + 1) * length)
        value = jnp.zeros((length, rank), f32)
        for a in range(held):
            value = jnp.where(pick_ref[s] == a, totals[a][at], value)
        chosen.append(value)
    for s in range(half):
        out_ref[s * length : (s + 1) * length, :] = jnp.concatenate(
            [chosen[s], chosen[s + half]], axis=1
        ).astype(bf16)


def fill_masked(pick_ref, pairs_ref, masked_ref, slots, length, held, rank):
    half = slots // 2
    for s in range(slots):
        left = (s // half) * rank
        block = pairs_ref[(s % half) * length : (s % half + 1) * length, :][:, left : left + rank]
        for a in range(held):
            masked_ref[s * length : (s + 1) * length, a * rank : (a + 1) * rank] = jnp.where(
                pick_ref[s] == a, block, jnp.zeros_like(block)
            )


def expand_body(pick_ref, pairs_ref, adapter_ref, out_ref, masked_ref):
    slots, length, width = out_ref.shape
    held, rank, _ = adapter_ref.shape
    fill_masked(pick_ref, pairs_ref, masked_ref, slots, length, held, rank)
    stacked = adapter_ref[...].reshape(held * rank, width)
    value = jnp.dot(masked_ref[...], stacked, preferred_element_type=f32) * adapter_scale
    out_ref[...] = value.astype(bf16).reshape(slots, length, width)


def gradient_body(pick_ref, scale_ref, pairs_ref, rows_ref, out_ref, masked_ref):
    slots, length, width = rows_ref.shape
    held, rank, _ = out_ref.shape
    fill_masked(pick_ref, pairs_ref, masked_ref, slots, length, held, rank)
    total = lax.dot_general(
        masked_ref[...],
        rows_ref[...].reshape(slots * length, width),
        (((0,), (0,)), ((), ())),
        preferred_element_type=f32,
    )
    for a in range(held):
        out_ref[a] = total[a * rank : (a + 1) * rank] * scale_ref[a]


def input_gradient_body(
    held, first_ref, index_ref, storage_ref, cot_ref, weight_ref, came_ref, out_ref, total_ref
):
    blocks, rows, width = cot_ref.shape
    length = came_ref.shape[1]
    dims = (((1,), (1,)), ((), ()))
    for b in range(blocks // 2):
        pair = jnp.concatenate([cot_ref[2 * b], cot_ref[2 * b + 1]], axis=1)
        part = lax.dot_general(
            pair,
            weight_ref[:, 2 * b * width : 2 * (b + 1) * width],
            dims,
            preferred_element_type=f32,
        )
        total_ref[...] = part if b == 0 else total_ref[...] + part
    first = first_ref[0]
    for j in range(rows // length):
        owner = owner_of(first, index_ref, storage_ref, held, j)
        at = slice(j * length, (j + 1) * length)
        out_ref[at, :] = (total_ref[at, :] + came_ref[owner].astype(f32)).astype(bf16)


def output_body(held, first_ref, index_ref, storage_ref, base_ref, came_ref, out_ref):
    length = came_ref.shape[1]
    first = first_ref[0]
    for j in range(base_ref.shape[0] // length):
        owner = owner_of(first, index_ref, storage_ref, held, j)
        at = slice(j * length, (j + 1) * length)
        out_ref[at, :] = (base_ref[at, :].astype(f32) + came_ref[owner].astype(f32)).astype(bf16)


def rank_total(part, count):
    cores = [[t, t + 1] for t in range(0, count, 2)]
    half = part.shape[0] // 2
    core = lax.axis_index("tensor") % 2
    both = lax.all_gather(part, "tensor", axis_index_groups=cores)
    mine = lax.dynamic_slice_in_dim(both, core * half, half, axis=1)
    total = mine.astype(f32).sum(0).astype(bf16)
    step = 2
    while step < count:
        other = lax.ppermute(total, "tensor", [(t, t ^ step) for t in range(count)])
        total = (total.astype(f32) + other.astype(f32)).astype(bf16)
        step *= 2
    return lax.all_gather(total, "tensor", axis_index_groups=cores).reshape(part.shape)


def exchange(value):
    return lax.all_to_all(value, "dp", split_axis=0, concat_axis=0, tiled=True)


def after(value, earlier):
    return lax.optimization_barrier((value, earlier))[0]


def on_device(tokens, weight, down, up, cotangent, sequence_index, storage_row):
    dp_count = lax.axis_size("dp")
    tensor_count = lax.axis_size("tensor")
    me = lax.axis_index("dp")
    held, rank, block = down.shape
    out_block = up.shape[2]
    rows = tokens.shape[0]
    seqs = sequence_index.shape[0] // dp_count
    length = rows // seqs
    slots = dp_count
    first = jnp.reshape(me * seqs, (1,)).astype(jnp.int32)
    core = jnp.reshape(lax.axis_index("tensor") % 2, (1,)).astype(jnp.int32)

    def shape(*dims, dtype=bf16):
        return jax.ShapeDtypeStruct(dims, dtype)

    def spread(value):
        width = value.shape[1]
        return local_call(
            functools.partial(spread_body, held),
            shape(slots, length, width),
            [SMEM, SMEM, SMEM, VMEM],
            moved=3 * slots * length * width,
        )(first, sequence_index, storage_row, value)

    cot_slots = exchange(spread(cotangent))

    codes = jnp.arange(storage_row.shape[0], dtype=jnp.int32)
    matches = sequence_index[:, None] == codes[None, :]
    seq_rows = jnp.sum(jnp.where(matches, storage_row[None, :], 0), axis=1)
    local = jnp.where(seq_rows // held == me, seq_rows - held * me, -1)
    pick = jnp.max(local.reshape(dp_count, seqs), axis=1).astype(jnp.int32)
    usage = jnp.sum((pick[:, None] == jnp.arange(held)[None, :]).astype(f32), axis=0)
    scale = adapter_scale / jnp.maximum(usage, 1.0)

    all_cot = lax.all_gather(cotangent, "tensor")
    half_blocks = tensor_count // 2
    own, send = local_call(
        projection_body,
        (shape(half_blocks, rows, out_block), shape(half_blocks, rows, out_block)),
        [SMEM, VMEM, VMEM],
        flops=2 * rows * block * tensor_count * out_block,
        moved=2 * (rows * block + 2 * block * tensor_count * out_block),
    )(core, tokens, weight)
    came = lax.ppermute(send, "tensor", [(t, t ^ 1) for t in range(tensor_count)])
    paired = (own.astype(f32) + came.astype(f32)).astype(bf16)
    same_core = [list(range(c, tensor_count, 2)) for c in range(2)]
    backbone = lax.psum_scatter(
        paired, "tensor", scatter_dimension=0, axis_index_groups=same_core, tiled=False
    )

    token_slots = exchange(after(spread(tokens), cot_slots))

    def rank_part(value, adapter):
        width = value.shape[2]
        return local_call(
            rank_body,
            shape(slots * length // 2, 2 * rank),
            [SMEM, VMEM, VMEM],
            flops=2 * slots * length * width * held * rank,
            moved=2 * slots * length * width,
        )(pick, value, adapter)

    masked = pltpu.VMEM((slots * length, held * rank), bf16)

    def expand(pairs, adapter):
        width = adapter.shape[2]
        return local_call(
            expand_body,
            shape(slots, length, width),
            [SMEM, VMEM, VMEM],
            [masked],
            flops=2 * slots * length * width * held * rank,
            moved=2 * slots * length * width,
        )(pick, pairs, adapter)

    def gradient(pairs, value):
        width = value.shape[2]
        return local_call(
            gradient_body,
            shape(held, rank, width, dtype=f32),
            [SMEM, SMEM, VMEM, VMEM],
            [masked],
            flops=2 * slots * length * width * held * rank,
            moved=2 * slots * length * width,
        )(pick, scale, pairs, value)

    back = rank_total(rank_part(cot_slots, up), tensor_count)
    token_parts = expand(back, down)
    token_slots, token_parts = lax.optimization_barrier((token_slots, token_parts))
    token_came = exchange(token_parts)
    inner = rank_total(rank_part(token_slots, down), tensor_count)
    output_parts = expand(inner, up)
    output_came = exchange(after(output_parts, token_came))
    grad_down = gradient(back, token_slots)
    grad_up = gradient(inner, cot_slots)

    token_gradient = local_call(
        functools.partial(input_gradient_body, held),
        shape(rows, block),
        [SMEM, SMEM, SMEM, VMEM, VMEM, VMEM],
        [pltpu.VMEM((rows, block), f32)],
        flops=2 * rows * block * tensor_count * out_block,
        moved=2 * (2 * rows * tensor_count * out_block + slots * length * block),
    )(first, sequence_index, storage_row, all_cot, weight, token_came)
    key_value_output = local_call(
        functools.partial(output_body, held),
        shape(rows, out_block),
        [SMEM, SMEM, SMEM, VMEM, VMEM],
        moved=2 * (2 * rows * out_block + slots * length * out_block),
    )(first, sequence_index, storage_row, backbone, output_came)
    return (key_value_output, token_gradient, grad_down, grad_up)


def solution(mesh):
    in_specs = (
        P("dp", "tensor"),
        P("tensor", None),
        P("dp", None, "tensor"),
        P("dp", None, "tensor"),
        P("dp", "tensor"),
        P(),
        P(),
    )
    out_specs = (
        P("dp", "tensor"),
        P("dp", "tensor"),
        P("dp", None, "tensor"),
        P("dp", None, "tensor"),
    )
    return jax.shard_map(
        on_device, mesh=mesh, in_specs=in_specs, out_specs=out_specs, check_vma=False
    )
```

time: 299 us -> 160 us (0.54)
  the two profiles are of different devices: /device:TPU:24 before, /device:TPU:1 now
where the time goes in v1:
time: 160 us; the launch traced here: 158 us
  starting transfers between devices  65.7 us (41%)
  waiting for transfers between devices  25.7 us (16%)
  Pallas kernels  21.8 us (14%)
  between operations  15.7 us (10%)
  blocking collectives  14.7 us (9%)
  local copies, waits for them, and re-layouts  11.5 us (7%)
  other arithmetic  3.01 us (2%)
    all_to_all x4, starting transfers between devices, exchange(): return lax.all_to_all(value, 'dp', split_axis=0, concat_axis=0, tiled=True)  37.6 us
    ppermute x6, starting transfers between devices, rank_total(): other = lax.ppermute(total, 'tensor', [(t, t ^ step) for t in range(count)])  25.5 us
    ppermute x6, waiting for transfers between devices, rank_total(): other = lax.ppermute(total, 'tensor', [(t, t ^ step) for t in range(count)])  16.2 us
    unnamed x34, local copies, waits for them, and re-layouts  11.2 us
    all_gather x2, blocking collectives, rank_total(): lax.all_gather(total, 'tensor', axis_index_groups=cores).reshape(part.shape)  8.99 us
    all_to_all x4, waiting for transfers between devices, exchange(): return lax.all_to_all(value, 'dp', split_axis=0, concat_axis=0, tiled=True)  8.82 us
    all_gather x2, blocking collectives, rank_total(): both = lax.all_gather(part, 'tensor', axis_index_groups=cores)  5.66 us
    pallas_call x1, Pallas kernels, on_device(): local_call(projection_body, (shape(half_blocks, rows, out_block), shape(h...  4.55 us
  transfers between devices with their start and end apart: 13, of which 7 were waited for; matrix products, arithmetic and copies ran while one was open for 2% of the time, Pallas kernels for 13%

profile of v1, /device:TPU:1, one launch (start us, length us, event | category | flops | bytes accessed | tf_op | source)
XLA Modules:
  0.0 158.1 jit_solution(11495412906697625105)
XLA Ops:
  8.0 0.0 all-gather.7.cloned.1.call-start
  8.0 0.7 all-gather.7.cloned.1.call-update
  8.7 0.9 copy-done.5
  9.6 0.7 copy-done.11
  10.3 0.7 copy-done.14
  11.0 1.4 shard_map.104
  12.4 13.8 %all-to-all-start = ((bf16[32,32,128]{2,1,0:T(8,128)(2,1)}), bf16[32,32,128]{2,1,0:T(8,128)(2,1)S(1)}, u32[]{:S(2)}, u32[]{:S(2)}) async-start(bf16[32,32,128]{2,1,0:T(8,128)(2,1)} %shard_map.104), calls=%async_computation.1 | async-start | bytes 524288 | tf_op jit(solution)/shard_map/all_to_all | solution.py:170
  26.2 0.0 copy-start.6
  26.2 1.0 copy-done.6
  27.3 0.7 copy-done.12
  27.9 0.7 copy-done.15
  28.6 1.7 %shard_map.103 = bf16[32,32,512]{2,1,0:T(8,128)(2,1)} custom-call(s32[1]{0:T(128)} %bitcast.first_ref, s32[512]{0:T(512)S(1)} %copy-done.12, s32[96]{0:T(128)S(1)} %copy-done.15, bf16[512,512]{1,0:T(8,128)(2,1)S(1)} %copy-done.6), custom_call_target="tpu_custom_call" | custom-call | bytes 1572864 | tf_op jit(solution)/shard_map/pallas_call | solution.py:195
  30.3 7.1 %all-to-all-done.rows_ref = bf16[32,32,128]{2,1,0:T(8,128)(2,1)S(1)} async-done(((bf16[32,32,128]{2,1,0:T(8,128)(2,1)}), bf16[32,32,128]{2,1,0:T(8,128)(2,1)S(1)}, u32[]{:S(2)}, u32[]{:S(2)}) %all-to-all-start) | async-done | bytes 262176 | tf_op jit(solution)/shard_map/all_to_all | solution.py:170
  37.4 4.8 %all-to-all-start.1 = ((bf16[32,32,512]{2,1,0:T(8,128)(2,1)}), bf16[32,32,512]{2,1,0:T(8,128)(2,1)S(1)}, u32[]{:S(2)}, u32[]{:S(2)}) async-start(bf16[32,32,512]{2,1,0:T(8,128)(2,1)} %shard_map.103), calls=%async_computation.2 | async-start | bytes 2097152 | tf_op jit(solution)/shard_map/all_to_all | solution.py:170
  42.2 0.1 select_reduce_fusion
  42.3 0.1 div.14
  42.4 0.1 sub.19
  42.5 0.1 and.19
  42.6 0.1 select_reduce_fusion.1.pick_ref
  42.7 1.0 shard_map.105
  43.7 3.4 %all-gather = bf16[1024,128]{1,0:T(8,128)(2,1)S(1)} all-gather(bf16[512,128]{1,0:T(8,128)(2,1)S(1)} %shard_map.105), channel_id=2, replica_groups={{0,1},{2,3},{4,5},{6,7},{8,9},{10,11},{12,13},{14,15},{16,17},{18,19},{..., dimensions={0}, use_global_device_ids=true | all-gather | bytes 393216 | tf_op jit(solution)/shard_map/all_gather | solution.py:158
  47.1 3.2 %collective-permute-start.1 = (bf16[256,128]{1,0:T(8,128)(2,1)S(1)}, bf16[256,128]{1,0:T(8,128)(2,1)S(1)}, u32[]{:S(2)}, u32[]{:S(2)}) collective-permute-start(bf16[256,128]{1,0:T(8,128)(2,1)S(1)} %dynamic-slice_reduce_fusion.1), channel_id=1, source_target_pairs={{0,2},{1,3},{2,0},{3,1},{4,6},{5,7},{6,4},{7,5},{8,10},{9,11},{10,... | collective-permute-start | bytes 196616 | tf_op jit(solution)/shard_map/ppermute | solution.py:163
  50.4 0.0 copy-done.7
  50.4 0.0 copy-start
  50.4 1.6 %copy-done = bf16[512,2048]{1,0:T(8,128)(2,1)S(1)} copy-done((bf16[512,2048]{1,0:T(8,128)(2,1)S(1)}, bf16[512,2048]{1,0:T(8,128)(2,1)}, u32[]{:S(2)}) %copy-start) | copy-done | bytes 2097176
  52.0 4.6 %shard_map.102 = (bf16[8,512,128]{2,1,0:T(8,128)(2,1)S(1)}, bf16[8,512,128]{2,1,0:T(8,128)(2,1)}) custom-call(s32[1]{0:T(128)} %bitcast.1.core_ref, bf16[512,512]{1,0:T(8,128)(2,1)S(1)} %copy-done.7, bf16[512,2048]{1,0:T(8,128)(2,1)S(1)} %copy-done), custom_call_target="tpu_custom_call" | custom-call | flops 1073741824 | bytes 4718592 | tf_op jit(solution)/shard_map/pallas_call | solution.py:214
  56.5 2.5 %collective-permute-start = (bf16[8,512,128]{2,1,0:T(8,128)(2,1)}, bf16[8,512,128]{2,1,0:T(8,128)(2,1)}, u32[]{:S(2)}, u32[]{:S(2)}) collective-permute-start(bf16[8,512,128]{2,1,0:T(8,128)(2,1)} %get-tuple-element.11), channel_id=1, source_target_pairs={{0,1},{1,0},{2,3},{3,2},{4,5},{5,4},{6,7},{7,6},{8,9},{9,8},{10,11... | collective-permute-start | bytes 3145736 | tf_op jit(solution)/shard_map/ppermute | solution.py:221
  59.0 0.0 collective-permute-done.1
  59.1 4.2 %collective-permute-start.2 = (bf16[256,128]{1,0:T(8,128)(2,1)S(1)}, bf16[256,128]{1,0:T(8,128)(2,1)S(1)}, u32[]{:S(2)}, u32[]{:S(2)}) collective-permute-start(bf16[256,128]{1,0:T(8,128)(2,1)S(1)} %add_convert_fusion.6), channel_id=1, source_target_pairs={{0,4},{1,5},{2,6},{3,7},{4,0},{5,1},{6,2},{7,3},{8,12},{9,13},{10,... | collective-permute-start | bytes 196616 | tf_op jit(solution)/shard_map/ppermute | solution.py:163
  63.3 3.9 %collective-permute-done.2 = bf16[256,128]{1,0:T(8,128)(2,1)S(1)} collective-permute-done((bf16[256,128]{1,0:T(8,128)(2,1)S(1)}, bf16[256,128]{1,0:T(8,128)(2,1)S(1)}, u32[]{:S(2)}, u32[]{:S(2)}) %collective-permute-start.2) | collective-permute-done | bytes 65568 | tf_op jit(solution)/shard_map/ppermute | solution.py:163
  67.3 6.3 %collective-permute-start.3 = (bf16[256,128]{1,0:T(8,128)(2,1)S(1)}, bf16[256,128]{1,0:T(8,128)(2,1)S(1)}, u32[]{:S(2)}, u32[]{:S(2)}) collective-permute-start(bf16[256,128]{1,0:T(8,128)(2,1)S(1)} %add_convert_fusion.5), channel_id=1, source_target_pairs={{0,8},{1,9},{2,10},{3,11},{4,12},{5,13},{6,14},{7,15},{8,0},{9,1},... | collective-permute-start | bytes 196616 | tf_op jit(solution)/shard_map/ppermute | solution.py:163
  73.6 2.7 %collective-permute-done.3 = bf16[256,128]{1,0:T(8,128)(2,1)S(1)} collective-permute-done((bf16[256,128]{1,0:T(8,128)(2,1)S(1)}, bf16[256,128]{1,0:T(8,128)(2,1)S(1)}, u32[]{:S(2)}, u32[]{:S(2)}) %collective-permute-start.3) | collective-permute-done | bytes 65568 | tf_op jit(solution)/shard_map/ppermute | solution.py:163
  76.3 3.7 %all-gather.1.pairs_ref = bf16[512,128]{1,0:T(8,128)(2,1)S(1)} all-gather(bf16[256,128]{1,0:T(8,128)(2,1)S(1)} %add_convert_fusion.4), channel_id=3, replica_groups={{0,1},{2,3},{4,5},{6,7},{8,9},{10,11},{12,13},{14,15},{16,17},{18,19},{..., dimensions={0}, use_global_device_ids=true | all-gather | bytes 196608 | tf_op jit(solution)/shard_map/all_gather | solution.py:166
  80.1 0.0 copy-done.3
  80.1 2.0 %shard_map.106 = bf16[32,32,512]{2,1,0:T(8,128)(2,1)} custom-call(s32[32]{0:T(128)S(1)} %select_reduce_fusion.1.pick_ref, bf16[512,128]{1,0:T(8,128)(2,1)S(1)} %all-gather.1.pairs_ref, bf16[3,64,512]{2,1,0:T(8,128)(2,1)S(1)} %copy-done.3), custom_call_target="tpu_custom_call" | custom-call | flops 201326592 | bytes 1048576 | tf_op jit(solution)/shard_map/pallas_call | solution.py:244
  82.1 0.0 all-to-all-done.1.rows_ref
  82.1 9.5 %all-to-all-start.2 = ((bf16[32,32,512]{2,1,0:T(8,128)(2,1)}), bf16[32,32,512]{2,1,0:T(8,128)(2,1)S(1)}, u32[]{:S(2)}, u32[]{:S(2)}) async-start(bf16[32,32,512]{2,1,0:T(8,128)(2,1)} %shard_map.106), calls=%async_computation.3 | async-start | bytes 2097152 | tf_op jit(solution)/shard_map/all_to_all | solution.py:170
  91.6 0.0 reduce-scatter.2.cloned.1.call-start
  91.7 0.0 collective-permute-done
  91.7 2.5 %add_convert_fusion = bf16[8,512,128]{2,1,0:T(8,128)(2,1)} fusion(bf16[8,512,128]{2,1,0:T(8,128)(2,1)} %collective-permute-done, bf16[8,512,128]{2,1,0:T(8,128)(2,1)S(1)} %get-tuple-element.10), kind=kLoop, calls=%fused_computation | loop fusion | flops 2097152 | bytes 3145728 | tf_op jit(solution)/shard_map/convert_element_type | solution.py:222
  94.1 0.0 reduce-scatter.2.cloned.1.call-update
  94.2 0.0 copy-start.4
  94.2 0.9 copy-done.4
  95.1 1.6 shard_map.107
  96.7 2.3 %all-gather.2 = bf16[1024,128]{1,0:T(8,128)(2,1)S(1)} all-gather(bf16[512,128]{1,0:T(8,128)(2,1)S(1)} %shard_map.107), channel_id=4, replica_groups={{0,1},{2,3},{4,5},{6,7},{8,9},{10,11},{12,13},{14,15},{16,17},{18,19},{..., dimensions={0}, use_global_device_ids=true | all-gather | bytes 393216 | tf_op jit(solution)/shard_map/all_gather | solution.py:158
  99.0 1.9 %collective-permute-start.4 = (bf16[256,128]{1,0:T(8,128)(2,1)S(1)}, bf16[256,128]{1,0:T(8,128)(2,1)S(1)}, u32[]{:S(2)}, u32[]{:S(2)}) collective-permute-start(bf16[256,128]{1,0:T(8,128)(2,1)S(1)} %dynamic-slice_reduce_fusion), channel_id=1, source_target_pairs={{0,2},{1,3},{2,0},{3,1},{4,6},{5,7},{6,4},{7,5},{8,10},{9,11},{10,... | collective-permute-start | bytes 196616 | tf_op jit(solution)/shard_map/ppermute | solution.py:163
  100.9 3.4 %collective-permute-done.4 = bf16[256,128]{1,0:T(8,128)(2,1)S(1)} collective-permute-done((bf16[256,128]{1,0:T(8,128)(2,1)S(1)}, bf16[256,128]{1,0:T(8,128)(2,1)S(1)}, u32[]{:S(2)}, u32[]{:S(2)}) %collective-permute-start.4) | collective-permute-done | bytes 65568 | tf_op jit(solution)/shard_map/ppermute | solution.py:163
  104.3 3.4 %collective-permute-start.5 = (bf16[256,128]{1,0:T(8,128)(2,1)S(1)}, bf16[256,128]{1,0:T(8,128)(2,1)S(1)}, u32[]{:S(2)}, u32[]{:S(2)}) collective-permute-start(bf16[256,128]{1,0:T(8,128)(2,1)S(1)} %add_convert_fusion.3), channel_id=1, source_target_pairs={{0,4},{1,5},{2,6},{3,7},{4,0},{5,1},{6,2},{7,3},{8,12},{9,13},{10,... | collective-permute-start | bytes 196616 | tf_op jit(solution)/shard_map/ppermute | solution.py:163
  107.7 3.5 %collective-permute-done.5 = bf16[256,128]{1,0:T(8,128)(2,1)S(1)} collective-permute-done((bf16[256,128]{1,0:T(8,128)(2,1)S(1)}, bf16[256,128]{1,0:T(8,128)(2,1)S(1)}, u32[]{:S(2)}, u32[]{:S(2)}) %collective-permute-start.5) | collective-permute-done | bytes 65568 | tf_op jit(solution)/shard_map/ppermute | solution.py:163
  111.2 6.4 %collective-permute-start.6 = (bf16[256,128]{1,0:T(8,128)(2,1)S(1)}, bf16[256,128]{1,0:T(8,128)(2,1)S(1)}, u32[]{:S(2)}, u32[]{:S(2)}) collective-permute-start(bf16[256,128]{1,0:T(8,128)(2,1)S(1)} %add_convert_fusion.2), channel_id=1, source_target_pairs={{0,8},{1,9},{2,10},{3,11},{4,12},{5,13},{6,14},{7,15},{8,0},{9,1},... | collective-permute-start | bytes 196616 | tf_op jit(solution)/shard_map/ppermute | solution.py:163
  117.6 2.7 %collective-permute-done.6 = bf16[256,128]{1,0:T(8,128)(2,1)S(1)} collective-permute-done((bf16[256,128]{1,0:T(8,128)(2,1)S(1)}, bf16[256,128]{1,0:T(8,128)(2,1)S(1)}, u32[]{:S(2)}, u32[]{:S(2)}) %collective-permute-start.6) | collective-permute-done | bytes 65568 | tf_op jit(solution)/shard_map/ppermute | solution.py:163
  120.3 5.3 %all-gather.3.pairs_ref = bf16[512,128]{1,0:T(8,128)(2,1)S(1)} all-gather(bf16[256,128]{1,0:T(8,128)(2,1)S(1)} %add_convert_fusion.1), channel_id=5, replica_groups={{0,1},{2,3},{4,5},{6,7},{8,9},{10,11},{12,13},{14,15},{16,17},{18,19},{..., dimensions={0}, use_global_device_ids=true | all-gather | bytes 196608 | tf_op jit(solution)/shard_map/all_gather | solution.py:166
  125.6 1.7 %shard_map.108 = bf16[32,32,128]{2,1,0:T(8,128)(2,1)} custom-call(s32[32]{0:T(128)S(1)} %select_reduce_fusion.1.pick_ref, bf16[512,128]{1,0:T(8,128)(2,1)S(1)} %all-gather.3.pairs_ref, bf16[3,64,128]{2,1,0:T(8,128)(2,1)S(1)} %copy-done.9), custom_call_target="tpu_custom_call" | custom-call | flops 50331648 | bytes 262144 | tf_op jit(solution)/shard_map/pallas_call | solution.py:244
  127.3 0.0 all-to-all-done.2.came_ref
  127.3 9.5 %all-to-all-start.3 = ((bf16[32,32,128]{2,1,0:T(8,128)(2,1)}), bf16[32,32,128]{2,1,0:T(8,128)(2,1)S(1)}, u32[]{:S(2)}, u32[]{:S(2)}) async-start(bf16[32,32,128]{2,1,0:T(8,128)(2,1)} %shard_map.108), calls=%async_computation.4 | async-start | bytes 524288 | tf_op jit(solution)/shard_map/all_to_all | solution.py:170
  136.8 0.1 convert_reduce_fusion
  137.0 2.1 %shard_map.111 = f32[3,64,512]{2,1,0:T(8,128)} custom-call(s32[32]{0:T(128)S(1)} %select_reduce_fusion.1.pick_ref, f32[3]{0:T(128)S(1)} %maximum_divide_fusion.scale_ref, bf16[512,128]{1,0:T(8,128)(2,1)S(1)} %all-gather.1.pairs_ref, bf16[32,32,512]{2,1,0:T(8,128)(2,1)S(1)} %all-to-all-done.1.rows_ref), custom_call_target="tpu_custom_call" | custom-call | flops 201326592 | bytes 1048576 | tf_op jit(solution)/shard_map/pallas_call | solution.py:255
  139.1 1.8 %shard_map.112 = f32[3,64,128]{2,1,0:T(8,128)} custom-call(s32[32]{0:T(128)S(1)} %select_reduce_fusion.1.pick_ref, f32[3]{0:T(128)S(1)} %maximum_divide_fusion.scale_ref, bf16[512,128]{1,0:T(8,128)(2,1)S(1)} %all-gather.3.pairs_ref, bf16[32,32,128]{2,1,0:T(8,128)(2,1)S(1)} %all-to-all-done.rows_ref), custom_call_target="tpu_custom_call" | custom-call | flops 50331648 | bytes 262144 | tf_op jit(solution)/shard_map/pallas_call | solution.py:255
  140.9 1.6 %copy-done.1 = bf16[512,2048]{1,0:T(8,128)(2,1)S(1)} copy-done((bf16[512,2048]{1,0:T(8,128)(2,1)S(1)}, bf16[512,2048]{1,0:T(8,128)(2,1)}, u32[]{:S(2)}) %copy-start.1) | copy-done | bytes 2097176
  142.5 1.6 %copy-done.2 = bf16[8192,128]{1,0:T(8,128)(2,1)S(1)} copy-done((bf16[8192,128]{1,0:T(8,128)(2,1)S(1)}, bf16[8192,128]{1,0:T(8,128)(2,1)}, u32[]{:S(2)}) %copy-start.2) | copy-done | bytes 2097176
  144.1 2.6 %shard_map.110 = bf16[512,512]{1,0:T(8,128)(2,1)} custom-call(s32[1]{0:T(128)} %bitcast.first_ref, s32[512]{0:T(512)S(1)} %copy-done.13, s32[96]{0:T(128)S(1)} %copy-done.16, bf16[16,512,128]{2,1,0:T(8,128)(2,1)S(1)} %bitcast.6, bf16[512,2048]{1,0:T(8,128)(2,1)S(1)} %copy-done.1, bf16[32,32,512]{2,1,0:T(8,128)(2,1)S(1)} %all-to-all-done.2.came_ref), custom_call_target="tpu_custom_call" | custom-call | flops 1073741824 | bytes 5242880 | tf_op jit(solution)/shard_map/pallas_call | solution.py:274
  146.7 1.7 %all-to-all-done.3.came_ref = bf16[32,32,128]{2,1,0:T(8,128)(2,1)S(1)} async-done(((bf16[32,32,128]{2,1,0:T(8,128)(2,1)}), bf16[32,32,128]{2,1,0:T(8,128)(2,1)S(1)}, u32[]{:S(2)}, u32[]{:S(2)}) %all-to-all-start.3) | async-done | bytes 262176 | tf_op jit(solution)/shard_map/all_to_all | solution.py:170
  148.4 0.9 copy-done.10
  149.3 1.3 shard_map.109
  (31 shorter events, 0.2 us)
Async XLA Ops:
  8.0 132.9 %all-gather.7.cloned.1.call-start = ((), (), s32[]{:S(2)}) async-start(), calls=%async_computation.6 | async-start | bytes 2228224 | tf_op jit(solution)/shard_map/all_gather | solution.py:212
  8.7 0.9 copy-start.5
  9.6 0.7 copy-start.11
  10.3 0.7 copy-start.14
  12.4 29.8 %copy-start.13 = (s32[512]{0:T(512)S(1)}, s32[512]{0:T(512)}, u32[]{:S(2)}) copy-start(s32[512]{0:T(512)} %index_ref.7) | copy-start | bytes 6148
  12.4 29.9 %copy-start.16 = (s32[96]{0:T(128)S(1)}, s32[96]{0:T(128)}, u32[]{:S(2)}) copy-start(s32[96]{0:T(128)} %storage_ref.7) | copy-start | bytes 1156
  12.4 30.4 %copy-start.8 = (bf16[3,64,128]{2,1,0:T(8,128)(2,1)S(1)}, bf16[3,64,128]{2,1,0:T(8,128)(2,1)}, u32[]{:S(2)}) copy-start(bf16[3,64,128]{2,1,0:T(8,128)(2,1)} %adapter_ref.7) | copy-start | bytes 147460
  12.4 25.0 %all-to-all-start = ((bf16[32,32,128]{2,1,0:T(8,128)(2,1)}), bf16[32,32,128]{2,1,0:T(8,128)(2,1)S(1)}, u32[]{:S(2)}, u32[]{:S(2)}) async-start(bf16[32,32,128]{2,1,0:T(8,128)(2,1)} %shard_map.104), calls=%async_computation.1 | async-start | bytes 524288 | tf_op jit(solution)/shard_map/all_to_all | solution.py:170
  26.2 1.0 copy-start.6
  27.3 0.7 copy-start.12
  27.9 0.7 copy-start.15
  28.6 21.8 %copy-start.7 = (bf16[512,512]{1,0:T(8,128)(2,1)S(1)}, bf16[512,512]{1,0:T(8,128)(2,1)}, u32[]{:S(2)}) copy-start(bf16[512,512]{1,0:T(8,128)(2,1)} %rows_ref.2) | copy-start | bytes 1572868
  37.4 44.7 %all-to-all-start.1 = ((bf16[32,32,512]{2,1,0:T(8,128)(2,1)}), bf16[32,32,512]{2,1,0:T(8,128)(2,1)S(1)}, u32[]{:S(2)}, u32[]{:S(2)}) async-start(bf16[32,32,512]{2,1,0:T(8,128)(2,1)} %shard_map.103), calls=%async_computation.2 | async-start | bytes 2097152 | tf_op jit(solution)/shard_map/all_to_all | solution.py:170
  47.1 11.9 %collective-permute-start.1 = (bf16[256,128]{1,0:T(8,128)(2,1)S(1)}, bf16[256,128]{1,0:T(8,128)(2,1)S(1)}, u32[]{:S(2)}, u32[]{:S(2)}) collective-permute-start(bf16[256,128]{1,0:T(8,128)(2,1)S(1)} %dynamic-slice_reduce_fusion.1), channel_id=1, source_target_pairs={{0,2},{1,3},{2,0},{3,1},{4,6},{5,7},{6,4},{7,5},{8,10},{9,11},{10,... | collective-permute-start | bytes 196616 | tf_op jit(solution)/shard_map/ppermute | solution.py:163
  50.4 1.6 %copy-start = (bf16[512,2048]{1,0:T(8,128)(2,1)S(1)}, bf16[512,2048]{1,0:T(8,128)(2,1)}, u32[]{:S(2)}) copy-start(bf16[512,2048]{1,0:T(8,128)(2,1)} %weight_ref.3) | copy-start | bytes 6291460
  52.0 28.1 %copy-start.3 = (bf16[3,64,512]{2,1,0:T(8,128)(2,1)S(1)}, bf16[3,64,512]{2,1,0:T(8,128)(2,1)}, u32[]{:S(2)}) copy-start(bf16[3,64,512]{2,1,0:T(8,128)(2,1)} %adapter_ref.6) | copy-start | bytes 589828
  56.5 35.1 %collective-permute-start = (bf16[8,512,128]{2,1,0:T(8,128)(2,1)}, bf16[8,512,128]{2,1,0:T(8,128)(2,1)}, u32[]{:S(2)}, u32[]{:S(2)}) collective-permute-start(bf16[8,512,128]{2,1,0:T(8,128)(2,1)} %get-tuple-element.11), channel_id=1, source_target_pairs={{0,1},{1,0},{2,3},{3,2},{4,5},{5,4},{6,7},{7,6},{8,9},{9,8},{10,11... | collective-permute-start | bytes 3145736 | tf_op jit(solution)/shard_map/ppermute | solution.py:221
  59.1 8.2 %collective-permute-start.2 = (bf16[256,128]{1,0:T(8,128)(2,1)S(1)}, bf16[256,128]{1,0:T(8,128)(2,1)S(1)}, u32[]{:S(2)}, u32[]{:S(2)}) collective-permute-start(bf16[256,128]{1,0:T(8,128)(2,1)S(1)} %add_convert_fusion.6), channel_id=1, source_target_pairs={{0,4},{1,5},{2,6},{3,7},{4,0},{5,1},{6,2},{7,3},{8,12},{9,13},{10,... | collective-permute-start | bytes 196616 | tf_op jit(solution)/shard_map/ppermute | solution.py:163
  67.3 9.0 %collective-permute-start.3 = (bf16[256,128]{1,0:T(8,128)(2,1)S(1)}, bf16[256,128]{1,0:T(8,128)(2,1)S(1)}, u32[]{:S(2)}, u32[]{:S(2)}) collective-permute-start(bf16[256,128]{1,0:T(8,128)(2,1)S(1)} %add_convert_fusion.5), channel_id=1, source_target_pairs={{0,8},{1,9},{2,10},{3,11},{4,12},{5,13},{6,14},{7,15},{8,0},{9,1},... | collective-permute-start | bytes 196616 | tf_op jit(solution)/shard_map/ppermute | solution.py:163
  82.1 45.2 %all-to-all-start.2 = ((bf16[32,32,512]{2,1,0:T(8,128)(2,1)}), bf16[32,32,512]{2,1,0:T(8,128)(2,1)S(1)}, u32[]{:S(2)}, u32[]{:S(2)}) async-start(bf16[32,32,512]{2,1,0:T(8,128)(2,1)} %shard_map.106), calls=%async_computation.3 | async-start | bytes 2097152 | tf_op jit(solution)/shard_map/all_to_all | solution.py:170
  91.6 55.1 %reduce-scatter.2.cloned.1.call-start = ((), (), s32[]{:S(2)}) async-start(), calls=%async_computation.5 | async-start | bytes 1179648 | tf_op jit(solution)/shard_map/reduce_scatter | solution.py:224
  94.1 31.4 %copy-start.9 = (bf16[3,64,128]{2,1,0:T(8,128)(2,1)S(1)}, bf16[3,64,128]{2,1,0:T(8,128)(2,1)}, u32[]{:S(2)}) copy-start(bf16[3,64,128]{2,1,0:T(8,128)(2,1)} %adapter_ref.7) | copy-start | bytes 147460
  94.2 0.9 copy-start.4
  99.0 5.3 %collective-permute-start.4 = (bf16[256,128]{1,0:T(8,128)(2,1)S(1)}, bf16[256,128]{1,0:T(8,128)(2,1)S(1)}, u32[]{:S(2)}, u32[]{:S(2)}) collective-permute-start(bf16[256,128]{1,0:T(8,128)(2,1)S(1)} %dynamic-slice_reduce_fusion), channel_id=1, source_target_pairs={{0,2},{1,3},{2,0},{3,1},{4,6},{5,7},{6,4},{7,5},{8,10},{9,11},{10,... | collective-permute-start | bytes 196616 | tf_op jit(solution)/shard_map/ppermute | solution.py:163
  104.3 6.9 %collective-permute-start.5 = (bf16[256,128]{1,0:T(8,128)(2,1)S(1)}, bf16[256,128]{1,0:T(8,128)(2,1)S(1)}, u32[]{:S(2)}, u32[]{:S(2)}) collective-permute-start(bf16[256,128]{1,0:T(8,128)(2,1)S(1)} %add_convert_fusion.3), channel_id=1, source_target_pairs={{0,4},{1,5},{2,6},{3,7},{4,0},{5,1},{6,2},{7,3},{8,12},{9,13},{10,... | collective-permute-start | bytes 196616 | tf_op jit(solution)/shard_map/ppermute | solution.py:163
  111.2 9.1 %collective-permute-start.6 = (bf16[256,128]{1,0:T(8,128)(2,1)S(1)}, bf16[256,128]{1,0:T(8,128)(2,1)S(1)}, u32[]{:S(2)}, u32[]{:S(2)}) collective-permute-start(bf16[256,128]{1,0:T(8,128)(2,1)S(1)} %add_convert_fusion.2), channel_id=1, source_target_pairs={{0,8},{1,9},{2,10},{3,11},{4,12},{5,13},{6,14},{7,15},{8,0},{9,1},... | collective-permute-start | bytes 196616 | tf_op jit(solution)/shard_map/ppermute | solution.py:163
  127.3 21.1 %all-to-all-start.3 = ((bf16[32,32,128]{2,1,0:T(8,128)(2,1)}), bf16[32,32,128]{2,1,0:T(8,128)(2,1)S(1)}, u32[]{:S(2)}, u32[]{:S(2)}) async-start(bf16[32,32,128]{2,1,0:T(8,128)(2,1)} %shard_map.108), calls=%async_computation.4 | async-start | bytes 524288 | tf_op jit(solution)/shard_map/all_to_all | solution.py:170
  140.9 1.6 %copy-start.1 = (bf16[512,2048]{1,0:T(8,128)(2,1)S(1)}, bf16[512,2048]{1,0:T(8,128)(2,1)}, u32[]{:S(2)}) copy-start(bf16[512,2048]{1,0:T(8,128)(2,1)} %weight_ref.3) | copy-start | bytes 6291460
  142.5 1.6 %copy-start.2 = (bf16[8192,128]{1,0:T(8,128)(2,1)S(1)}, bf16[8192,128]{1,0:T(8,128)(2,1)}, u32[]{:S(2)}) copy-start(bf16[8192,128]{1,0:T(8,128)(2,1)} %all-gather.7.cloned.1.call-done) | copy-start | bytes 6291460
  148.4 0.9 copy-start.10
Sparse Core Ops, SparseCore 0:
  11.0 47.7 all-gather.6
Sparse Core Ops, SparseCore 1:
  94.9 38.1 reduce-scatter.1

commit v2 on v1

v2 whole, which is shorter than its diff:
```python
import functools

import jax
import jax.numpy as jnp
from jax import lax
from jax.experimental import pallas as pl
from jax.experimental.pallas import tpu as pltpu
from jax.sharding import PartitionSpec as P

adapter_scale = 0.25
f32 = jnp.float32
bf16 = jnp.bfloat16
SMEM = pl.BlockSpec(memory_space=pltpu.SMEM)
VMEM = pl.BlockSpec(memory_space=pltpu.VMEM)
VMEM_LIMIT = 40 * 1024 * 1024


def local_call(body, out_shape, specs, scratch=(), flops=0, moved=0):
    multiple = isinstance(out_shape, (tuple, list))
    return pl.pallas_call(
        body,
        out_shape=out_shape,
        in_specs=specs,
        out_specs=(VMEM,) * len(out_shape) if multiple else VMEM,
        scratch_shapes=list(scratch),
        compiler_params=pltpu.CompilerParams(vmem_limit_bytes=VMEM_LIMIT),
        cost_estimate=pl.CostEstimate(flops=flops, bytes_accessed=moved, transcendentals=0),
    )


def owner_of(place_ref, index_ref, storage_ref, held, j):
    return storage_ref[index_ref[place_ref[0] + j]] // held


def spread_body(held, place_ref, index_ref, storage_ref, tokens_ref, cot_ref, out_ref):
    slots, length, width = out_ref.shape
    block = tokens_ref.shape[1]
    out_ref[...] = jnp.zeros_like(out_ref)
    for j in range(tokens_ref.shape[0] // length):
        owner = owner_of(place_ref, index_ref, storage_ref, held, j)
        at = slice(j * length, (j + 1) * length)
        out_ref[owner, :, :block] = tokens_ref[at, :]
        out_ref[owner, :, block:] = cot_ref[at, :]


def block_columns(place_ref, offset, blocks, width):
    chip = lax.rem(place_ref[2] + offset, blocks)
    return pl.ds(pl.multiple_of(chip * width, width), width)


def projection_body(place_ref, tokens_ref, weight_ref, own_ref, send_ref):
    blocks, rows, width = own_ref.shape
    core = place_ref[1]
    tokens = tokens_ref[...]
    for b in range(blocks):
        columns = block_columns(place_ref, b, blocks, 2 * width)
        part = jnp.dot(tokens, weight_ref[:, columns], preferred_element_type=f32).astype(bf16)
        low, high = part[:, :width], part[:, width:]

        @pl.when(core == 0)
        def _():
            own_ref[b] = low
            send_ref[b] = high

        @pl.when(core != 0)
        def _():
            own_ref[b] = high
            send_ref[b] = low


def pair_body(own_ref, came_ref, *out_refs):
    for b, out_ref in enumerate(out_refs):
        out_ref[...] = (own_ref[b].astype(f32) + came_ref[b].astype(f32)).astype(bf16)


def rank_body(pick_ref, rows_ref, down_ref, up_ref, out_ref):
    slots, length, width = rows_ref.shape
    held, rank, block = down_ref.shape
    flat = rows_ref[...].reshape(slots * length, width)
    dims = (((1,), (1,)), ((), ()))
    inner = [
        lax.dot_general(flat[:, :block], down_ref[a], dims, preferred_element_type=f32)
        for a in range(held)
    ]
    back = [
        lax.dot_general(flat[:, block:], up_ref[a], dims, preferred_element_type=f32)
        for a in range(held)
    ]
    joined = [jnp.concatenate([inner[a], back[a]], axis=1) for a in range(held)]
    for s in range(slots):
        at = slice(s * length, (s + 1) * length)
        value = jnp.zeros((length, 2 * rank), f32)
        for a in range(held):
            value = jnp.where(pick_ref[s] == a, joined[a][at], value)
        out_ref[at, :] = value.astype(bf16)


def total_body(parts_ref, out_ref):
    total = jnp.sum(parts_ref[...].astype(f32), axis=0).astype(bf16)
    for b in range(out_ref.shape[0]):
        out_ref[b] = total


def fill_masked(pick_ref, ranks_ref, masked_ref, left, slots, held, rank):
    length = ranks_ref.shape[0] // slots
    for s in range(slots):
        at = slice(s * length, (s + 1) * length)
        block = ranks_ref[at, :][:, left : left + rank]
        for a in range(held):
            masked_ref[at, a * rank : (a + 1) * rank] = jnp.where(
                pick_ref[s] == a, block, jnp.zeros_like(block)
            )


def expand_body(pick_ref, ranks_ref, down_ref, up_ref, out_ref, inner_ref, back_ref):
    slots, length, width = out_ref.shape
    held, rank, block = down_ref.shape
    fill_masked(pick_ref, ranks_ref, inner_ref, 0, slots, held, rank)
    fill_masked(pick_ref, ranks_ref, back_ref, rank, slots, held, rank)
    down = down_ref[...].reshape(held * rank, block)
    up = up_ref[...].reshape(held * rank, width - block)
    token_part = jnp.dot(back_ref[...], down, preferred_element_type=f32) * adapter_scale
    output_part = jnp.dot(inner_ref[...], up, preferred_element_type=f32) * adapter_scale
    out_ref[:, :, :block] = token_part.astype(bf16).reshape(slots, length, block)
    out_ref[:, :, block:] = output_part.astype(bf16).reshape(slots, length, width - block)


def gradient_body(
    pick_ref, scale_ref, ranks_ref, rows_ref, down_out_ref, up_out_ref, inner_ref, back_ref
):
    slots, length, width = rows_ref.shape
    held, rank, block = down_out_ref.shape
    fill_masked(pick_ref, ranks_ref, inner_ref, 0, slots, held, rank)
    fill_masked(pick_ref, ranks_ref, back_ref, rank, slots, held, rank)
    flat = rows_ref[...].reshape(slots * length, width)
    dims = (((0,), (0,)), ((), ()))
    down = lax.dot_general(back_ref[...], flat[:, :block], dims, preferred_element_type=f32)
    up = lax.dot_general(inner_ref[...], flat[:, block:], dims, preferred_element_type=f32)
    for a in range(held):
        at = slice(a * rank, (a + 1) * rank)
        down_out_ref[a] = down[at] * scale_ref[a]
        up_out_ref[a] = up[at] * scale_ref[a]


def base_body(offsets, place_ref, own_ref, other_ref, weight_ref, out_ref):
    blocks, rows, width = own_ref.shape
    dims = (((1,), (1,)), ((), ()))
    first_core = place_ref[1] == 0
    for b, offset in enumerate(offsets):
        own, other = own_ref[b], other_ref[b]
        low = jnp.where(first_core, own, other)
        high = jnp.where(first_core, other, own)
        pair = jnp.concatenate([low, high], axis=1)
        columns = block_columns(place_ref, offset, blocks, 2 * width)
        part = lax.dot_general(pair, weight_ref[:, columns], dims, preferred_element_type=f32)
        out_ref[...] = part if b == 0 else out_ref[...] + part


def final_body(held, place_ref, index_ref, storage_ref, base_ref, came_ref, *refs):
    part_refs, (token_out_ref, output_ref) = refs[:-2], refs[-2:]
    slots, length, width = came_ref.shape
    block = base_ref.shape[1]
    for j in range(base_ref.shape[0] // length):
        owner = owner_of(place_ref, index_ref, storage_ref, held, j)
        at = slice(j * length, (j + 1) * length)
        came = came_ref[owner].astype(f32)
        token_out_ref[at, :] = (base_ref[at, :] + came[:, :block]).astype(bf16)
        total = came[:, block:]
        for part_ref in part_refs:
            total = total + part_ref[at, :].astype(f32)
        output_ref[at, :] = total.astype(bf16)


def exchange(value, axis, groups=None):
    return lax.all_to_all(
        value, axis, split_axis=0, concat_axis=0, axis_index_groups=groups, tiled=True
    )


def after(value, earlier):
    return lax.optimization_barrier((value, earlier))[0]


def on_device(tokens, weight, down, up, cotangent, sequence_index, storage_row):
    dp_count = lax.axis_size("dp")
    tensor_count = lax.axis_size("tensor")
    chips = tensor_count // 2
    me = lax.axis_index("dp")
    here = lax.axis_index("tensor")
    held, rank, block = down.shape
    out_block = up.shape[2]
    rows = tokens.shape[0]
    seqs = sequence_index.shape[0] // dp_count
    length = rows // seqs
    slots = dp_count
    width = block + out_block
    core = here & 1
    chip = here >> 1
    place = jnp.stack([me * seqs, core, chip, me]).astype(jnp.int32)
    pairs = [[t, t + 1] for t in range(0, tensor_count, 2)]
    same_core = [list(range(c, tensor_count, 2)) for c in range(2)]

    def shape(*dims, dtype=bf16):
        return jax.ShapeDtypeStruct(dims, dtype)

    def moved_along(value, distance):
        perm = [(t, (t + 2 * distance) % tensor_count) for t in range(tensor_count)]
        return lax.ppermute(value, "tensor", perm)

    spread = local_call(
        functools.partial(spread_body, held),
        shape(slots, length, width),
        [SMEM, SMEM, SMEM, VMEM, VMEM],
        moved=3 * slots * length * width,
    )(place, sequence_index, storage_row, tokens, cotangent)
    arrived = exchange(spread, "dp")

    codes = jnp.arange(storage_row.shape[0], dtype=jnp.int32)
    matches = sequence_index[:, None] == codes[None, :]
    seq_rows = jnp.sum(jnp.where(matches, storage_row[None, :], 0), axis=1)
    local = seq_rows - held * me
    local = jnp.where((local >= 0) & (local < held), local, -1)
    pick = jnp.max(local.reshape(dp_count, seqs), axis=1).astype(jnp.int32)
    usage = jnp.sum((pick[:, None] == jnp.arange(held)[None, :]).astype(f32), axis=0)
    scale = adapter_scale / jnp.maximum(usage, 1.0)

    own, send = local_call(
        projection_body,
        (shape(chips, rows, out_block), shape(chips, rows, out_block)),
        [SMEM, VMEM, VMEM],
        flops=2 * rows * block * tensor_count * out_block,
        moved=2 * (rows * block + 2 * block * tensor_count * out_block),
    )(after(place, spread), tokens, weight)
    swap = [(t, t ^ 1) for t in range(tensor_count)]
    came = lax.ppermute(send, "tensor", swap)
    paired = local_call(
        pair_body,
        (shape(rows, out_block),) * chips,
        [VMEM, VMEM],
        moved=6 * chips * rows * out_block,
    )(own, came)
    parts = [paired[0]] + [moved_along(paired[d], d) for d in range(1, chips)]
    arrived, parts = lax.optimization_barrier((arrived, parts))

    half = slots * length // 2
    part = local_call(
        rank_body,
        shape(slots * length, 2 * rank),
        [SMEM, VMEM, VMEM, VMEM],
        flops=2 * slots * length * width * held * rank,
        moved=2 * slots * length * width,
    )(pick, arrived, down, up)
    both = lax.all_gather(part, "tensor", axis_index_groups=pairs)
    mine = lax.dynamic_slice_in_dim(both, core * half, half, axis=1)
    mine = mine.astype(f32).sum(0).astype(bf16).reshape(chips, half // chips, 2 * rank)
    totals = local_call(
        total_body,
        shape(*mine.shape),
        [VMEM],
        moved=4 * half * 2 * rank,
    )(exchange(mine, "tensor", same_core))
    shared = exchange(totals, "tensor", same_core).reshape(half, 2 * rank)
    ranks = lax.all_gather(shared, "tensor", axis_index_groups=pairs).reshape(part.shape)

    masked = pltpu.VMEM((slots * length, held * rank), bf16)
    contributions = local_call(
        expand_body,
        shape(slots, length, width),
        [SMEM, VMEM, VMEM, VMEM],
        [masked, masked],
        flops=2 * slots * length * width * held * rank,
        moved=2 * slots * length * width,
    )(pick, ranks, down, up)
    returned = exchange(contributions, "dp")

    right = left = after(cotangent, contributions)
    pieces, offsets = [right], [0]
    for d in range(1, chips // 2 + 1):
        right = moved_along(right, 1)
        pieces.append(right)
        offsets.append(chips - d)
        if d < chips - d:
            left = moved_along(left, -1)
            pieces.append(left)
            offsets.append(d)
    own_cot = jnp.stack(pieces)
    other_cot = lax.ppermute(own_cot, "tensor", swap)

    grad_down, grad_up = local_call(
        gradient_body,
        (shape(held, rank, block, dtype=f32), shape(held, rank, out_block, dtype=f32)),
        [SMEM, SMEM, VMEM, VMEM],
        [masked, masked],
        flops=2 * slots * length * width * held * rank,
        moved=2 * slots * length * width,
    )(pick, scale, ranks, arrived)
    base = local_call(
        functools.partial(base_body, offsets),
        shape(rows, block, dtype=f32),
        [SMEM, VMEM, VMEM, VMEM],
        flops=2 * rows * block * tensor_count * out_block,
        moved=2 * (2 * rows * tensor_count * out_block),
    )(place, own_cot, other_cot, weight)
    token_gradient, key_value_output = local_call(
        functools.partial(final_body, held),
        (shape(rows, block), shape(rows, out_block)),
        [SMEM, SMEM, SMEM, VMEM, VMEM] + [VMEM] * chips,
        moved=2 * (3 * rows * block + slots * length * width),
    )(place, sequence_index, storage_row, base, returned, *parts)
    return (key_value_output, token_gradient, grad_down, grad_up)


def solution(mesh):
    in_specs = (
        P("dp", "tensor"),
        P("tensor", None),
        P("dp", None, "tensor"),
        P("dp", None, "tensor"),
        P("dp", "tensor"),
        P(),
        P(),
    )
    out_specs = (
        P("dp", "tensor"),
        P("dp", "tensor"),
        P("dp", None, "tensor"),
        P("dp", None, "tensor"),
    )
    return jax.shard_map(
        on_device, mesh=mesh, in_specs=in_specs, out_specs=out_specs, check_vma=False
    )
```

time: 160 us -> 161 us (level)
  blocking collectives: 14.7 us -> 29.6 us
  between operations: 15.7 us -> 1.15 us
  starting transfers between devices: 65.7 us -> 80 us
  Pallas kernels: 21.8 us -> 15.3 us
  local copies, waits for them, and re-layouts: 11.5 us -> 7.88 us
  other arithmetic: 3.01 us -> 0.47 us
    ppermute x7 -> x16, starting transfers between devices: 28 us -> 56.5 us  [the longest x14 47.3 us: moved_along(): return lax.ppermute(value, 'tensor', perm)]
    all_to_all x0 -> x2, blocking collectives: none -> 22 us  [exchange(): lax.all_to_all(value, axis, split_axis=0, concat_axis=0, axis_index_group...]
    all_to_all x4 -> x2, starting transfers between devices: 37.6 us -> 23.5 us  [exchange(): lax.all_to_all(value, axis, split_axis=0, concat_axis=0, axis_index_group...]
    ppermute x7 -> x16, waiting for transfers between devices: 16.2 us -> 25.9 us  [the longest x14 23.7 us: moved_along(): return lax.ppermute(value, 'tensor', perm)]
    all_to_all x4 -> x2, waiting for transfers between devices: 8.82 us -> 0.01 us  [exchange(): lax.all_to_all(value, axis, split_axis=0, concat_axis=0, axis_index_group...]
    all_gather x4 -> x2, blocking collectives: 14.7 us -> 7.56 us  [the longest x1 4.8 us: on_device(): lax.all_gather(shared, 'tensor', axis_index_groups=pairs)]
    pallas_call x11 -> x9, Pallas kernels: 21.8 us -> 15.3 us  [the longest x1 4.15 us: on_device(): local_call(projection_body, (shape(chips, rows, out_block), shape(chips,...]
    unnamed x34 -> x53, local copies, waits for them, and re-layouts: 11.2 us -> 7.78 us
  transfers between devices with their start and end apart: 13 -> 18, of which waited for: 7 -> 8; matrix products, arithmetic and copies ran while one was open for 2% -> 0% of each run, Pallas kernels for 13% -> 5%
where the time goes in v2:
time: 161 us; the launch traced here: 160 us
  starting transfers between devices  80 us (50%)
  blocking collectives  29.6 us (18%)
  waiting for transfers between devices  26 us (16%)
  Pallas kernels  15.3 us (10%)
  local copies, waits for them, and re-layouts  7.88 us (5%)
    ppermute x14, starting transfers between devices, moved_along(): return lax.ppermute(value, 'tensor', perm)  47.3 us
    ppermute x14, waiting for transfers between devices, moved_along(): return lax.ppermute(value, 'tensor', perm)  23.7 us
    all_to_all x2, starting transfers between devices, exchange(): lax.all_to_all(value, axis, split_axis=0, concat_axis=0, axis_index_group...  23.5 us
    all_to_all x2, blocking collectives, exchange(): lax.all_to_all(value, axis, split_axis=0, concat_axis=0, axis_index_group...  22 us
    unnamed x53, local copies, waits for them, and re-layouts  7.78 us
    ppermute x1, starting transfers between devices, on_device(): other_cot = lax.ppermute(own_cot, 'tensor', swap)  6.26 us
    all_gather x1, blocking collectives, on_device(): lax.all_gather(shared, 'tensor', axis_index_groups=pairs)  4.8 us
    pallas_call x1, Pallas kernels, on_device(): local_call(projection_body, (shape(chips, rows, out_block), shape(chips,...  4.15 us
  transfers between devices with their start and end apart: 18, of which 8 were waited for; matrix products, arithmetic and copies ran while one was open for 0% of the time, Pallas kernels for 5%

profile of v2, /device:TPU:1, one launch (start us, length us, event | category | flops | bytes accessed | tf_op | source)
XLA Modules:
  0.0 160.3 jit_solution(7731874366962056827)
XLA Ops:
  0.6 0.1 pad_add_fusion.place_ref
  0.7 0.9 copy-done.6
  1.6 1.0 copy-done.8
  2.7 0.7 copy-done.19
  3.3 0.7 copy-done.21
  4.0 1.8 %shard_map.102 = bf16[32,32,640]{2,1,0:T(8,128)(2,1)} custom-call(s32[4]{0:T(128)S(1)} %pad_add_fusion.place_ref, s32[512]{0:T(512)S(1)} %copy-done.19, s32[96]{0:T(128)S(1)} %copy-done.21, bf16[512,512]{1,0:T(8,128)(2,1)S(1)} %copy-done.8, bf16[512,128]{1,0:T(8,128)(2,1)S(1)} %copy-done.6), custom_call_target="tpu_custom_call" | custom-call | bytes 1966080 | tf_op jit(solution)/shard_map/pallas_call | solution.py:210
  5.8 13.8 %all-to-all-start = ((bf16[32,32,640]{2,1,0:T(8,128)(2,1)}), bf16[32,32,640]{2,1,0:T(8,128)(2,1)S(1)}, u32[]{:S(2)}, u32[]{:S(2)}) async-start(bf16[32,32,640]{2,1,0:T(8,128)(2,1)} %shard_map.102), calls=%async_computation | async-start | bytes 2621440 | tf_op jit(solution)/shard_map/all_to_all | solution.py:175
  19.7 0.0 copy-start.9
  19.7 1.0 copy-done.9
  20.7 4.1 %shard_map.103 = (bf16[8,512,128]{2,1,0:T(8,128)(2,1)S(1)}, bf16[8,512,128]{2,1,0:T(8,128)(2,1)S(1)}) custom-call(s32[4]{0:T(128)S(1)} %pad_add_fusion.place_ref, bf16[512,512]{1,0:T(8,128)(2,1)S(1)} %copy-done.9, bf16[512,2048]{1,0:T(8,128)(2,1)S(1)} %copy-done.3), custom_call_target="tpu_custom_call" | custom-call | flops 1073741824 | bytes 4718592 | tf_op jit(solution)/shard_map/pallas_call | solution.py:227
  24.9 0.0 copy-start.20
  24.9 0.0 copy-start.22
  24.9 0.0 copy-start.5
  24.9 0.0 copy-start.10
  24.9 3.0 %collective-permute-start = (bf16[8,512,128]{2,1,0:T(8,128)(2,1)S(1)}, bf16[8,512,128]{2,1,0:T(8,128)(2,1)S(1)}, u32[]{:S(2)}, u32[]{:S(2)}) collective-permute-start(bf16[8,512,128]{2,1,0:T(8,128)(2,1)S(1)} %get-tuple-element.31), channel_id=1, source_target_pairs={{0,1},{1,0},{2,3},{3,2},{4,5},{5,4},{6,7},{7,6},{8,9},{9,8},{10,11... | collective-permute-start | bytes 3145736 | tf_op jit(solution)/shard_map/ppermute | solution.py:235
  27.9 2.3 %collective-permute-done.came_ref = bf16[8,512,128]{2,1,0:T(8,128)(2,1)S(1)} collective-permute-done((bf16[8,512,128]{2,1,0:T(8,128)(2,1)S(1)}, bf16[8,512,128]{2,1,0:T(8,128)(2,1)S(1)}, u32[]{:S(2)}, u32[]{:S(2)}) %collective-permute-start) | collective-permute-done | bytes 1048608 | tf_op jit(solution)/shard_map/ppermute | solution.py:235
  30.2 0.2 shard_map.104
  30.4 3.2 %collective-permute-start.1 = (bf16[512,128]{1,0:T(8,128)(2,1)S(1)}, bf16[512,128]{1,0:T(8,128)(2,1)S(1)}, u32[]{:S(2)}, u32[]{:S(2)}) collective-permute-start(bf16[512,128]{1,0:T(8,128)(2,1)S(1)} %get-tuple-element.33), channel_id=1, source_target_pairs={{0,2},{1,3},{2,4},{3,5},{4,6},{5,7},{6,8},{7,9},{8,10},{9,11},{10,... | collective-permute-start | bytes 393224 | tf_op jit(solution)/shard_map/ppermute | solution.py:208
  33.6 4.2 %collective-permute-start.2 = (bf16[512,128]{1,0:T(8,128)(2,1)S(1)}, bf16[512,128]{1,0:T(8,128)(2,1)S(1)}, u32[]{:S(2)}, u32[]{:S(2)}) collective-permute-start(bf16[512,128]{1,0:T(8,128)(2,1)S(1)} %get-tuple-element.34), channel_id=1, source_target_pairs={{0,4},{1,5},{2,6},{3,7},{4,8},{5,9},{6,10},{7,11},{8,12},{9,13},{1... | collective-permute-start | bytes 393224 | tf_op jit(solution)/shard_map/ppermute | solution.py:208
  37.9 0.1 select_reduce_fusion
  38.0 4.6 %collective-permute-start.3 = (bf16[512,128]{1,0:T(8,128)(2,1)S(1)}, bf16[512,128]{1,0:T(8,128)(2,1)S(1)}, u32[]{:S(2)}, u32[]{:S(2)}) collective-permute-start(bf16[512,128]{1,0:T(8,128)(2,1)S(1)} %get-tuple-element.35), channel_id=1, source_target_pairs={{0,6},{1,7},{2,8},{3,9},{4,10},{5,11},{6,12},{7,13},{8,14},{9,15},... | collective-permute-start | bytes 393224 | tf_op jit(solution)/shard_map/ppermute | solution.py:208
  42.6 3.5 %collective-permute-start.4 = (bf16[512,128]{1,0:T(8,128)(2,1)S(1)}, bf16[512,128]{1,0:T(8,128)(2,1)S(1)}, u32[]{:S(2)}, u32[]{:S(2)}) collective-permute-start(bf16[512,128]{1,0:T(8,128)(2,1)S(1)} %get-tuple-element.36), channel_id=1, source_target_pairs={{0,8},{1,9},{2,10},{3,11},{4,12},{5,13},{6,14},{7,15},{8,0},{9,1},... | collective-permute-start | bytes 393224 | tf_op jit(solution)/shard_map/ppermute | solution.py:208
  46.2 4.9 %collective-permute-start.5 = (bf16[512,128]{1,0:T(8,128)(2,1)S(1)}, bf16[512,128]{1,0:T(8,128)(2,1)S(1)}, u32[]{:S(2)}, u32[]{:S(2)}) collective-permute-start(bf16[512,128]{1,0:T(8,128)(2,1)S(1)} %get-tuple-element.37), channel_id=1, source_target_pairs={{0,10},{1,11},{2,12},{3,13},{4,14},{5,15},{6,0},{7,1},{8,2},{9,3},... | collective-permute-start | bytes 393224 | tf_op jit(solution)/shard_map/ppermute | solution.py:208
  51.1 0.0 collective-permute-done.1.refs_1_
  51.1 5.0 %collective-permute-start.6 = (bf16[512,128]{1,0:T(8,128)(2,1)S(1)}, bf16[512,128]{1,0:T(8,128)(2,1)S(1)}, u32[]{:S(2)}, u32[]{:S(2)}) collective-permute-start(bf16[512,128]{1,0:T(8,128)(2,1)S(1)} %get-tuple-element.38), channel_id=1, source_target_pairs={{0,12},{1,13},{2,14},{3,15},{4,0},{5,1},{6,2},{7,3},{8,4},{9,5},{1... | collective-permute-start | bytes 393224 | tf_op jit(solution)/shard_map/ppermute | solution.py:208
  56.1 0.0 collective-permute-done.2.refs_2_
  56.1 3.0 %collective-permute-start.7 = (bf16[512,128]{1,0:T(8,128)(2,1)S(1)}, bf16[512,128]{1,0:T(8,128)(2,1)S(1)}, u32[]{:S(2)}, u32[]{:S(2)}) collective-permute-start(bf16[512,128]{1,0:T(8,128)(2,1)S(1)} %get-tuple-element.39), channel_id=1, source_target_pairs={{0,14},{1,15},{2,0},{3,1},{4,2},{5,3},{6,4},{7,5},{8,6},{9,7},{10,... | collective-permute-start | bytes 393224 | tf_op jit(solution)/shard_map/ppermute | solution.py:208
  59.1 0.1 sub.12
  59.2 0.1 select_reduce_fusion.1.pick_ref
  59.3 0.0 collective-permute-done.4.refs_4_
  59.3 0.0 copy-start.11
  59.3 3.0 %collective-permute-done.5.refs_5_ = bf16[512,128]{1,0:T(8,128)(2,1)S(1)} collective-permute-done((bf16[512,128]{1,0:T(8,128)(2,1)S(1)}, bf16[512,128]{1,0:T(8,128)(2,1)S(1)}, u32[]{:S(2)}, u32[]{:S(2)}) %collective-permute-start.5) | collective-permute-done | bytes 131104 | tf_op jit(solution)/shard_map/ppermute | solution.py:208
  62.3 7.7 %collective-permute-done.6.refs_6_ = bf16[512,128]{1,0:T(8,128)(2,1)S(1)} collective-permute-done((bf16[512,128]{1,0:T(8,128)(2,1)S(1)}, bf16[512,128]{1,0:T(8,128)(2,1)S(1)}, u32[]{:S(2)}, u32[]{:S(2)}) %collective-permute-start.6) | collective-permute-done | bytes 131104 | tf_op jit(solution)/shard_map/ppermute | solution.py:208
  70.0 0.9 collective-permute-done.7.refs_7_
  70.9 0.0 all-to-all-done.rows_ref
  70.9 1.8 %shard_map.105 = bf16[1024,128]{1,0:T(8,128)(2,1)S(1)} custom-call(s32[32]{0:T(128)S(1)} %select_reduce_fusion.1.pick_ref, bf16[32,32,640]{2,1,0:T(8,128)(2,1)S(1)} %all-to-all-done.rows_ref, bf16[3,64,512]{2,1,0:T(8,128)(2,1)S(1)} %copy-done.5, bf16[3,64,128]{2,1,0:T(8,128)(2,1)S(1)} %copy-done.10), custom_call_target="tpu_custom_call" | custom-call | flops 251658240 | bytes 1310720 | tf_op jit(solution)/shard_map/pallas_call | solution.py:246
  72.7 2.8 %all-gather = bf16[2048,128]{1,0:T(8,128)(2,1)S(1)} all-gather(bf16[1024,128]{1,0:T(8,128)(2,1)S(1)} %shard_map.105), channel_id=2, replica_groups={{0,1},{2,3},{4,5},{6,7},{8,9},{10,11},{12,13},{14,15},{16,17},{18,19},{..., dimensions={0}, use_global_device_ids=true | all-gather | bytes 786432 | tf_op jit(solution)/shard_map/all_gather | solution.py:253
  75.5 11.6 %all_to_all.20.parts_ref = bf16[8,64,128]{2,1,0:T(8,128)(2,1)S(1)} all-to-all(bf16[8,64,128]{2,1,0:T(8,128)(2,1)S(1)} %bitcast.28), channel_id=1, replica_groups={{0,2,4,6,8,10,12,14},{1,3,5,7,9,11,13,15},{16,18,20,22,24,26,28,30},{17..., dimensions={0} | all-to-all | bytes 262144 | tf_op jit(solution)/shard_map/all_to_all | solution.py:175
  87.2 10.4 %all_to_all.21 = bf16[8,64,128]{2,1,0:T(8,128)(2,1)S(1)} all-to-all(bf16[8,64,128]{2,1,0:T(8,128)(2,1)S(1)} %shard_map.106), channel_id=1, replica_groups={{0,2,4,6,8,10,12,14},{1,3,5,7,9,11,13,15},{16,18,20,22,24,26,28,30},{17..., dimensions={0} | all-to-all | bytes 262144 | tf_op jit(solution)/shard_map/all_to_all | solution.py:175
  97.6 4.8 %all_gather.11 = bf16[2,512,128]{2,1,0:T(8,128)(2,1)S(1)} all-gather(bf16[1,512,128]{2,1,0:T(8,128)(2,1)S(1)} %bitcast.27), channel_id=1, replica_groups={{0,1},{2,3},{4,5},{6,7},{8,9},{10,11},{12,13},{14,15},{16,17},{18,19},{..., dimensions={0}, use_global_device_ids=true | all-gather | bytes 393216 | tf_op jit(solution)/shard_map/all_gather | solution.py:263
  102.4 1.4 shard_map.107
  103.8 1.1 copy-done
  104.9 9.6 %all-to-all-start.3 = ((bf16[32,32,640]{2,1,0:T(8,128)(2,1)}), bf16[32,32,640]{2,1,0:T(8,128)(2,1)S(1)}, u32[]{:S(2)}, u32[]{:S(2)}) async-start(bf16[32,32,640]{2,1,0:T(8,128)(2,1)} %copy-done), calls=%async_computation.3 | async-start | bytes 2621440 | tf_op jit(solution)/shard_map/all_to_all | solution.py:175
  114.5 2.1 %collective-permute-start.9 = (bf16[512,128]{1,0:T(8,128)(2,1)S(1)}, bf16[512,128]{1,0:T(8,128)(2,1)S(1)}, u32[]{:S(2)}, u32[]{:S(2)}) collective-permute-start(bf16[512,128]{1,0:T(8,128)(2,1)S(1)} %copy-done.7), channel_id=1, source_target_pairs={{0,14},{1,15},{2,0},{3,1},{4,2},{5,3},{6,4},{7,5},{8,6},{9,7},{10,... | collective-permute-start | bytes 393224 | tf_op jit(solution)/shard_map/ppermute | solution.py:208
  116.6 3.2 %collective-permute-start.8 = (bf16[512,128]{1,0:T(8,128)(2,1)S(1)}, bf16[512,128]{1,0:T(8,128)(2,1)S(1)}, u32[]{:S(2)}, u32[]{:S(2)}) collective-permute-start(bf16[512,128]{1,0:T(8,128)(2,1)S(1)} %copy-done.7), channel_id=1, source_target_pairs={{0,2},{1,3},{2,4},{3,5},{4,6},{5,7},{6,8},{7,9},{8,10},{9,11},{10,... | collective-permute-start | bytes 393224 | tf_op jit(solution)/shard_map/ppermute | solution.py:208
  119.8 1.0 collective-permute-done.9
  120.8 3.3 %collective-permute-start.11 = (bf16[512,128]{1,0:T(8,128)(2,1)S(1)}, bf16[512,128]{1,0:T(8,128)(2,1)S(1)}, u32[]{:S(2)}, u32[]{:S(2)}) collective-permute-start(bf16[512,128]{1,0:T(8,128)(2,1)S(1)} %collective-permute-done.9), channel_id=1, source_target_pairs={{0,14},{1,15},{2,0},{3,1},{4,2},{5,3},{6,4},{7,5},{8,6},{9,7},{10,... | collective-permute-start | bytes 393224 | tf_op jit(solution)/shard_map/ppermute | solution.py:208
  124.1 0.0 collective-permute-done.8
  124.1 2.0 %collective-permute-start.10 = (bf16[512,128]{1,0:T(8,128)(2,1)S(1)}, bf16[512,128]{1,0:T(8,128)(2,1)S(1)}, u32[]{:S(2)}, u32[]{:S(2)}) collective-permute-start(bf16[512,128]{1,0:T(8,128)(2,1)S(1)} %collective-permute-done.8), channel_id=1, source_target_pairs={{0,2},{1,3},{2,4},{3,5},{4,6},{5,7},{6,8},{7,9},{8,10},{9,11},{10,... | collective-permute-start | bytes 393224 | tf_op jit(solution)/shard_map/ppermute | solution.py:208
  126.2 0.6 collective-permute-done.11
  126.8 4.5 %collective-permute-start.13 = (bf16[512,128]{1,0:T(8,128)(2,1)S(1)}, bf16[512,128]{1,0:T(8,128)(2,1)S(1)}, u32[]{:S(2)}, u32[]{:S(2)}) collective-permute-start(bf16[512,128]{1,0:T(8,128)(2,1)S(1)} %collective-permute-done.11), channel_id=1, source_target_pairs={{0,14},{1,15},{2,0},{3,1},{4,2},{5,3},{6,4},{7,5},{8,6},{9,7},{10,... | collective-permute-start | bytes 393224 | tf_op jit(solution)/shard_map/ppermute | solution.py:208
  131.3 0.0 collective-permute-done.10
  131.3 1.9 %collective-permute-start.12 = (bf16[512,128]{1,0:T(8,128)(2,1)S(1)}, bf16[512,128]{1,0:T(8,128)(2,1)S(1)}, u32[]{:S(2)}, u32[]{:S(2)}) collective-permute-start(bf16[512,128]{1,0:T(8,128)(2,1)S(1)} %collective-permute-done.10), channel_id=1, source_target_pairs={{0,2},{1,3},{2,4},{3,5},{4,6},{5,7},{6,8},{7,9},{8,10},{9,11},{10,... | collective-permute-start | bytes 393224 | tf_op jit(solution)/shard_map/ppermute | solution.py:208
  133.2 0.0 copy-start.4
  133.3 5.2 %collective-permute-done.12 = bf16[512,128]{1,0:T(8,128)(2,1)S(1)} collective-permute-done((bf16[512,128]{1,0:T(8,128)(2,1)S(1)}, bf16[512,128]{1,0:T(8,128)(2,1)S(1)}, u32[]{:S(2)}, u32[]{:S(2)}) %collective-permute-start.12) | collective-permute-done | bytes 131104 | tf_op jit(solution)/shard_map/ppermute | solution.py:208
  138.5 1.9 %collective-permute-start.14 = (bf16[512,128]{1,0:T(8,128)(2,1)S(1)}, bf16[512,128]{1,0:T(8,128)(2,1)S(1)}, u32[]{:S(2)}, u32[]{:S(2)}) collective-permute-start(bf16[512,128]{1,0:T(8,128)(2,1)S(1)} %collective-permute-done.12), channel_id=1, source_target_pairs={{0,2},{1,3},{2,4},{3,5},{4,6},{5,7},{6,8},{7,9},{8,10},{9,11},{10,... | collective-permute-start | bytes 393224 | tf_op jit(solution)/shard_map/ppermute | solution.py:208
  140.5 5.2 %collective-permute-done.14 = bf16[512,128]{1,0:T(8,128)(2,1)S(1)} collective-permute-done((bf16[512,128]{1,0:T(8,128)(2,1)S(1)}, bf16[512,128]{1,0:T(8,128)(2,1)S(1)}, u32[]{:S(2)}, u32[]{:S(2)}) %collective-permute-start.14) | collective-permute-done | bytes 131104 | tf_op jit(solution)/shard_map/ppermute | solution.py:208
  145.7 6.3 %collective-permute-start.15 = (bf16[8,512,128]{2,1,0:T(8,128)(2,1)S(1)}, bf16[8,512,128]{2,1,0:T(8,128)(2,1)S(1)}, u32[]{:S(2)}, u32[]{:S(2)}) collective-permute-start(bf16[8,512,128]{2,1,0:T(8,128)(2,1)S(1)} %bitcast_dynamic-update-slice_fusion.own_ref), channel_id=1, source_target_pairs={{0,1},{1,0},{2,3},{3,2},{4,5},{5,4},{6,7},{7,6},{8,9},{9,8},{10,11... | collective-permute-start | bytes 3145736 | tf_op jit(solution)/shard_map/ppermute | solution.py:287
  152.0 0.1 convert_reduce_fusion
  152.1 2.4 %shard_map.110 = (f32[3,64,512]{2,1,0:T(8,128)}, f32[3,64,128]{2,1,0:T(8,128)}) custom-call(s32[32]{0:T(128)S(1)} %select_reduce_fusion.1.pick_ref, f32[3]{0:T(128)S(1)} %maximum_divide_fusion.scale_ref, bf16[1024,128]{1,0:T(8,128)(2,1)S(1)} %bitcast.25, bf16[32,32,640]{2,1,0:T(8,128)(2,1)S(1)} %all-to-all-done.rows_ref), custom_call_target="tpu_custom_call" | custom-call | flops 251658240 | bytes 1310720 | tf_op jit(solution)/shard_map/pallas_call | solution.py:289
  154.5 1.8 %shard_map.108.base_ref = f32[512,512]{1,0:T(8,128)S(1)} custom-call(s32[4]{0:T(128)S(1)} %pad_add_fusion.place_ref, bf16[8,512,128]{2,1,0:T(8,128)(2,1)S(1)} %bitcast_dynamic-update-slice_fusion.own_ref, bf16[8,512,128]{2,1,0:T(8,128)(2,1)S(1)} %collective-permute-done.15.other_ref, bf16[512,2048]{1,0:T(8,128)(2,1)S(1)} %copy-done.4), custom_call_target="tpu_custom_call" | custom-call | flops 1073741824 | bytes 4194304 | tf_op jit(solution)/shard_map/pallas_call | solution.py:297
  156.4 1.0 copy-done.1
  157.4 1.2 copy-done.2
  158.6 1.7 %shard_map.109 = (bf16[512,512]{1,0:T(8,128)(2,1)}, bf16[512,128]{1,0:T(8,128)(2,1)}) custom-call(s32[4]{0:T(128)S(1)} %pad_add_fusion.place_ref, s32[512]{0:T(512)S(1)} %copy-done.20, s32[96]{0:T(128)S(1)} %copy-done.22, f32[512,512]{1,0:T(8,128)S(1)} %copy-done.2, bf16[32,32,640]{2,1,0:T(8,128)(2,1)S(1)} %all-to-all-done.3.came_ref, ...), custom_call_target="tpu_custom_call" | custom-call | bytes 2883584 | tf_op jit(solution)/shard_map/pallas_call | solution.py:304
  (47 shorter events, 0.3 us)
Async XLA Ops:
  0.7 0.9 copy-start.6
  1.6 1.0 copy-start.8
  2.7 0.7 copy-start.19
  3.3 0.7 copy-start.21
  5.8 13.9 %copy-start.3 = (bf16[512,2048]{1,0:T(8,128)(2,1)S(1)}, bf16[512,2048]{1,0:T(8,128)(2,1)}, u32[]{:S(2)}) copy-start(bf16[512,2048]{1,0:T(8,128)(2,1)} %weight_ref.3) | copy-start | bytes 6291460
  5.8 65.1 %all-to-all-start = ((bf16[32,32,640]{2,1,0:T(8,128)(2,1)}), bf16[32,32,640]{2,1,0:T(8,128)(2,1)S(1)}, u32[]{:S(2)}, u32[]{:S(2)}) async-start(bf16[32,32,640]{2,1,0:T(8,128)(2,1)} %shard_map.102), calls=%async_computation | async-start | bytes 2621440 | tf_op jit(solution)/shard_map/all_to_all | solution.py:175
  19.7 1.0 copy-start.9
  24.9 13.0 %copy-start.20 = (s32[512]{0:T(512)S(1)}, s32[512]{0:T(512)}, u32[]{:S(2)}) copy-start(s32[512]{0:T(512)} %index_ref.3) | copy-start | bytes 6148
  24.9 13.0 %copy-start.22 = (s32[96]{0:T(128)S(1)}, s32[96]{0:T(128)}, u32[]{:S(2)}) copy-start(s32[96]{0:T(128)} %storage_ref.3) | copy-start | bytes 1156
  24.9 46.0 %copy-start.5 = (bf16[3,64,512]{2,1,0:T(8,128)(2,1)S(1)}, bf16[3,64,512]{2,1,0:T(8,128)(2,1)}, u32[]{:S(2)}) copy-start(bf16[3,64,512]{2,1,0:T(8,128)(2,1)} %down_ref.3) | copy-start | bytes 589828
  24.9 46.0 %copy-start.10 = (bf16[3,64,128]{2,1,0:T(8,128)(2,1)S(1)}, bf16[3,64,128]{2,1,0:T(8,128)(2,1)}, u32[]{:S(2)}) copy-start(bf16[3,64,128]{2,1,0:T(8,128)(2,1)} %up_ref.3) | copy-start | bytes 147460
  24.9 5.3 %collective-permute-start = (bf16[8,512,128]{2,1,0:T(8,128)(2,1)S(1)}, bf16[8,512,128]{2,1,0:T(8,128)(2,1)S(1)}, u32[]{:S(2)}, u32[]{:S(2)}) collective-permute-start(bf16[8,512,128]{2,1,0:T(8,128)(2,1)S(1)} %get-tuple-element.31), channel_id=1, source_target_pairs={{0,1},{1,0},{2,3},{3,2},{4,5},{5,4},{6,7},{7,6},{8,9},{9,8},{10,11... | collective-permute-start | bytes 3145736 | tf_op jit(solution)/shard_map/ppermute | solution.py:235
  30.4 20.6 %collective-permute-start.1 = (bf16[512,128]{1,0:T(8,128)(2,1)S(1)}, bf16[512,128]{1,0:T(8,128)(2,1)S(1)}, u32[]{:S(2)}, u32[]{:S(2)}) collective-permute-start(bf16[512,128]{1,0:T(8,128)(2,1)S(1)} %get-tuple-element.33), channel_id=1, source_target_pairs={{0,2},{1,3},{2,4},{3,5},{4,6},{5,7},{6,8},{7,9},{8,10},{9,11},{10,... | collective-permute-start | bytes 393224 | tf_op jit(solution)/shard_map/ppermute | solution.py:208
  33.6 22.4 %collective-permute-start.2 = (bf16[512,128]{1,0:T(8,128)(2,1)S(1)}, bf16[512,128]{1,0:T(8,128)(2,1)S(1)}, u32[]{:S(2)}, u32[]{:S(2)}) collective-permute-start(bf16[512,128]{1,0:T(8,128)(2,1)S(1)} %get-tuple-element.34), channel_id=1, source_target_pairs={{0,4},{1,5},{2,6},{3,7},{4,8},{5,9},{6,10},{7,11},{8,12},{9,13},{1... | collective-permute-start | bytes 393224 | tf_op jit(solution)/shard_map/ppermute | solution.py:208
  38.0 21.3 %collective-permute-start.3 = (bf16[512,128]{1,0:T(8,128)(2,1)S(1)}, bf16[512,128]{1,0:T(8,128)(2,1)S(1)}, u32[]{:S(2)}, u32[]{:S(2)}) collective-permute-start(bf16[512,128]{1,0:T(8,128)(2,1)S(1)} %get-tuple-element.35), channel_id=1, source_target_pairs={{0,6},{1,7},{2,8},{3,9},{4,10},{5,11},{6,12},{7,13},{8,14},{9,15},... | collective-permute-start | bytes 393224 | tf_op jit(solution)/shard_map/ppermute | solution.py:208
  42.6 16.6 %collective-permute-start.4 = (bf16[512,128]{1,0:T(8,128)(2,1)S(1)}, bf16[512,128]{1,0:T(8,128)(2,1)S(1)}, u32[]{:S(2)}, u32[]{:S(2)}) collective-permute-start(bf16[512,128]{1,0:T(8,128)(2,1)S(1)} %get-tuple-element.36), channel_id=1, source_target_pairs={{0,8},{1,9},{2,10},{3,11},{4,12},{5,13},{6,14},{7,15},{8,0},{9,1},... | collective-permute-start | bytes 393224 | tf_op jit(solution)/shard_map/ppermute | solution.py:208
  46.2 16.1 %collective-permute-start.5 = (bf16[512,128]{1,0:T(8,128)(2,1)S(1)}, bf16[512,128]{1,0:T(8,128)(2,1)S(1)}, u32[]{:S(2)}, u32[]{:S(2)}) collective-permute-start(bf16[512,128]{1,0:T(8,128)(2,1)S(1)} %get-tuple-element.37), channel_id=1, source_target_pairs={{0,10},{1,11},{2,12},{3,13},{4,14},{5,15},{6,0},{7,1},{8,2},{9,3},... | collective-permute-start | bytes 393224 | tf_op jit(solution)/shard_map/ppermute | solution.py:208
  51.1 18.9 %collective-permute-start.6 = (bf16[512,128]{1,0:T(8,128)(2,1)S(1)}, bf16[512,128]{1,0:T(8,128)(2,1)S(1)}, u32[]{:S(2)}, u32[]{:S(2)}) collective-permute-start(bf16[512,128]{1,0:T(8,128)(2,1)S(1)} %get-tuple-element.38), channel_id=1, source_target_pairs={{0,12},{1,13},{2,14},{3,15},{4,0},{5,1},{6,2},{7,3},{8,4},{9,5},{1... | collective-permute-start | bytes 393224 | tf_op jit(solution)/shard_map/ppermute | solution.py:208
  56.1 14.8 %collective-permute-start.7 = (bf16[512,128]{1,0:T(8,128)(2,1)S(1)}, bf16[512,128]{1,0:T(8,128)(2,1)S(1)}, u32[]{:S(2)}, u32[]{:S(2)}) collective-permute-start(bf16[512,128]{1,0:T(8,128)(2,1)S(1)} %get-tuple-element.39), channel_id=1, source_target_pairs={{0,14},{1,15},{2,0},{3,1},{4,2},{5,3},{6,4},{7,5},{8,6},{9,7},{10,... | collective-permute-start | bytes 393224 | tf_op jit(solution)/shard_map/ppermute | solution.py:208
  59.3 16.2 %copy-start.11 = (bf16[512,128]{1,0:T(8,128)(2,1)}, bf16[512,128]{1,0:T(8,128)(2,1)S(1)}, u32[]{:S(2)}) copy-start(bf16[512,128]{1,0:T(8,128)(2,1)S(1)} %collective-permute-done.4.refs_4_) | copy-start | bytes 393220
  62.3 13.2 %copy-start.13 = (bf16[512,128]{1,0:T(8,128)(2,1)}, bf16[512,128]{1,0:T(8,128)(2,1)S(1)}, u32[]{:S(2)}) copy-start(bf16[512,128]{1,0:T(8,128)(2,1)S(1)} %collective-permute-done.5.refs_5_) | copy-start | bytes 393220
  70.0 5.5 %copy-start.15 = (bf16[512,128]{1,0:T(8,128)(2,1)}, bf16[512,128]{1,0:T(8,128)(2,1)S(1)}, u32[]{:S(2)}) copy-start(bf16[512,128]{1,0:T(8,128)(2,1)S(1)} %collective-permute-done.6.refs_6_) | copy-start | bytes 393220
  70.9 4.6 %copy-start.17 = (bf16[512,128]{1,0:T(8,128)(2,1)}, bf16[512,128]{1,0:T(8,128)(2,1)S(1)}, u32[]{:S(2)}) copy-start(bf16[512,128]{1,0:T(8,128)(2,1)S(1)} %collective-permute-done.7.refs_7_) | copy-start | bytes 393220
  103.8 1.1 copy-start
  104.9 9.6 %copy-start.7 = (bf16[512,128]{1,0:T(8,128)(2,1)S(1)}, bf16[512,128]{1,0:T(8,128)(2,1)}, u32[]{:S(2)}) copy-start(bf16[512,128]{1,0:T(8,128)(2,1)} %cot_ref.1) | copy-start | bytes 393220
  104.9 52.5 %all-to-all-start.3 = ((bf16[32,32,640]{2,1,0:T(8,128)(2,1)}), bf16[32,32,640]{2,1,0:T(8,128)(2,1)S(1)}, u32[]{:S(2)}, u32[]{:S(2)}) async-start(bf16[32,32,640]{2,1,0:T(8,128)(2,1)} %copy-done), calls=%async_computation.3 | async-start | bytes 2621440 | tf_op jit(solution)/shard_map/all_to_all | solution.py:175
  114.5 6.3 %collective-permute-start.9 = (bf16[512,128]{1,0:T(8,128)(2,1)S(1)}, bf16[512,128]{1,0:T(8,128)(2,1)S(1)}, u32[]{:S(2)}, u32[]{:S(2)}) collective-permute-start(bf16[512,128]{1,0:T(8,128)(2,1)S(1)} %copy-done.7), channel_id=1, source_target_pairs={{0,14},{1,15},{2,0},{3,1},{4,2},{5,3},{6,4},{7,5},{8,6},{9,7},{10,... | collective-permute-start | bytes 393224 | tf_op jit(solution)/shard_map/ppermute | solution.py:208
  116.6 7.5 %collective-permute-start.8 = (bf16[512,128]{1,0:T(8,128)(2,1)S(1)}, bf16[512,128]{1,0:T(8,128)(2,1)S(1)}, u32[]{:S(2)}, u32[]{:S(2)}) collective-permute-start(bf16[512,128]{1,0:T(8,128)(2,1)S(1)} %copy-done.7), channel_id=1, source_target_pairs={{0,2},{1,3},{2,4},{3,5},{4,6},{5,7},{6,8},{7,9},{8,10},{9,11},{10,... | collective-permute-start | bytes 393224 | tf_op jit(solution)/shard_map/ppermute | solution.py:208
  120.8 6.0 %collective-permute-start.11 = (bf16[512,128]{1,0:T(8,128)(2,1)S(1)}, bf16[512,128]{1,0:T(8,128)(2,1)S(1)}, u32[]{:S(2)}, u32[]{:S(2)}) collective-permute-start(bf16[512,128]{1,0:T(8,128)(2,1)S(1)} %collective-permute-done.9), channel_id=1, source_target_pairs={{0,14},{1,15},{2,0},{3,1},{4,2},{5,3},{6,4},{7,5},{8,6},{9,7},{10,... | collective-permute-start | bytes 393224 | tf_op jit(solution)/shard_map/ppermute | solution.py:208
  124.1 7.2 %collective-permute-start.10 = (bf16[512,128]{1,0:T(8,128)(2,1)S(1)}, bf16[512,128]{1,0:T(8,128)(2,1)S(1)}, u32[]{:S(2)}, u32[]{:S(2)}) collective-permute-start(bf16[512,128]{1,0:T(8,128)(2,1)S(1)} %collective-permute-done.8), channel_id=1, source_target_pairs={{0,2},{1,3},{2,4},{3,5},{4,6},{5,7},{6,8},{7,9},{8,10},{9,11},{10,... | collective-permute-start | bytes 393224 | tf_op jit(solution)/shard_map/ppermute | solution.py:208
  126.8 13.7 %collective-permute-start.13 = (bf16[512,128]{1,0:T(8,128)(2,1)S(1)}, bf16[512,128]{1,0:T(8,128)(2,1)S(1)}, u32[]{:S(2)}, u32[]{:S(2)}) collective-permute-start(bf16[512,128]{1,0:T(8,128)(2,1)S(1)} %collective-permute-done.11), channel_id=1, source_target_pairs={{0,14},{1,15},{2,0},{3,1},{4,2},{5,3},{6,4},{7,5},{8,6},{9,7},{10,... | collective-permute-start | bytes 393224 | tf_op jit(solution)/shard_map/ppermute | solution.py:208
  131.3 7.2 %collective-permute-start.12 = (bf16[512,128]{1,0:T(8,128)(2,1)S(1)}, bf16[512,128]{1,0:T(8,128)(2,1)S(1)}, u32[]{:S(2)}, u32[]{:S(2)}) collective-permute-start(bf16[512,128]{1,0:T(8,128)(2,1)S(1)} %collective-permute-done.10), channel_id=1, source_target_pairs={{0,2},{1,3},{2,4},{3,5},{4,6},{5,7},{6,8},{7,9},{8,10},{9,11},{10,... | collective-permute-start | bytes 393224 | tf_op jit(solution)/shard_map/ppermute | solution.py:208
  133.2 21.3 %copy-start.4 = (bf16[512,2048]{1,0:T(8,128)(2,1)S(1)}, bf16[512,2048]{1,0:T(8,128)(2,1)}, u32[]{:S(2)}) copy-start(bf16[512,2048]{1,0:T(8,128)(2,1)} %weight_ref.3) | copy-start | bytes 6291460
  138.5 7.2 %collective-permute-start.14 = (bf16[512,128]{1,0:T(8,128)(2,1)S(1)}, bf16[512,128]{1,0:T(8,128)(2,1)S(1)}, u32[]{:S(2)}, u32[]{:S(2)}) collective-permute-start(bf16[512,128]{1,0:T(8,128)(2,1)S(1)} %collective-permute-done.12), channel_id=1, source_target_pairs={{0,2},{1,3},{2,4},{3,5},{4,6},{5,7},{6,8},{7,9},{8,10},{9,11},{10,... | collective-permute-start | bytes 393224 | tf_op jit(solution)/shard_map/ppermute | solution.py:208
  145.7 8.8 %collective-permute-start.15 = (bf16[8,512,128]{2,1,0:T(8,128)(2,1)S(1)}, bf16[8,512,128]{2,1,0:T(8,128)(2,1)S(1)}, u32[]{:S(2)}, u32[]{:S(2)}) collective-permute-start(bf16[8,512,128]{2,1,0:T(8,128)(2,1)S(1)} %bitcast_dynamic-update-slice_fusion.own_ref), channel_id=1, source_target_pairs={{0,1},{1,0},{2,3},{3,2},{4,5},{5,4},{6,7},{7,6},{8,9},{9,8},{10,11... | collective-permute-start | bytes 3145736 | tf_op jit(solution)/shard_map/ppermute | solution.py:287
  154.5 2.9 %copy-start.12 = (bf16[512,128]{1,0:T(8,128)(2,1)S(1)}, bf16[512,128]{1,0:T(8,128)(2,1)}, u32[]{:S(2)}) copy-start(bf16[512,128]{1,0:T(8,128)(2,1)} %copy-done.11) | copy-start | bytes 393220
  154.5 2.9 %copy-start.14 = (bf16[512,128]{1,0:T(8,128)(2,1)S(1)}, bf16[512,128]{1,0:T(8,128)(2,1)}, u32[]{:S(2)}) copy-start(bf16[512,128]{1,0:T(8,128)(2,1)} %copy-done.13) | copy-start | bytes 393220
  154.5 2.9 %copy-start.16 = (bf16[512,128]{1,0:T(8,128)(2,1)S(1)}, bf16[512,128]{1,0:T(8,128)(2,1)}, u32[]{:S(2)}) copy-start(bf16[512,128]{1,0:T(8,128)(2,1)} %copy-done.15) | copy-start | bytes 393220
  154.5 2.9 %copy-start.18 = (bf16[512,128]{1,0:T(8,128)(2,1)S(1)}, bf16[512,128]{1,0:T(8,128)(2,1)}, u32[]{:S(2)}) copy-start(bf16[512,128]{1,0:T(8,128)(2,1)} %copy-done.17) | copy-start | bytes 393220
  156.4 1.0 copy-start.1
  157.4 1.2 copy-start.2

commit v3 on v2

--- a/solution.py
+++ b/solution.py
@@ -43,8 +43,10 @@
         out_ref[owner, :, block:] = cot_ref[at, :]
 
 
-def block_columns(place_ref, offset, blocks, width):
-    chip = lax.rem(place_ref[2] + offset, blocks)
+def chip_columns(place_ref, k, blocks, width):
+    steps = (0, 2, blocks - 2, blocks // 2)
+    chip = place_ref[2] if k < 4 else place_ref[3]
+    chip = lax.rem(chip + steps[k % 4], blocks)
     return pl.ds(pl.multiple_of(chip * width, width), width)
 
 
@@ -53,7 +55,7 @@
     core = place_ref[1]
     tokens = tokens_ref[...]
     for b in range(blocks):
-        columns = block_columns(place_ref, b, blocks, 2 * width)
+        columns = chip_columns(place_ref, b, blocks, 2 * width)
         part = jnp.dot(tokens, weight_ref[:, columns], preferred_element_type=f32).astype(bf16)
         low, high = part[:, :width], part[:, width:]
 
@@ -68,9 +70,22 @@
             send_ref[b] = low
 
 
-def pair_body(own_ref, came_ref, *out_refs):
+def pair_body(own_ref, came_ref, keep_ref, give_ref):
+    half = keep_ref.shape[0]
+    for b in range(half):
+        keep_ref[b] = (own_ref[b].astype(f32) + came_ref[b].astype(f32)).astype(bf16)
+        other = own_ref[half + b].astype(f32) + came_ref[half + b].astype(f32)
+        give_ref[b] = other.astype(bf16)
+
+
+def neighbour_body(keep_ref, came_ref, *out_refs):
     for b, out_ref in enumerate(out_refs):
-        out_ref[...] = (own_ref[b].astype(f32) + came_ref[b].astype(f32)).astype(bf16)
+        out_ref[...] = (keep_ref[b].astype(f32) + came_ref[b].astype(f32)).astype(bf16)
+
+
+def pack_body(*refs):
+    for b, ref in enumerate(refs[:-1]):
+        refs[-1][b] = ref[...]
 
 
 def rank_body(pick_ref, rows_ref, down_ref, up_ref, out_ref):
@@ -142,18 +157,19 @@
         up_out_ref[a] = up[at] * scale_ref[a]
 
 
-def base_body(offsets, place_ref, own_ref, other_ref, weight_ref, out_ref):
-    blocks, rows, width = own_ref.shape
+def base_body(place_ref, near_ref, near_other_ref, far_ref, far_other_ref, weight_ref, out_ref):
+    blocks, rows, width = near_ref.shape
     dims = (((1,), (1,)), ((), ()))
     first_core = place_ref[1] == 0
-    for b, offset in enumerate(offsets):
-        own, other = own_ref[b], other_ref[b]
+    for k in range(2 * blocks):
+        own_ref, other_ref = (near_ref, near_other_ref) if k < blocks else (far_ref, far_other_ref)
+        own, other = own_ref[k % blocks], other_ref[k % blocks]
         low = jnp.where(first_core, own, other)
         high = jnp.where(first_core, other, own)
         pair = jnp.concatenate([low, high], axis=1)
-        columns = block_columns(place_ref, offset, blocks, 2 * width)
+        columns = chip_columns(place_ref, k, 2 * blocks, 2 * width)
         part = lax.dot_general(pair, weight_ref[:, columns], dims, preferred_element_type=f32)
-        out_ref[...] = part if b == 0 else out_ref[...] + part
+        out_ref[...] = part if k == 0 else out_ref[...] + part
 
 
 def final_body(held, place_ref, index_ref, storage_ref, base_ref, came_ref, *refs):
@@ -196,7 +212,7 @@
     width = block + out_block
     core = here & 1
     chip = here >> 1
-    place = jnp.stack([me * seqs, core, chip, me]).astype(jnp.int32)
+    place = jnp.stack([me * seqs, core, chip, chip ^ 1]).astype(jnp.int32)
     pairs = [[t, t + 1] for t in range(0, tensor_count, 2)]
     same_core = [list(range(c, tensor_count, 2)) for c in range(2)]
 
@@ -224,6 +240,20 @@
     usage = jnp.sum((pick[:, None] == jnp.arange(held)[None, :]).astype(f32), axis=0)
     scale = adapter_scale / jnp.maximum(usage, 1.0)
 
+    swap = [(t, t ^ 1) for t in range(tensor_count)]
+    across = [(t, t ^ 2) for t in range(tensor_count)]
+    quarter = chips // 2
+    cot = after(cotangent, spread)
+    near = local_call(
+        pack_body,
+        shape(quarter, rows, out_block),
+        [VMEM] * quarter,
+        moved=4 * quarter * rows * out_block,
+    )(cot, moved_along(cot, -2), moved_along(cot, 2), moved_along(cot, quarter))
+    far = lax.ppermute(near, "tensor", across)
+    near_other = lax.ppermute(near, "tensor", swap)
+    far_other = lax.ppermute(far, "tensor", swap)
+
     own, send = local_call(
         projection_body,
         (shape(chips, rows, out_block), shape(chips, rows, out_block)),
@@ -231,16 +261,21 @@
         flops=2 * rows * block * tensor_count * out_block,
         moved=2 * (rows * block + 2 * block * tensor_count * out_block),
     )(after(place, spread), tokens, weight)
-    swap = [(t, t ^ 1) for t in range(tensor_count)]
     came = lax.ppermute(send, "tensor", swap)
-    paired = local_call(
+    keep, give = local_call(
         pair_body,
-        (shape(rows, out_block),) * chips,
+        (shape(quarter, rows, out_block),) * 2,
         [VMEM, VMEM],
         moved=6 * chips * rows * out_block,
     )(own, came)
-    parts = [paired[0]] + [moved_along(paired[d], d) for d in range(1, chips)]
-    arrived, parts = lax.optimization_barrier((arrived, parts))
+    base = local_call(
+        base_body,
+        shape(rows, block, dtype=f32),
+        [SMEM, VMEM, VMEM, VMEM, VMEM, VMEM],
+        flops=2 * rows * block * tensor_count * out_block,
+        moved=2 * (2 * rows * tensor_count * out_block),
+    )(place, near, near_other, far, far_other, weight)
+    arrived, base, keep, give = lax.optimization_barrier((arrived, base, keep, give))
 
     half = slots * length // 2
     part = local_call(
@@ -273,18 +308,16 @@
     )(pick, ranks, down, up)
     returned = exchange(contributions, "dp")
 
-    right = left = after(cotangent, contributions)
-    pieces, offsets = [right], [0]
-    for d in range(1, chips // 2 + 1):
-        right = moved_along(right, 1)
-        pieces.append(right)
-        offsets.append(chips - d)
-        if d < chips - d:
-            left = moved_along(left, -1)
-            pieces.append(left)
-            offsets.append(d)
-    own_cot = jnp.stack(pieces)
-    other_cot = lax.ppermute(own_cot, "tensor", swap)
+    crossed = lax.ppermute(after(give, contributions), "tensor", across)
+    summed = local_call(
+        neighbour_body,
+        (shape(rows, out_block),) * quarter,
+        [VMEM, VMEM],
+        moved=6 * quarter * rows * out_block,
+    )(keep, crossed)
+    parts = [summed[0]]
+    for value, distance in zip(summed[1:], (2, -2, quarter)):
+        parts.append(moved_along(value, distance))
 
     grad_down, grad_up = local_call(
         gradient_body,
@@ -294,17 +327,10 @@
         flops=2 * slots * length * width * held * rank,
         moved=2 * slots * length * width,
     )(pick, scale, ranks, arrived)
-    base = local_call(
-        functools.partial(base_body, offsets),
-        shape(rows, block, dtype=f32),
-        [SMEM, VMEM, VMEM, VMEM],
-        flops=2 * rows * block * tensor_count * out_block,
-        moved=2 * (2 * rows * tensor_count * out_block),
-    )(place, own_cot, other_cot, weight)
     token_gradient, key_value_output = local_call(
         functools.partial(final_body, held),
         (shape(rows, block), shape(rows, out_block)),
-        [SMEM, SMEM, SMEM, VMEM, VMEM] + [VMEM] * chips,
+        [SMEM, SMEM, SMEM, VMEM, VMEM] + [VMEM] * quarter,
         moved=2 * (3 * rows * block + slots * length * width),
     )(place, sequence_index, storage_row, base, returned, *parts)
     return (key_value_output, token_gradient, grad_down, grad_up)

time: 161 us -> 154 us (0.957)
  starting transfers between devices: 80 us -> 59.8 us
  waiting for transfers between devices: 26 us -> 31.2 us
  local copies, waits for them, and re-layouts: 7.88 us -> 12.4 us
  Pallas kernels: 15.3 us -> 19.5 us
    ppermute x14 -> x6, starting transfers between devices: 47.3 us -> 23.2 us  [moved_along(): return lax.ppermute(value, 'tensor', perm)]
    ppermute x1 -> x4, waiting for transfers between devices: 0.01 us -> 23.9 us  [the longest x1 12.6 us: on_device(): crossed = lax.ppermute(after(give, contributions), 'tensor', across)]
    ppermute x14 -> x6, waiting for transfers between devices: 23.7 us -> 7.33 us  [moved_along(): return lax.ppermute(value, 'tensor', perm)]
    unnamed x53 -> x40, local copies, waits for them, and re-layouts: 7.78 us -> 12.4 us
    pallas_call x2 -> x4, Pallas kernels: 2.08 us -> 5.35 us  [the longest x1 2.84 us: on_device(): local_call(base_body, shape(rows, block, dtype=f32), [SMEM, VMEM, VMEM, V...]
    ppermute x1 -> x4, starting transfers between devices: 6.26 us -> 9.38 us  [the longest x1 2.69 us: on_device(): far_other = lax.ppermute(far, 'tensor', swap)]
    ppermute x1, waiting for transfers between devices: 2.26 us -> 0.01 us  [on_device(): came = lax.ppermute(send, 'tensor', swap)]
  transfers between devices with their start and end apart: 18 -> 13, of which waited for: 8 -> 4; matrix products, arithmetic and copies ran while one was open for 0% -> 0% of each run, Pallas kernels for 5% -> 8%
where the time goes in v3:
time: 154 us; the launch traced here: 153 us
  starting transfers between devices  59.8 us (39%)
  waiting for transfers between devices  31.2 us (20%)
  blocking collectives  28.3 us (18%)
  Pallas kernels  19.5 us (13%)
  local copies, waits for them, and re-layouts  12.4 us (8%)
    all_to_all x2, starting transfers between devices, exchange(): lax.all_to_all(value, axis, split_axis=0, concat_axis=0, axis_index_group...  23.5 us
    ppermute x6, starting transfers between devices, moved_along(): return lax.ppermute(value, 'tensor', perm)  23.2 us
    all_to_all x2, blocking collectives, exchange(): lax.all_to_all(value, axis, split_axis=0, concat_axis=0, axis_index_group...  21.6 us
    ppermute x1, waiting for transfers between devices, on_device(): crossed = lax.ppermute(after(give, contributions), 'tensor', across)  12.6 us
    unnamed x40, local copies, waits for them, and re-layouts  12.4 us
    ppermute x1, waiting for transfers between devices, on_device(): far = lax.ppermute(near, 'tensor', across)  11.2 us
    ppermute x6, waiting for transfers between devices, moved_along(): return lax.ppermute(value, 'tensor', perm)  7.33 us
    pallas_call x1, Pallas kernels, on_device(): local_call(projection_body, (shape(chips, rows, out_block), shape(chips,...  5.13 us
  transfers between devices with their start and end apart: 13, of which 4 were waited for; matrix products, arithmetic and copies ran while one was open for 0% of the time, Pallas kernels for 8%

profile of v3, /device:TPU:1, one launch (start us, length us, event | category | flops | bytes accessed | tf_op | source)
XLA Modules:
  0.0 152.6 jit_solution(7853787437303672977)
XLA Ops:
  0.6 0.1 pad_add_fusion.place_ref
  0.7 1.0 copy-done.10
  1.8 0.9 copy-done.12
  2.7 0.7 copy-done.15
  3.3 0.7 copy-done.17
  4.0 1.8 %shard_map.102 = bf16[32,32,640]{2,1,0:T(8,128)(2,1)} custom-call(s32[4]{0:T(128)S(1)} %pad_add_fusion.place_ref, s32[512]{0:T(512)S(1)} %copy-done.15, s32[96]{0:T(128)S(1)} %copy-done.17, bf16[512,512]{1,0:T(8,128)(2,1)S(1)} %copy-done.10, bf16[512,128]{1,0:T(8,128)(2,1)S(1)} %copy-done.12), custom_call_target="tpu_custom_call" | custom-call | bytes 1966080 | tf_op jit(solution)/shard_map/pallas_call | solution.py:226
  5.8 13.9 %all-to-all-start = ((bf16[32,32,640]{2,1,0:T(8,128)(2,1)}), bf16[32,32,640]{2,1,0:T(8,128)(2,1)S(1)}, u32[]{:S(2)}, u32[]{:S(2)}) async-start(bf16[32,32,640]{2,1,0:T(8,128)(2,1)} %shard_map.102), calls=%async_computation | async-start | bytes 2621440 | tf_op jit(solution)/shard_map/all_to_all | solution.py:191
  19.7 5.9 %collective-permute-start = (bf16[512,128]{1,0:T(8,128)(2,1)S(1)}, bf16[512,128]{1,0:T(8,128)(2,1)S(1)}, u32[]{:S(2)}, u32[]{:S(2)}) collective-permute-start(bf16[512,128]{1,0:T(8,128)(2,1)S(1)} %copy-done.13), channel_id=1, source_target_pairs={{0,12},{1,13},{2,14},{3,15},{4,0},{5,1},{6,2},{7,3},{8,4},{9,5},{1... | collective-permute-start | bytes 393224 | tf_op jit(solution)/shard_map/ppermute | solution.py:224
  25.6 1.9 %collective-permute-start.1 = (bf16[512,128]{1,0:T(8,128)(2,1)S(1)}, bf16[512,128]{1,0:T(8,128)(2,1)S(1)}, u32[]{:S(2)}, u32[]{:S(2)}) collective-permute-start(bf16[512,128]{1,0:T(8,128)(2,1)S(1)} %copy-done.13), channel_id=1, source_target_pairs={{0,4},{1,5},{2,6},{3,7},{4,8},{5,9},{6,10},{7,11},{8,12},{9,13},{1... | collective-permute-start | bytes 393224 | tf_op jit(solution)/shard_map/ppermute | solution.py:224
  27.5 5.8 %collective-permute-start.2 = (bf16[512,128]{1,0:T(8,128)(2,1)S(1)}, bf16[512,128]{1,0:T(8,128)(2,1)S(1)}, u32[]{:S(2)}, u32[]{:S(2)}) collective-permute-start(bf16[512,128]{1,0:T(8,128)(2,1)S(1)} %copy-done.13), channel_id=1, source_target_pairs={{0,8},{1,9},{2,10},{3,11},{4,12},{5,13},{6,14},{7,15},{8,0},{9,1},... | collective-permute-start | bytes 393224 | tf_op jit(solution)/shard_map/ppermute | solution.py:224
  33.4 0.0 copy-start.11
  33.4 1.0 copy-done.11
  34.4 5.1 %shard_map.105 = (bf16[8,512,128]{2,1,0:T(8,128)(2,1)S(1)}, bf16[8,512,128]{2,1,0:T(8,128)(2,1)}) custom-call(s32[4]{0:T(128)S(1)} %pad_add_fusion.place_ref, bf16[512,512]{1,0:T(8,128)(2,1)S(1)} %copy-done.11, bf16[512,2048]{1,0:T(8,128)(2,1)S(1)} %copy-done.3), custom_call_target="tpu_custom_call" | custom-call | flops 1073741824 | bytes 4718592 | tf_op jit(solution)/shard_map/pallas_call | solution.py:257
  39.6 1.0 copy-done.4
  40.5 3.7 %collective-permute-start.6 = (bf16[8,512,128]{2,1,0:T(8,128)(2,1)}, bf16[8,512,128]{2,1,0:T(8,128)(2,1)}, u32[]{:S(2)}, u32[]{:S(2)}) collective-permute-start(bf16[8,512,128]{2,1,0:T(8,128)(2,1)} %get-tuple-element.26), channel_id=1, source_target_pairs={{0,1},{1,0},{2,3},{3,2},{4,5},{5,4},{6,7},{7,6},{8,9},{9,8},{10,11... | collective-permute-start | bytes 3145736 | tf_op jit(solution)/shard_map/ppermute | solution.py:264
  44.2 0.0 collective-permute-done.refs_1_
  44.2 0.0 collective-permute-done.1.refs_2_
  44.3 0.0 collective-permute-done.2.refs_3_
  44.3 0.8 shard_map.103.near_ref
  45.1 2.3 %collective-permute-start.4 = (bf16[4,512,128]{2,1,0:T(8,128)(2,1)}, bf16[4,512,128]{2,1,0:T(8,128)(2,1)}, u32[]{:S(2)}, u32[]{:S(2)}) collective-permute-start(bf16[4,512,128]{2,1,0:T(8,128)(2,1)} %shard_map.103.near_ref), channel_id=1, source_target_pairs={{0,2},{1,3},{2,0},{3,1},{4,6},{5,7},{6,4},{7,5},{8,10},{9,11},{10,... | collective-permute-start | bytes 1572872 | tf_op jit(solution)/shard_map/ppermute | solution.py:253
  47.4 2.2 %collective-permute-start.3 = (bf16[4,512,128]{2,1,0:T(8,128)(2,1)}, bf16[4,512,128]{2,1,0:T(8,128)(2,1)}, u32[]{:S(2)}, u32[]{:S(2)}) collective-permute-start(bf16[4,512,128]{2,1,0:T(8,128)(2,1)} %shard_map.103.near_ref), channel_id=1, source_target_pairs={{0,1},{1,0},{2,3},{3,2},{4,5},{5,4},{6,7},{7,6},{8,9},{9,8},{10,11... | collective-permute-start | bytes 1572872 | tf_op jit(solution)/shard_map/ppermute | solution.py:254
  49.6 11.2 %collective-permute-done.4.far_ref = bf16[4,512,128]{2,1,0:T(8,128)(2,1)} collective-permute-done((bf16[4,512,128]{2,1,0:T(8,128)(2,1)}, bf16[4,512,128]{2,1,0:T(8,128)(2,1)}, u32[]{:S(2)}, u32[]{:S(2)}) %collective-permute-start.4) | collective-permute-done | bytes 524320 | tf_op jit(solution)/shard_map/ppermute | solution.py:253
  60.8 2.7 %collective-permute-start.5 = (bf16[4,512,128]{2,1,0:T(8,128)(2,1)}, bf16[4,512,128]{2,1,0:T(8,128)(2,1)}, u32[]{:S(2)}, u32[]{:S(2)}) collective-permute-start(bf16[4,512,128]{2,1,0:T(8,128)(2,1)} %collective-permute-done.4.far_ref), channel_id=1, source_target_pairs={{0,1},{1,0},{2,3},{3,2},{4,5},{5,4},{6,7},{7,6},{8,9},{9,8},{10,11... | collective-permute-start | bytes 1572872 | tf_op jit(solution)/shard_map/ppermute | solution.py:255
  63.5 0.0 copy-done.16
  63.6 0.0 copy-done.18
  63.6 0.1 select_reduce_fusion
  63.7 0.1 sub.12
  63.8 0.1 select_reduce_fusion.1.pick_ref
  63.9 0.0 collective-permute-done.6.came_ref
  63.9 1.2 copy-done.5
  65.1 1.6 %shard_map.106 = (bf16[4,512,128]{2,1,0:T(8,128)(2,1)S(1)}, bf16[4,512,128]{2,1,0:T(8,128)(2,1)S(1)}) custom-call(bf16[8,512,128]{2,1,0:T(8,128)(2,1)S(1)} %copy-done.5, bf16[8,512,128]{2,1,0:T(8,128)(2,1)} %collective-permute-done.6.came_ref), custom_call_target="tpu_custom_call" | custom-call | bytes 3145728 | tf_op jit(solution)/shard_map/pallas_call | solution.py:265
  66.7 0.0 copy-start.8
  66.7 0.8 copy-done.8
  67.5 0.8 copy-done.19
  68.3 0.0 collective-permute-done.3.near_other_ref
  68.3 0.0 collective-permute-done.5.far_other_ref
  68.3 2.8 %shard_map.104.base_ref = f32[512,512]{1,0:T(8,128)S(1)} custom-call(s32[4]{0:T(128)S(1)} %pad_add_fusion.place_ref, bf16[4,512,128]{2,1,0:T(8,128)(2,1)} %shard_map.103.near_ref, bf16[4,512,128]{2,1,0:T(8,128)(2,1)} %collective-permute-done.3.near_other_ref, bf16[4,512,128]{2,1,0:T(8,128)(2,1)} %collective-permute-done.4.far_ref, ...), custom_call_target="tpu_custom_call" | custom-call | flops 1073741824 | bytes 4194304 | tf_op jit(solution)/shard_map/pallas_call | solution.py:271
  71.2 1.0 copy-done.1
  72.1 0.0 all-to-all-done.rows_ref
  72.2 0.9 copy-done.6
  73.1 1.8 %shard_map.107 = bf16[1024,128]{1,0:T(8,128)(2,1)S(1)} custom-call(s32[32]{0:T(128)S(1)} %select_reduce_fusion.1.pick_ref, bf16[32,32,640]{2,1,0:T(8,128)(2,1)S(1)} %all-to-all-done.rows_ref, bf16[3,64,512]{2,1,0:T(8,128)(2,1)S(1)} %copy-done.6, bf16[3,64,128]{2,1,0:T(8,128)(2,1)S(1)} %copy-done.14), custom_call_target="tpu_custom_call" | custom-call | flops 251658240 | bytes 1310720 | tf_op jit(solution)/shard_map/pallas_call | solution.py:281
  74.9 0.0 copy-start.7
  74.9 2.3 %all-gather = bf16[2048,128]{1,0:T(8,128)(2,1)S(1)} all-gather(bf16[1024,128]{1,0:T(8,128)(2,1)S(1)} %shard_map.107), channel_id=2, replica_groups={{0,1},{2,3},{4,5},{6,7},{8,9},{10,11},{12,13},{14,15},{16,17},{18,19},{..., dimensions={0}, use_global_device_ids=true | all-gather | bytes 786432 | tf_op jit(solution)/shard_map/all_gather | solution.py:288
  77.2 11.3 %all_to_all.20.parts_ref = bf16[8,64,128]{2,1,0:T(8,128)(2,1)S(1)} all-to-all(bf16[8,64,128]{2,1,0:T(8,128)(2,1)S(1)} %bitcast.12), channel_id=1, replica_groups={{0,2,4,6,8,10,12,14},{1,3,5,7,9,11,13,15},{16,18,20,22,24,26,28,30},{17..., dimensions={0} | all-to-all | bytes 262144 | tf_op jit(solution)/shard_map/all_to_all | solution.py:191
  88.5 10.3 %all_to_all.21 = bf16[8,64,128]{2,1,0:T(8,128)(2,1)S(1)} all-to-all(bf16[8,64,128]{2,1,0:T(8,128)(2,1)S(1)} %shard_map.108), channel_id=1, replica_groups={{0,2,4,6,8,10,12,14},{1,3,5,7,9,11,13,15},{16,18,20,22,24,26,28,30},{17..., dimensions={0} | all-to-all | bytes 262144 | tf_op jit(solution)/shard_map/all_to_all | solution.py:191
  98.9 4.4 %all_gather.11 = bf16[2,512,128]{2,1,0:T(8,128)(2,1)S(1)} all-gather(bf16[1,512,128]{2,1,0:T(8,128)(2,1)S(1)} %bitcast.11), channel_id=1, replica_groups={{0,1},{2,3},{4,5},{6,7},{8,9},{10,11},{12,13},{14,15},{16,17},{18,19},{..., dimensions={0}, use_global_device_ids=true | all-gather | bytes 393216 | tf_op jit(solution)/shard_map/all_gather | solution.py:298
  103.3 1.4 shard_map.109
  104.7 1.1 copy-done
  105.8 9.6 %all-to-all-start.3 = ((bf16[32,32,640]{2,1,0:T(8,128)(2,1)}), bf16[32,32,640]{2,1,0:T(8,128)(2,1)S(1)}, u32[]{:S(2)}, u32[]{:S(2)}) async-start(bf16[32,32,640]{2,1,0:T(8,128)(2,1)} %copy-done), calls=%async_computation.3 | async-start | bytes 2621440 | tf_op jit(solution)/shard_map/all_to_all | solution.py:191
  115.4 2.2 %collective-permute-start.7 = (bf16[4,512,128]{2,1,0:T(8,128)(2,1)}, bf16[4,512,128]{2,1,0:T(8,128)(2,1)S(1)}, u32[]{:S(2)}, u32[]{:S(2)}) collective-permute-start(bf16[4,512,128]{2,1,0:T(8,128)(2,1)} %copy-done.19), channel_id=1, source_target_pairs={{0,2},{1,3},{2,0},{3,1},{4,6},{5,7},{6,4},{7,5},{8,10},{9,11},{10,... | collective-permute-start | bytes 1572872 | tf_op jit(solution)/shard_map/ppermute | solution.py:311
  117.6 0.1 convert_reduce_fusion
  117.7 12.6 %collective-permute-done.7.came_ref = bf16[4,512,128]{2,1,0:T(8,128)(2,1)S(1)} collective-permute-done((bf16[4,512,128]{2,1,0:T(8,128)(2,1)}, bf16[4,512,128]{2,1,0:T(8,128)(2,1)S(1)}, u32[]{:S(2)}, u32[]{:S(2)}) %collective-permute-start.7) | collective-permute-done | bytes 524320 | tf_op jit(solution)/shard_map/ppermute | solution.py:311
  130.3 0.0 copy-done.9
  130.3 0.1 shard_map.110
  130.5 2.2 %collective-permute-start.10 = (bf16[512,128]{1,0:T(8,128)(2,1)S(1)}, bf16[512,128]{1,0:T(8,128)(2,1)S(1)}, u32[]{:S(2)}, u32[]{:S(2)}) collective-permute-start(bf16[512,128]{1,0:T(8,128)(2,1)S(1)} %get-tuple-element.37), channel_id=1, source_target_pairs={{0,8},{1,9},{2,10},{3,11},{4,12},{5,13},{6,14},{7,15},{8,0},{9,1},... | collective-permute-start | bytes 393224 | tf_op jit(solution)/shard_map/ppermute | solution.py:224
  132.6 3.8 %collective-permute-start.8 = (bf16[512,128]{1,0:T(8,128)(2,1)S(1)}, bf16[512,128]{1,0:T(8,128)(2,1)S(1)}, u32[]{:S(2)}, u32[]{:S(2)}) collective-permute-start(bf16[512,128]{1,0:T(8,128)(2,1)S(1)} %get-tuple-element.35), channel_id=1, source_target_pairs={{0,4},{1,5},{2,6},{3,7},{4,8},{5,9},{6,10},{7,11},{8,12},{9,13},{1... | collective-permute-start | bytes 393224 | tf_op jit(solution)/shard_map/ppermute | solution.py:224
  136.5 3.6 %collective-permute-start.9 = (bf16[512,128]{1,0:T(8,128)(2,1)S(1)}, bf16[512,128]{1,0:T(8,128)(2,1)S(1)}, u32[]{:S(2)}, u32[]{:S(2)}) collective-permute-start(bf16[512,128]{1,0:T(8,128)(2,1)S(1)} %get-tuple-element.36), channel_id=1, source_target_pairs={{0,12},{1,13},{2,14},{3,15},{4,0},{5,1},{6,2},{7,3},{8,4},{9,5},{1... | collective-permute-start | bytes 393224 | tf_op jit(solution)/shard_map/ppermute | solution.py:224
  140.1 2.4 %shard_map.112 = (f32[3,64,512]{2,1,0:T(8,128)}, f32[3,64,128]{2,1,0:T(8,128)}) custom-call(s32[32]{0:T(128)S(1)} %select_reduce_fusion.1.pick_ref, f32[3]{0:T(128)S(1)} %maximum_divide_fusion.scale_ref, bf16[1024,128]{1,0:T(8,128)(2,1)S(1)} %bitcast.9, bf16[32,32,640]{2,1,0:T(8,128)(2,1)S(1)} %all-to-all-done.rows_ref), custom_call_target="tpu_custom_call" | custom-call | flops 251658240 | bytes 1310720 | tf_op jit(solution)/shard_map/pallas_call | solution.py:322
  142.4 0.0 collective-permute-done.10.refs_3_
  142.4 1.6 %collective-permute-done.8.refs_1_ = bf16[512,128]{1,0:T(8,128)(2,1)S(1)} collective-permute-done((bf16[512,128]{1,0:T(8,128)(2,1)S(1)}, bf16[512,128]{1,0:T(8,128)(2,1)S(1)}, u32[]{:S(2)}, u32[]{:S(2)}) %collective-permute-start.8) | collective-permute-done | bytes 131104 | tf_op jit(solution)/shard_map/ppermute | solution.py:224
  144.1 5.7 %collective-permute-done.9.refs_2_ = bf16[512,128]{1,0:T(8,128)(2,1)S(1)} collective-permute-done((bf16[512,128]{1,0:T(8,128)(2,1)S(1)}, bf16[512,128]{1,0:T(8,128)(2,1)S(1)}, u32[]{:S(2)}, u32[]{:S(2)}) %collective-permute-start.9) | collective-permute-done | bytes 131104 | tf_op jit(solution)/shard_map/ppermute | solution.py:224
  149.8 0.0 all-to-all-done.3.came_ref
  149.8 1.2 copy-done.2
  151.0 1.6 %shard_map.111 = (bf16[512,512]{1,0:T(8,128)(2,1)}, bf16[512,128]{1,0:T(8,128)(2,1)}) custom-call(s32[4]{0:T(128)S(1)} %pad_add_fusion.place_ref, s32[512]{0:T(512)S(1)} %copy-done.16, s32[96]{0:T(128)S(1)} %copy-done.18, f32[512,512]{1,0:T(8,128)S(1)} %copy-done.2, bf16[32,32,640]{2,1,0:T(8,128)(2,1)S(1)} %all-to-all-done.3.came_ref, ...), custom_call_target="tpu_custom_call" | custom-call | bytes 2883584 | tf_op jit(solution)/shard_map/pallas_call | solution.py:330
  (25 shorter events, 0.1 us)
Async XLA Ops:
  0.7 1.0 copy-start.10
  1.8 0.9 copy-start.12
  2.7 0.7 copy-start.15
  3.3 0.7 copy-start.17
  5.8 13.9 %copy-start.13 = (bf16[512,128]{1,0:T(8,128)(2,1)S(1)}, bf16[512,128]{1,0:T(8,128)(2,1)}, u32[]{:S(2)}) copy-start(bf16[512,128]{1,0:T(8,128)(2,1)} %refs_0_) | copy-start | bytes 393220
  5.8 27.5 %copy-start.3 = (bf16[512,2048]{1,0:T(8,128)(2,1)S(1)}, bf16[512,2048]{1,0:T(8,128)(2,1)}, u32[]{:S(2)}) copy-start(bf16[512,2048]{1,0:T(8,128)(2,1)} %weight_ref.3) | copy-start | bytes 6291460
  5.8 57.7 %copy-start.16 = (s32[512]{0:T(512)S(1)}, s32[512]{0:T(512)}, u32[]{:S(2)}) copy-start(s32[512]{0:T(512)} %index_ref.3) | copy-start | bytes 6148
  5.8 57.7 %copy-start.18 = (s32[96]{0:T(128)S(1)}, s32[96]{0:T(128)}, u32[]{:S(2)}) copy-start(s32[96]{0:T(128)} %storage_ref.3) | copy-start | bytes 1156
  5.8 66.3 %all-to-all-start = ((bf16[32,32,640]{2,1,0:T(8,128)(2,1)}), bf16[32,32,640]{2,1,0:T(8,128)(2,1)S(1)}, u32[]{:S(2)}, u32[]{:S(2)}) async-start(bf16[32,32,640]{2,1,0:T(8,128)(2,1)} %shard_map.102), calls=%async_computation | async-start | bytes 2621440 | tf_op jit(solution)/shard_map/all_to_all | solution.py:191
  19.7 24.5 %collective-permute-start = (bf16[512,128]{1,0:T(8,128)(2,1)S(1)}, bf16[512,128]{1,0:T(8,128)(2,1)S(1)}, u32[]{:S(2)}, u32[]{:S(2)}) collective-permute-start(bf16[512,128]{1,0:T(8,128)(2,1)S(1)} %copy-done.13), channel_id=1, source_target_pairs={{0,12},{1,13},{2,14},{3,15},{4,0},{5,1},{6,2},{7,3},{8,4},{9,5},{1... | collective-permute-start | bytes 393224 | tf_op jit(solution)/shard_map/ppermute | solution.py:224
  25.6 18.6 %collective-permute-start.1 = (bf16[512,128]{1,0:T(8,128)(2,1)S(1)}, bf16[512,128]{1,0:T(8,128)(2,1)S(1)}, u32[]{:S(2)}, u32[]{:S(2)}) collective-permute-start(bf16[512,128]{1,0:T(8,128)(2,1)S(1)} %copy-done.13), channel_id=1, source_target_pairs={{0,4},{1,5},{2,6},{3,7},{4,8},{5,9},{6,10},{7,11},{8,12},{9,13},{1... | collective-permute-start | bytes 393224 | tf_op jit(solution)/shard_map/ppermute | solution.py:224
  27.5 16.7 %collective-permute-start.2 = (bf16[512,128]{1,0:T(8,128)(2,1)S(1)}, bf16[512,128]{1,0:T(8,128)(2,1)S(1)}, u32[]{:S(2)}, u32[]{:S(2)}) collective-permute-start(bf16[512,128]{1,0:T(8,128)(2,1)S(1)} %copy-done.13), channel_id=1, source_target_pairs={{0,8},{1,9},{2,10},{3,11},{4,12},{5,13},{6,14},{7,15},{8,0},{9,1},... | collective-permute-start | bytes 393224 | tf_op jit(solution)/shard_map/ppermute | solution.py:224
  33.4 1.0 copy-start.11
  39.6 1.0 copy-start.4
  40.5 23.3 %collective-permute-start.6 = (bf16[8,512,128]{2,1,0:T(8,128)(2,1)}, bf16[8,512,128]{2,1,0:T(8,128)(2,1)}, u32[]{:S(2)}, u32[]{:S(2)}) collective-permute-start(bf16[8,512,128]{2,1,0:T(8,128)(2,1)} %get-tuple-element.26), channel_id=1, source_target_pairs={{0,1},{1,0},{2,3},{3,2},{4,5},{5,4},{6,7},{7,6},{8,9},{9,8},{10,11... | collective-permute-start | bytes 3145736 | tf_op jit(solution)/shard_map/ppermute | solution.py:264
  45.1 15.7 %collective-permute-start.4 = (bf16[4,512,128]{2,1,0:T(8,128)(2,1)}, bf16[4,512,128]{2,1,0:T(8,128)(2,1)}, u32[]{:S(2)}, u32[]{:S(2)}) collective-permute-start(bf16[4,512,128]{2,1,0:T(8,128)(2,1)} %shard_map.103.near_ref), channel_id=1, source_target_pairs={{0,2},{1,3},{2,0},{3,1},{4,6},{5,7},{6,4},{7,5},{8,10},{9,11},{10,... | collective-permute-start | bytes 1572872 | tf_op jit(solution)/shard_map/ppermute | solution.py:253
  47.4 20.9 %collective-permute-start.3 = (bf16[4,512,128]{2,1,0:T(8,128)(2,1)}, bf16[4,512,128]{2,1,0:T(8,128)(2,1)}, u32[]{:S(2)}, u32[]{:S(2)}) collective-permute-start(bf16[4,512,128]{2,1,0:T(8,128)(2,1)} %shard_map.103.near_ref), channel_id=1, source_target_pairs={{0,1},{1,0},{2,3},{3,2},{4,5},{5,4},{6,7},{7,6},{8,9},{9,8},{10,11... | collective-permute-start | bytes 1572872 | tf_op jit(solution)/shard_map/ppermute | solution.py:254
  60.8 7.5 %collective-permute-start.5 = (bf16[4,512,128]{2,1,0:T(8,128)(2,1)}, bf16[4,512,128]{2,1,0:T(8,128)(2,1)}, u32[]{:S(2)}, u32[]{:S(2)}) collective-permute-start(bf16[4,512,128]{2,1,0:T(8,128)(2,1)} %collective-permute-done.4.far_ref), channel_id=1, source_target_pairs={{0,1},{1,0},{2,3},{3,2},{4,5},{5,4},{6,7},{7,6},{8,9},{9,8},{10,11... | collective-permute-start | bytes 1572872 | tf_op jit(solution)/shard_map/ppermute | solution.py:255
  63.9 1.2 copy-start.5
  66.7 0.8 copy-start.8
  67.5 0.8 copy-start.19
  68.3 3.8 %copy-start.14 = (bf16[3,64,128]{2,1,0:T(8,128)(2,1)S(1)}, bf16[3,64,128]{2,1,0:T(8,128)(2,1)}, u32[]{:S(2)}) copy-start(bf16[3,64,128]{2,1,0:T(8,128)(2,1)} %up_ref.3) | copy-start | bytes 147460
  71.2 1.0 copy-start.1
  72.2 0.9 copy-start.6
  74.9 28.4 %copy-start.7 = (bf16[3,64,512]{2,1,0:T(8,128)(2,1)S(1)}, bf16[3,64,512]{2,1,0:T(8,128)(2,1)}, u32[]{:S(2)}) copy-start(bf16[3,64,512]{2,1,0:T(8,128)(2,1)} %down_ref.3) | copy-start | bytes 589828
  104.7 1.1 copy-start
  105.8 24.6 %copy-start.9 = (bf16[4,512,128]{2,1,0:T(8,128)(2,1)S(1)}, bf16[4,512,128]{2,1,0:T(8,128)(2,1)}, u32[]{:S(2)}) copy-start(bf16[4,512,128]{2,1,0:T(8,128)(2,1)} %copy-done.8) | copy-start | bytes 1572868
  105.8 44.0 %all-to-all-start.3 = ((bf16[32,32,640]{2,1,0:T(8,128)(2,1)}), bf16[32,32,640]{2,1,0:T(8,128)(2,1)S(1)}, u32[]{:S(2)}, u32[]{:S(2)}) async-start(bf16[32,32,640]{2,1,0:T(8,128)(2,1)} %copy-done), calls=%async_computation.3 | async-start | bytes 2621440 | tf_op jit(solution)/shard_map/all_to_all | solution.py:191
  115.4 14.9 %collective-permute-start.7 = (bf16[4,512,128]{2,1,0:T(8,128)(2,1)}, bf16[4,512,128]{2,1,0:T(8,128)(2,1)S(1)}, u32[]{:S(2)}, u32[]{:S(2)}) collective-permute-start(bf16[4,512,128]{2,1,0:T(8,128)(2,1)} %copy-done.19), channel_id=1, source_target_pairs={{0,2},{1,3},{2,0},{3,1},{4,6},{5,7},{6,4},{7,5},{8,10},{9,11},{10,... | collective-permute-start | bytes 1572872 | tf_op jit(solution)/shard_map/ppermute | solution.py:311
  130.5 12.0 %collective-permute-start.10 = (bf16[512,128]{1,0:T(8,128)(2,1)S(1)}, bf16[512,128]{1,0:T(8,128)(2,1)S(1)}, u32[]{:S(2)}, u32[]{:S(2)}) collective-permute-start(bf16[512,128]{1,0:T(8,128)(2,1)S(1)} %get-tuple-element.37), channel_id=1, source_target_pairs={{0,8},{1,9},{2,10},{3,11},{4,12},{5,13},{6,14},{7,15},{8,0},{9,1},... | collective-permute-start | bytes 393224 | tf_op jit(solution)/shard_map/ppermute | solution.py:224
  132.6 11.4 %collective-permute-start.8 = (bf16[512,128]{1,0:T(8,128)(2,1)S(1)}, bf16[512,128]{1,0:T(8,128)(2,1)S(1)}, u32[]{:S(2)}, u32[]{:S(2)}) collective-permute-start(bf16[512,128]{1,0:T(8,128)(2,1)S(1)} %get-tuple-element.35), channel_id=1, source_target_pairs={{0,4},{1,5},{2,6},{3,7},{4,8},{5,9},{6,10},{7,11},{8,12},{9,13},{1... | collective-permute-start | bytes 393224 | tf_op jit(solution)/shard_map/ppermute | solution.py:224
  136.5 13.3 %collective-permute-start.9 = (bf16[512,128]{1,0:T(8,128)(2,1)S(1)}, bf16[512,128]{1,0:T(8,128)(2,1)S(1)}, u32[]{:S(2)}, u32[]{:S(2)}) collective-permute-start(bf16[512,128]{1,0:T(8,128)(2,1)S(1)} %get-tuple-element.36), channel_id=1, source_target_pairs={{0,12},{1,13},{2,14},{3,15},{4,0},{5,1},{6,2},{7,3},{8,4},{9,5},{1... | collective-permute-start | bytes 393224 | tf_op jit(solution)/shard_map/ppermute | solution.py:224
  149.8 1.2 copy-start.2

commit v4 on v3

--- a/solution.py
+++ b/solution.py
@@ -12,18 +12,20 @@
 bf16 = jnp.bfloat16
 SMEM = pl.BlockSpec(memory_space=pltpu.SMEM)
 VMEM = pl.BlockSpec(memory_space=pltpu.VMEM)
-VMEM_LIMIT = 40 * 1024 * 1024
-
-
-def local_call(body, out_shape, specs, scratch=(), flops=0, moved=0):
+VMEM_LIMIT = 16 * 1024 * 1024
+HBM_LIMIT = 60 * 1024 * 1024
+ANY = pl.BlockSpec(memory_space=pl.ANY)
+
+
+def local_call(body, out_shape, specs, scratch=(), flops=0, moved=0, out=VMEM, limit=VMEM_LIMIT):
     multiple = isinstance(out_shape, (tuple, list))
     return pl.pallas_call(
         body,
         out_shape=out_shape,
         in_specs=specs,
-        out_specs=(VMEM,) * len(out_shape) if multiple else VMEM,
+        out_specs=(out,) * len(out_shape) if multiple else out,
         scratch_shapes=list(scratch),
-        compiler_params=pltpu.CompilerParams(vmem_limit_bytes=VMEM_LIMIT),
+        compiler_params=pltpu.CompilerParams(vmem_limit_bytes=limit),
         cost_estimate=pl.CostEstimate(flops=flops, bytes_accessed=moved, transcendentals=0),
     )
 
@@ -32,15 +34,53 @@
     return storage_ref[index_ref[place_ref[0] + j]] // held
 
 
-def spread_body(held, place_ref, index_ref, storage_ref, tokens_ref, cot_ref, out_ref):
-    slots, length, width = out_ref.shape
-    block = tokens_ref.shape[1]
-    out_ref[...] = jnp.zeros_like(out_ref)
-    for j in range(tokens_ref.shape[0] // length):
-        owner = owner_of(place_ref, index_ref, storage_ref, held, j)
-        at = slice(j * length, (j + 1) * length)
-        out_ref[owner, :, :block] = tokens_ref[at, :]
-        out_ref[owner, :, block:] = cot_ref[at, :]
+def spread_body(
+    held,
+    place_ref,
+    index_hbm,
+    storage_hbm,
+    tokens_hbm,
+    cot_hbm,
+    out_hbm,
+    index_ref,
+    storage_ref,
+    source_ref,
+    table_sems,
+    token_sems,
+    cot_sems,
+):
+    slots, length, width = out_hbm.shape
+    block = tokens_hbm.shape[1]
+    tables = [
+        pltpu.make_async_copy(index_hbm, index_ref, table_sems.at[0]),
+        pltpu.make_async_copy(storage_hbm, storage_ref, table_sems.at[1]),
+    ]
+    for table in tables:
+        table.start()
+    seqs = tokens_hbm.shape[0] // length
+    for s in range(slots):
+        source_ref[s] = s % seqs
+    for table in tables:
+        table.wait()
+    for j in range(seqs):
+        source_ref[owner_of(place_ref, index_ref, storage_ref, held, j)] = j
+    copies = []
+    for s in range(slots):
+        at = pl.ds(pl.multiple_of(source_ref[s] * length, length), length)
+        copies.append(
+            pltpu.make_async_copy(
+                tokens_hbm.at[at, :], out_hbm.at[s, :, pl.ds(0, block)], token_sems.at[s]
+            )
+        )
+        copies.append(
+            pltpu.make_async_copy(
+                cot_hbm.at[at, :], out_hbm.at[s, :, pl.ds(block, width - block)], cot_sems.at[s]
+            )
+        )
+        copies[-2].start()
+        copies[-1].start()
+    for copy in copies:
+        copy.wait()
 
 
 def chip_columns(place_ref, k, blocks, width):
@@ -226,8 +266,18 @@
     spread = local_call(
         functools.partial(spread_body, held),
         shape(slots, length, width),
-        [SMEM, SMEM, SMEM, VMEM, VMEM],
+        [SMEM, ANY, ANY, ANY, ANY],
+        [
+            pltpu.SMEM(sequence_index.shape, jnp.int32),
+            pltpu.SMEM(storage_row.shape, jnp.int32),
+            pltpu.SMEM((slots,), jnp.int32),
+            pltpu.SemaphoreType.DMA((2,)),
+            pltpu.SemaphoreType.DMA((slots,)),
+            pltpu.SemaphoreType.DMA((slots,)),
+        ],
         moved=3 * slots * length * width,
+        out=ANY,
+        limit=HBM_LIMIT,
     )(place, sequence_index, storage_row, tokens, cotangent)
     arrived = exchange(spread, "dp")
 
@@ -260,22 +310,11 @@
         [SMEM, VMEM, VMEM],
         flops=2 * rows * block * tensor_count * out_block,
         moved=2 * (rows * block + 2 * block * tensor_count * out_block),
-    )(after(place, spread), tokens, weight)
+    )(after(place, near), tokens, weight)
     came = lax.ppermute(send, "tensor", swap)
-    keep, give = local_call(
-        pair_body,
-        (shape(quarter, rows, out_block),) * 2,
-        [VMEM, VMEM],
-        moved=6 * chips * rows * out_block,
-    )(own, came)
-    base = local_call(
-        base_body,
-        shape(rows, block, dtype=f32),
-        [SMEM, VMEM, VMEM, VMEM, VMEM, VMEM],
-        flops=2 * rows * block * tensor_count * out_block,
-        moved=2 * (2 * rows * tensor_count * out_block),
-    )(place, near, near_other, far, far_other, weight)
-    arrived, base, keep, give = lax.optimization_barrier((arrived, base, keep, give))
+    arrived, near_other, far_other, own, came = lax.optimization_barrier(
+        (arrived, near_other, far_other, own, came)
+    )
 
     half = slots * length // 2
     part = local_call(
@@ -288,13 +327,31 @@
     both = lax.all_gather(part, "tensor", axis_index_groups=pairs)
     mine = lax.dynamic_slice_in_dim(both, core * half, half, axis=1)
     mine = mine.astype(f32).sum(0).astype(bf16).reshape(chips, half // chips, 2 * rank)
+    base = local_call(
+        base_body,
+        shape(rows, block, dtype=f32),
+        [SMEM, VMEM, VMEM, VMEM, VMEM, VMEM],
+        flops=2 * rows * block * tensor_count * out_block,
+        moved=2 * (2 * rows * tensor_count * out_block),
+    )(after(place, mine), near, near_other, far, far_other, weight)
+    pieces, base = lax.optimization_barrier((exchange(mine, "tensor", same_core), base))
     totals = local_call(
         total_body,
         shape(*mine.shape),
         [VMEM],
         moved=4 * half * 2 * rank,
-    )(exchange(mine, "tensor", same_core))
-    shared = exchange(totals, "tensor", same_core).reshape(half, 2 * rank)
+    )(pieces)
+    own, totals = lax.optimization_barrier((own, totals))
+    keep, give = local_call(
+        pair_body,
+        (shape(quarter, rows, out_block),) * 2,
+        [VMEM, VMEM],
+        moved=6 * chips * rows * out_block,
+    )(own, came)
+    shared, keep, give = lax.optimization_barrier(
+        (exchange(totals, "tensor", same_core), keep, give)
+    )
+    shared = shared.reshape(half, 2 * rank)
     ranks = lax.all_gather(shared, "tensor", axis_index_groups=pairs).reshape(part.shape)
 
     masked = pltpu.VMEM((slots * length, held * rank), bf16)
@@ -305,6 +362,7 @@
         [masked, masked],
         flops=2 * slots * length * width * held * rank,
         moved=2 * slots * length * width,
+        limit=HBM_LIMIT,
     )(pick, ranks, down, up)
     returned = exchange(contributions, "dp")
 
@@ -332,6 +390,7 @@
         (shape(rows, block), shape(rows, out_block)),
         [SMEM, SMEM, SMEM, VMEM, VMEM] + [VMEM] * quarter,
         moved=2 * (3 * rows * block + slots * length * width),
+        limit=HBM_LIMIT,
     )(place, sequence_index, storage_row, base, returned, *parts)
     return (key_value_output, token_gradient, grad_down, grad_up)
 

time: 154 us -> 187 us (1.21)
  Pallas kernels: 19.5 us -> 63.8 us
  blocking collectives: 28.3 us -> 7.12 us
  starting transfers between devices: 59.8 us -> 68 us
  local copies, waits for them, and re-layouts: 12.4 us -> 5.87 us
  waiting for transfers between devices: 31.2 us -> 36.7 us
    pallas_call x1, Pallas kernels: 1.82 us -> 42.9 us  [on_device(): local_call(functools.partial(spread_body, held), shape(slots, length, wid...]
    all_to_all x2 -> x0, blocking collectives: 21.6 us -> none  [exchange(): lax.all_to_all(value, axis, split_axis=0, concat_axis=0, axis_index_group...]
    ppermute x1, waiting for transfers between devices: 11.2 us -> 0.01 us  [on_device(): far = lax.ppermute(near, 'tensor', across)]
    all_to_all x2 -> x4, waiting for transfers between devices: 0.01 us -> 9.33 us  [exchange(): lax.all_to_all(value, axis, split_axis=0, concat_axis=0, axis_index_group...]
    all_to_all x2 -> x4, starting transfers between devices: 23.5 us -> 31.4 us  [exchange(): lax.all_to_all(value, axis, split_axis=0, concat_axis=0, axis_index_group...]
    unnamed x40 -> x36, local copies, waits for them, and re-layouts: 12.4 us -> 5.8 us
    ppermute x6, waiting for transfers between devices: 7.33 us -> 13.4 us  [moved_along(): return lax.ppermute(value, 'tensor', perm)]
  transfers between devices with their start and end apart: 13 -> 15, of which waited for: 4 -> 8; matrix products, arithmetic and copies ran while one was open for 0% -> 0% of each run, Pallas kernels for 8% -> 7%
where the time goes in v4:
time: 187 us; the launch traced here: 184 us
  starting transfers between devices  68 us (36%)
  Pallas kernels  63.8 us (34%)
  waiting for transfers between devices  36.7 us (20%)
  blocking collectives  7.12 us (4%)
  local copies, waits for them, and re-layouts  5.87 us (3%)
    pallas_call x1, Pallas kernels, on_device(): local_call(functools.partial(spread_body, held), shape(slots, length, wid...  42.9 us
    all_to_all x4, starting transfers between devices, exchange(): lax.all_to_all(value, axis, split_axis=0, concat_axis=0, axis_index_group...  31.4 us
    ppermute x6, starting transfers between devices, moved_along(): return lax.ppermute(value, 'tensor', perm)  23.2 us
    ppermute x6, waiting for transfers between devices, moved_along(): return lax.ppermute(value, 'tensor', perm)  13.4 us
    ppermute x1, waiting for transfers between devices, on_device(): crossed = lax.ppermute(after(give, contributions), 'tensor', across)  12.5 us
    all_to_all x4, waiting for transfers between devices, exchange(): lax.all_to_all(value, axis, split_axis=0, concat_axis=0, axis_index_group...  9.33 us
    unnamed x36, local copies, waits for them, and re-layouts  5.8 us
    pallas_call x1, Pallas kernels, on_device(): local_call(projection_body, (shape(chips, rows, out_block), shape(chips,...  5.15 us
  transfers between devices with their start and end apart: 15, of which 8 were waited for; matrix products, arithmetic and copies ran while one was open for 0% of the time, Pallas kernels for 7%

profile of v4, /device:TPU:1, one launch (start us, length us, event | category | flops | bytes accessed | tf_op | source)
XLA Modules:
  0.0 184.2 jit_solution(3103079216088859762)
XLA Ops:
  0.6 0.6 pad_add_fusion.place_ref
  1.3 42.9 %shard_map.102 = bf16[32,32,640]{2,1,0:T(8,128)(2,1)} custom-call(s32[4]{0:T(128)} %pad_add_fusion.place_ref, s32[512]{0:T(512)} %index_ref.1, s32[96]{0:T(128)} %storage_ref.1, bf16[512,512]{1,0:T(8,128)(2,1)} %tokens_ref.1, bf16[512,128]{1,0:T(8,128)(2,1)} %refs_0_), custom_call_target="tpu_custom_call" | custom-call | bytes 1966080 | tf_op jit(solution)/shard_map/pallas_call | solution.py:266
  44.1 0.0 copy-start.7
  44.2 0.0 copy-start.2
  44.2 13.9 %all-to-all-start = ((bf16[32,32,640]{2,1,0:T(8,128)(2,1)}), bf16[32,32,640]{2,1,0:T(8,128)(2,1)S(1)}, u32[]{:S(2)}, u32[]{:S(2)}) async-start(bf16[32,32,640]{2,1,0:T(8,128)(2,1)} %shard_map.102), calls=%async_computation | async-start | bytes 2621440 | tf_op jit(solution)/shard_map/all_to_all | solution.py:231
  58.1 5.9 %collective-permute-start = (bf16[512,128]{1,0:T(8,128)(2,1)S(1)}, bf16[512,128]{1,0:T(8,128)(2,1)S(1)}, u32[]{:S(2)}, u32[]{:S(2)}) collective-permute-start(bf16[512,128]{1,0:T(8,128)(2,1)S(1)} %copy-done.7), channel_id=1, source_target_pairs={{0,12},{1,13},{2,14},{3,15},{4,0},{5,1},{6,2},{7,3},{8,4},{9,5},{1... | collective-permute-start | bytes 393224 | tf_op jit(solution)/shard_map/ppermute | solution.py:264
  63.9 1.9 %collective-permute-start.1 = (bf16[512,128]{1,0:T(8,128)(2,1)S(1)}, bf16[512,128]{1,0:T(8,128)(2,1)S(1)}, u32[]{:S(2)}, u32[]{:S(2)}) collective-permute-start(bf16[512,128]{1,0:T(8,128)(2,1)S(1)} %copy-done.7), channel_id=1, source_target_pairs={{0,4},{1,5},{2,6},{3,7},{4,8},{5,9},{6,10},{7,11},{8,12},{9,13},{1... | collective-permute-start | bytes 393224 | tf_op jit(solution)/shard_map/ppermute | solution.py:264
  65.9 5.8 %collective-permute-start.2 = (bf16[512,128]{1,0:T(8,128)(2,1)S(1)}, bf16[512,128]{1,0:T(8,128)(2,1)S(1)}, u32[]{:S(2)}, u32[]{:S(2)}) collective-permute-start(bf16[512,128]{1,0:T(8,128)(2,1)S(1)} %copy-done.7), channel_id=1, source_target_pairs={{0,8},{1,9},{2,10},{3,11},{4,12},{5,13},{6,14},{7,15},{8,0},{9,1},... | collective-permute-start | bytes 393224 | tf_op jit(solution)/shard_map/ppermute | solution.py:264
  71.7 0.0 collective-permute-done.refs_1_
  71.7 1.2 collective-permute-done.1.refs_2_
  73.0 6.6 %collective-permute-done.2.refs_3_ = bf16[512,128]{1,0:T(8,128)(2,1)S(1)} collective-permute-done((bf16[512,128]{1,0:T(8,128)(2,1)S(1)}, bf16[512,128]{1,0:T(8,128)(2,1)S(1)}, u32[]{:S(2)}, u32[]{:S(2)}) %collective-permute-start.2) | collective-permute-done | bytes 131104 | tf_op jit(solution)/shard_map/ppermute | solution.py:264
  79.6 0.8 shard_map.103.near_ref
  80.4 1.9 %collective-permute-start.4 = (bf16[4,512,128]{2,1,0:T(8,128)(2,1)}, bf16[4,512,128]{2,1,0:T(8,128)(2,1)}, u32[]{:S(2)}, u32[]{:S(2)}) collective-permute-start(bf16[4,512,128]{2,1,0:T(8,128)(2,1)} %shard_map.103.near_ref), channel_id=1, source_target_pairs={{0,2},{1,3},{2,0},{3,1},{4,6},{5,7},{6,4},{7,5},{8,10},{9,11},{10,... | collective-permute-start | bytes 1572872 | tf_op jit(solution)/shard_map/ppermute | solution.py:303
  82.3 0.0 copy-start.6
  82.4 1.0 copy-done.6
  83.4 5.1 %shard_map.104 = (bf16[8,512,128]{2,1,0:T(8,128)(2,1)S(1)}, bf16[8,512,128]{2,1,0:T(8,128)(2,1)}) custom-call(s32[4]{0:T(128)S(1)} %copy-done.12, bf16[512,512]{1,0:T(8,128)(2,1)S(1)} %copy-done.6, bf16[512,2048]{1,0:T(8,128)(2,1)S(1)} %copy-done.2), custom_call_target="tpu_custom_call" | custom-call | flops 1073741824 | bytes 4718592 | tf_op jit(solution)/shard_map/pallas_call | solution.py:307
  88.5 1.0 copy-done.3
  89.5 4.5 %collective-permute-start.6 = (bf16[8,512,128]{2,1,0:T(8,128)(2,1)}, bf16[8,512,128]{2,1,0:T(8,128)(2,1)}, u32[]{:S(2)}, u32[]{:S(2)}) collective-permute-start(bf16[8,512,128]{2,1,0:T(8,128)(2,1)} %get-tuple-element.35), channel_id=1, source_target_pairs={{0,1},{1,0},{2,3},{3,2},{4,5},{5,4},{6,7},{7,6},{8,9},{9,8},{10,11... | collective-permute-start | bytes 3145736 | tf_op jit(solution)/shard_map/ppermute | solution.py:314
  94.0 1.9 %collective-permute-start.3 = (bf16[4,512,128]{2,1,0:T(8,128)(2,1)}, bf16[4,512,128]{2,1,0:T(8,128)(2,1)}, u32[]{:S(2)}, u32[]{:S(2)}) collective-permute-start(bf16[4,512,128]{2,1,0:T(8,128)(2,1)} %shard_map.103.near_ref), channel_id=1, source_target_pairs={{0,1},{1,0},{2,3},{3,2},{4,5},{5,4},{6,7},{7,6},{8,9},{9,8},{10,11... | collective-permute-start | bytes 1572872 | tf_op jit(solution)/shard_map/ppermute | solution.py:304
  95.9 0.0 collective-permute-done.4.far_ref
  96.0 2.9 %collective-permute-start.5 = (bf16[4,512,128]{2,1,0:T(8,128)(2,1)}, bf16[4,512,128]{2,1,0:T(8,128)(2,1)}, u32[]{:S(2)}, u32[]{:S(2)}) collective-permute-start(bf16[4,512,128]{2,1,0:T(8,128)(2,1)} %collective-permute-done.4.far_ref), channel_id=1, source_target_pairs={{0,1},{1,0},{2,3},{3,2},{4,5},{5,4},{6,7},{7,6},{8,9},{9,8},{10,11... | collective-permute-start | bytes 1572872 | tf_op jit(solution)/shard_map/ppermute | solution.py:305
  98.9 0.0 copy-done.16
  98.9 0.0 copy-done.17
  98.9 0.1 select_reduce_fusion
  99.0 0.1 sub.12
  99.1 0.1 select_reduce_fusion.1.pick_ref
  99.2 0.0 copy-start.10
  99.2 0.0 collective-permute-done.3.near_other_ref
  99.2 1.5 collective-permute-done.5.far_other_ref
  100.7 0.0 collective-permute-done.6.came_ref
  100.7 0.0 all-to-all-done.rows_ref
  100.7 0.0 copy-start.5
  100.7 0.9 copy-done.5
  101.7 1.8 shard_map.105
  103.4 2.2 %all-gather = bf16[2048,128]{1,0:T(8,128)(2,1)S(1)} all-gather(bf16[1024,128]{1,0:T(8,128)(2,1)S(1)} %shard_map.105), channel_id=2, replica_groups={{0,1},{2,3},{4,5},{6,7},{8,9},{10,11},{12,13},{14,15},{16,17},{18,19},{..., dimensions={0}, use_global_device_ids=true | all-gather | bytes 786432 | tf_op jit(solution)/shard_map/all_gather | solution.py:327
  105.6 0.7 dynamic-slice_reduce_fusion
  106.3 4.7 %all-to-all-start.1 = ((bf16[8,64,128]{2,1,0:T(8,128)(2,1)}), bf16[8,64,128]{2,1,0:T(8,128)(2,1)S(1)}, u32[]{:S(2)}, u32[]{:S(2)}) async-start(bf16[8,64,128]{2,1,0:T(8,128)(2,1)} %bitcast.12), calls=%async_computation.1 | async-start | bytes 262144 | tf_op jit(solution)/shard_map/all_to_all | solution.py:231
  111.0 2.8 %shard_map.106.base_ref = f32[512,512]{1,0:T(8,128)S(1)} custom-call(s32[4]{0:T(128)S(1)} %copy-done.12, bf16[4,512,128]{2,1,0:T(8,128)(2,1)} %shard_map.103.near_ref, bf16[4,512,128]{2,1,0:T(8,128)(2,1)} %collective-permute-done.3.near_other_ref, bf16[4,512,128]{2,1,0:T(8,128)(2,1)} %collective-permute-done.4.far_ref, ...), custom_call_target="tpu_custom_call" | custom-call | flops 1073741824 | bytes 4194304 | tf_op jit(solution)/shard_map/pallas_call | solution.py:330
  113.8 1.0 copy-done
  114.8 4.1 %all-to-all-done.1.parts_ref = bf16[8,64,128]{2,1,0:T(8,128)(2,1)S(1)} async-done(((bf16[8,64,128]{2,1,0:T(8,128)(2,1)}), bf16[8,64,128]{2,1,0:T(8,128)(2,1)S(1)}, u32[]{:S(2)}, u32[]{:S(2)}) %all-to-all-start.1) | async-done | bytes 131104 | tf_op jit(solution)/shard_map/all_to_all | solution.py:231
  118.9 0.7 shard_map.107
  119.5 3.4 %all-to-all-start.2 = ((bf16[8,64,128]{2,1,0:T(8,128)(2,1)}), bf16[8,64,128]{2,1,0:T(8,128)(2,1)S(1)}, u32[]{:S(2)}, u32[]{:S(2)}) async-start(bf16[8,64,128]{2,1,0:T(8,128)(2,1)} %shard_map.107), calls=%async_computation.2 | async-start | bytes 262144 | tf_op jit(solution)/shard_map/all_to_all | solution.py:231
  122.9 0.0 copy-start.4
  122.9 1.2 copy-done.4
  124.2 1.5 shard_map.108
  125.6 5.2 %all-to-all-done.2 = bf16[8,64,128]{2,1,0:T(8,128)(2,1)S(1)} async-done(((bf16[8,64,128]{2,1,0:T(8,128)(2,1)}), bf16[8,64,128]{2,1,0:T(8,128)(2,1)S(1)}, u32[]{:S(2)}, u32[]{:S(2)}) %all-to-all-start.2) | async-done | bytes 131104 | tf_op jit(solution)/shard_map/all_to_all | solution.py:231
  130.9 4.9 %all_gather.11 = bf16[2,512,128]{2,1,0:T(8,128)(2,1)} all-gather(bf16[1,512,128]{2,1,0:T(8,128)(2,1)S(1)} %bitcast.11), channel_id=1, replica_groups={{0,1},{2,3},{4,5},{6,7},{8,9},{10,11},{12,13},{14,15},{16,17},{18,19},{..., dimensions={0}, use_global_device_ids=true | all-gather | bytes 393216 | tf_op jit(solution)/shard_map/all_gather | solution.py:355
  135.8 3.0 %shard_map.109 = bf16[32,32,640]{2,1,0:T(8,128)(2,1)} custom-call(s32[32]{0:T(128)} %copy-done.10, bf16[1024,128]{1,0:T(8,128)(2,1)} %bitcast.8, bf16[3,64,512]{2,1,0:T(8,128)(2,1)} %down_ref.3, bf16[3,64,128]{2,1,0:T(8,128)(2,1)} %up_ref.3), custom_call_target="tpu_custom_call" | custom-call | flops 251658240 | bytes 1310720 | tf_op jit(solution)/shard_map/pallas_call | solution.py:358
  138.8 9.5 %all-to-all-start.3 = ((bf16[32,32,640]{2,1,0:T(8,128)(2,1)}), bf16[32,32,640]{2,1,0:T(8,128)(2,1)}, u32[]{:S(2)}, u32[]{:S(2)}) async-start(bf16[32,32,640]{2,1,0:T(8,128)(2,1)} %shard_map.109), calls=%async_computation.3 | async-start | bytes 2621440 | tf_op jit(solution)/shard_map/all_to_all | solution.py:231
  148.3 2.2 %collective-permute-start.7 = (bf16[4,512,128]{2,1,0:T(8,128)(2,1)S(1)}, bf16[4,512,128]{2,1,0:T(8,128)(2,1)S(1)}, u32[]{:S(2)}, u32[]{:S(2)}) collective-permute-start(bf16[4,512,128]{2,1,0:T(8,128)(2,1)S(1)} %get-tuple-element.51), channel_id=1, source_target_pairs={{0,2},{1,3},{2,0},{3,1},{4,6},{5,7},{6,4},{7,5},{8,10},{9,11},{10,... | collective-permute-start | bytes 1572872 | tf_op jit(solution)/shard_map/ppermute | solution.py:369
  150.5 0.1 convert_reduce_fusion
  150.6 12.5 %collective-permute-done.7.came_ref = bf16[4,512,128]{2,1,0:T(8,128)(2,1)S(1)} collective-permute-done((bf16[4,512,128]{2,1,0:T(8,128)(2,1)S(1)}, bf16[4,512,128]{2,1,0:T(8,128)(2,1)S(1)}, u32[]{:S(2)}, u32[]{:S(2)}) %collective-permute-start.7) | collective-permute-done | bytes 524320 | tf_op jit(solution)/shard_map/ppermute | solution.py:369
  163.1 0.1 shard_map.110
  163.2 0.0 copy-start.9
  163.3 2.0 %collective-permute-start.8 = (bf16[512,128]{1,0:T(8,128)(2,1)S(1)}, bf16[512,128]{1,0:T(8,128)(2,1)S(1)}, u32[]{:S(2)}, u32[]{:S(2)}) collective-permute-start(bf16[512,128]{1,0:T(8,128)(2,1)S(1)} %get-tuple-element.53), channel_id=1, source_target_pairs={{0,4},{1,5},{2,6},{3,7},{4,8},{5,9},{6,10},{7,11},{8,12},{9,13},{1... | collective-permute-start | bytes 393224 | tf_op jit(solution)/shard_map/ppermute | solution.py:264
  165.3 5.4 %collective-permute-start.9 = (bf16[512,128]{1,0:T(8,128)(2,1)S(1)}, bf16[512,128]{1,0:T(8,128)(2,1)S(1)}, u32[]{:S(2)}, u32[]{:S(2)}) collective-permute-start(bf16[512,128]{1,0:T(8,128)(2,1)S(1)} %get-tuple-element.54), channel_id=1, source_target_pairs={{0,12},{1,13},{2,14},{3,15},{4,0},{5,1},{6,2},{7,3},{8,4},{9,5},{1... | collective-permute-start | bytes 393224 | tf_op jit(solution)/shard_map/ppermute | solution.py:264
  170.7 2.2 %collective-permute-start.10 = (bf16[512,128]{1,0:T(8,128)(2,1)S(1)}, bf16[512,128]{1,0:T(8,128)(2,1)S(1)}, u32[]{:S(2)}, u32[]{:S(2)}) collective-permute-start(bf16[512,128]{1,0:T(8,128)(2,1)S(1)} %get-tuple-element.55), channel_id=1, source_target_pairs={{0,8},{1,9},{2,10},{3,11},{4,12},{5,13},{6,14},{7,15},{8,0},{9,1},... | collective-permute-start | bytes 393224 | tf_op jit(solution)/shard_map/ppermute | solution.py:264
  172.9 2.4 %shard_map.112 = (f32[3,64,512]{2,1,0:T(8,128)}, f32[3,64,128]{2,1,0:T(8,128)}) custom-call(s32[32]{0:T(128)S(1)} %copy-done.11, f32[3]{0:T(128)S(1)} %maximum_divide_fusion.scale_ref, bf16[1024,128]{1,0:T(8,128)(2,1)S(1)} %bitcast.9, bf16[32,32,640]{2,1,0:T(8,128)(2,1)S(1)} %all-to-all-done.rows_ref), custom_call_target="tpu_custom_call" | custom-call | flops 251658240 | bytes 1310720 | tf_op jit(solution)/shard_map/pallas_call | solution.py:380
  175.2 0.0 collective-permute-done.8.refs_1_
  175.2 0.4 collective-permute-done.9.refs_2_
  175.6 5.2 %collective-permute-done.10.refs_3_ = bf16[512,128]{1,0:T(8,128)(2,1)S(1)} collective-permute-done((bf16[512,128]{1,0:T(8,128)(2,1)S(1)}, bf16[512,128]{1,0:T(8,128)(2,1)S(1)}, u32[]{:S(2)}, u32[]{:S(2)}) %collective-permute-start.10) | collective-permute-done | bytes 131104 | tf_op jit(solution)/shard_map/ppermute | solution.py:264
  180.8 0.0 all-to-all-done.3.came_ref
  180.8 0.6 copy-done.15
  181.4 2.8 %shard_map.111 = (bf16[512,512]{1,0:T(8,128)(2,1)}, bf16[512,128]{1,0:T(8,128)(2,1)}) custom-call(s32[4]{0:T(128)} %pad_add_fusion.place_ref, s32[512]{0:T(512)} %index_ref.1, s32[96]{0:T(128)} %storage_ref.1, f32[512,512]{1,0:T(8,128)} %copy-done, bf16[32,32,640]{2,1,0:T(8,128)(2,1)} %all-to-all-done.3.came_ref, bf16[512,128]{1,0:T(8,128)(2,1)} %copy-done.9, ...), custom_call_target="tpu_custom_call" | custom-call | bytes 2883584 | tf_op jit(solution)/shard_map/pallas_call | solution.py:388
  (23 shorter events, 0.1 us)
Async XLA Ops:
  44.1 13.9 %copy-start.7 = (bf16[512,128]{1,0:T(8,128)(2,1)S(1)}, bf16[512,128]{1,0:T(8,128)(2,1)}, u32[]{:S(2)}) copy-start(bf16[512,128]{1,0:T(8,128)(2,1)} %refs_0_) | copy-start | bytes 393220
  44.2 38.2 %copy-start.2 = (bf16[512,2048]{1,0:T(8,128)(2,1)S(1)}, bf16[512,2048]{1,0:T(8,128)(2,1)}, u32[]{:S(2)}) copy-start(bf16[512,2048]{1,0:T(8,128)(2,1)} %weight_ref.3) | copy-start | bytes 6291460
  44.2 38.2 %copy-start.12 = (s32[4]{0:T(128)S(1)}, s32[4]{0:T(128)}, u32[]{:S(2)}) copy-start(s32[4]{0:T(128)} %pad_add_fusion.place_ref) | copy-start | bytes 52
  44.2 56.5 %all-to-all-start = ((bf16[32,32,640]{2,1,0:T(8,128)(2,1)}), bf16[32,32,640]{2,1,0:T(8,128)(2,1)S(1)}, u32[]{:S(2)}, u32[]{:S(2)}) async-start(bf16[32,32,640]{2,1,0:T(8,128)(2,1)} %shard_map.102), calls=%async_computation | async-start | bytes 2621440 | tf_op jit(solution)/shard_map/all_to_all | solution.py:231
  58.1 13.7 %collective-permute-start = (bf16[512,128]{1,0:T(8,128)(2,1)S(1)}, bf16[512,128]{1,0:T(8,128)(2,1)S(1)}, u32[]{:S(2)}, u32[]{:S(2)}) collective-permute-start(bf16[512,128]{1,0:T(8,128)(2,1)S(1)} %copy-done.7), channel_id=1, source_target_pairs={{0,12},{1,13},{2,14},{3,15},{4,0},{5,1},{6,2},{7,3},{8,4},{9,5},{1... | collective-permute-start | bytes 393224 | tf_op jit(solution)/shard_map/ppermute | solution.py:264
  63.9 9.0 %collective-permute-start.1 = (bf16[512,128]{1,0:T(8,128)(2,1)S(1)}, bf16[512,128]{1,0:T(8,128)(2,1)S(1)}, u32[]{:S(2)}, u32[]{:S(2)}) collective-permute-start(bf16[512,128]{1,0:T(8,128)(2,1)S(1)} %copy-done.7), channel_id=1, source_target_pairs={{0,4},{1,5},{2,6},{3,7},{4,8},{5,9},{6,10},{7,11},{8,12},{9,13},{1... | collective-permute-start | bytes 393224 | tf_op jit(solution)/shard_map/ppermute | solution.py:264
  65.9 13.7 %collective-permute-start.2 = (bf16[512,128]{1,0:T(8,128)(2,1)S(1)}, bf16[512,128]{1,0:T(8,128)(2,1)S(1)}, u32[]{:S(2)}, u32[]{:S(2)}) collective-permute-start(bf16[512,128]{1,0:T(8,128)(2,1)S(1)} %copy-done.7), channel_id=1, source_target_pairs={{0,8},{1,9},{2,10},{3,11},{4,12},{5,13},{6,14},{7,15},{8,0},{9,1},... | collective-permute-start | bytes 393224 | tf_op jit(solution)/shard_map/ppermute | solution.py:264
  80.4 15.5 %collective-permute-start.4 = (bf16[4,512,128]{2,1,0:T(8,128)(2,1)}, bf16[4,512,128]{2,1,0:T(8,128)(2,1)}, u32[]{:S(2)}, u32[]{:S(2)}) collective-permute-start(bf16[4,512,128]{2,1,0:T(8,128)(2,1)} %shard_map.103.near_ref), channel_id=1, source_target_pairs={{0,2},{1,3},{2,0},{3,1},{4,6},{5,7},{6,4},{7,5},{8,10},{9,11},{10,... | collective-permute-start | bytes 1572872 | tf_op jit(solution)/shard_map/ppermute | solution.py:303
  82.3 1.0 copy-start.6
  83.4 15.5 %copy-start.16 = (s32[512]{0:T(512)S(1)}, s32[512]{0:T(512)}, u32[]{:S(2)}) copy-start(s32[512]{0:T(512)} %index_ref.1) | copy-start | bytes 6148
  83.4 15.5 %copy-start.17 = (s32[96]{0:T(128)S(1)}, s32[96]{0:T(128)}, u32[]{:S(2)}) copy-start(s32[96]{0:T(128)} %storage_ref.1) | copy-start | bytes 1156
  83.4 17.3 %copy-start.8 = (bf16[3,64,128]{2,1,0:T(8,128)(2,1)S(1)}, bf16[3,64,128]{2,1,0:T(8,128)(2,1)}, u32[]{:S(2)}) copy-start(bf16[3,64,128]{2,1,0:T(8,128)(2,1)} %up_ref.3) | copy-start | bytes 147460
  88.5 1.0 copy-start.3
  89.5 11.2 %collective-permute-start.6 = (bf16[8,512,128]{2,1,0:T(8,128)(2,1)}, bf16[8,512,128]{2,1,0:T(8,128)(2,1)}, u32[]{:S(2)}, u32[]{:S(2)}) collective-permute-start(bf16[8,512,128]{2,1,0:T(8,128)(2,1)} %get-tuple-element.35), channel_id=1, source_target_pairs={{0,1},{1,0},{2,3},{3,2},{4,5},{5,4},{6,7},{7,6},{8,9},{9,8},{10,11... | collective-permute-start | bytes 3145736 | tf_op jit(solution)/shard_map/ppermute | solution.py:314
  94.0 5.2 %collective-permute-start.3 = (bf16[4,512,128]{2,1,0:T(8,128)(2,1)}, bf16[4,512,128]{2,1,0:T(8,128)(2,1)}, u32[]{:S(2)}, u32[]{:S(2)}) collective-permute-start(bf16[4,512,128]{2,1,0:T(8,128)(2,1)} %shard_map.103.near_ref), channel_id=1, source_target_pairs={{0,1},{1,0},{2,3},{3,2},{4,5},{5,4},{6,7},{7,6},{8,9},{9,8},{10,11... | collective-permute-start | bytes 1572872 | tf_op jit(solution)/shard_map/ppermute | solution.py:304
  96.0 4.8 %collective-permute-start.5 = (bf16[4,512,128]{2,1,0:T(8,128)(2,1)}, bf16[4,512,128]{2,1,0:T(8,128)(2,1)}, u32[]{:S(2)}, u32[]{:S(2)}) collective-permute-start(bf16[4,512,128]{2,1,0:T(8,128)(2,1)} %collective-permute-done.4.far_ref), channel_id=1, source_target_pairs={{0,1},{1,0},{2,3},{3,2},{4,5},{5,4},{6,7},{7,6},{8,9},{9,8},{10,11... | collective-permute-start | bytes 1572872 | tf_op jit(solution)/shard_map/ppermute | solution.py:305
  99.2 7.1 %copy-start.10 = (s32[32]{0:T(128)}, s32[32]{0:T(128)S(1)}, u32[]{:S(2)}) copy-start(s32[32]{0:T(128)S(1)} %select_reduce_fusion.1.pick_ref) | copy-start | bytes 388
  100.7 0.9 copy-start.5
  106.3 12.5 %all-to-all-start.1 = ((bf16[8,64,128]{2,1,0:T(8,128)(2,1)}), bf16[8,64,128]{2,1,0:T(8,128)(2,1)S(1)}, u32[]{:S(2)}, u32[]{:S(2)}) async-start(bf16[8,64,128]{2,1,0:T(8,128)(2,1)} %bitcast.12), calls=%async_computation.1 | async-start | bytes 262144 | tf_op jit(solution)/shard_map/all_to_all | solution.py:231
  113.8 1.0 copy-start
  119.5 11.3 %all-to-all-start.2 = ((bf16[8,64,128]{2,1,0:T(8,128)(2,1)}), bf16[8,64,128]{2,1,0:T(8,128)(2,1)S(1)}, u32[]{:S(2)}, u32[]{:S(2)}) async-start(bf16[8,64,128]{2,1,0:T(8,128)(2,1)} %shard_map.107), calls=%async_computation.2 | async-start | bytes 262144 | tf_op jit(solution)/shard_map/all_to_all | solution.py:231
  122.9 1.2 copy-start.4
  138.8 11.7 %copy-start.11 = (s32[32]{0:T(128)S(1)}, s32[32]{0:T(128)}, u32[]{:S(2)}) copy-start(s32[32]{0:T(128)} %copy-done.10) | copy-start | bytes 388
  138.8 34.1 %copy-start.1 = (bf16[2,512,128]{2,1,0:T(8,128)(2,1)S(1)}, bf16[2,512,128]{2,1,0:T(8,128)(2,1)}, u32[]{:S(2)}) copy-start(bf16[2,512,128]{2,1,0:T(8,128)(2,1)} %all_gather.11) | copy-start | bytes 786436
  138.8 42.0 %all-to-all-start.3 = ((bf16[32,32,640]{2,1,0:T(8,128)(2,1)}), bf16[32,32,640]{2,1,0:T(8,128)(2,1)}, u32[]{:S(2)}, u32[]{:S(2)}) async-start(bf16[32,32,640]{2,1,0:T(8,128)(2,1)} %shard_map.109), calls=%async_computation.3 | async-start | bytes 2621440 | tf_op jit(solution)/shard_map/all_to_all | solution.py:231
  148.3 14.8 %collective-permute-start.7 = (bf16[4,512,128]{2,1,0:T(8,128)(2,1)S(1)}, bf16[4,512,128]{2,1,0:T(8,128)(2,1)S(1)}, u32[]{:S(2)}, u32[]{:S(2)}) collective-permute-start(bf16[4,512,128]{2,1,0:T(8,128)(2,1)S(1)} %get-tuple-element.51), channel_id=1, source_target_pairs={{0,2},{1,3},{2,0},{3,1},{4,6},{5,7},{6,4},{7,5},{8,10},{9,11},{10,... | collective-permute-start | bytes 1572872 | tf_op jit(solution)/shard_map/ppermute | solution.py:369
  163.2 12.0 %copy-start.9 = (bf16[512,128]{1,0:T(8,128)(2,1)}, bf16[512,128]{1,0:T(8,128)(2,1)S(1)}, u32[]{:S(2)}) copy-start(bf16[512,128]{1,0:T(8,128)(2,1)S(1)} %get-tuple-element.52.refs_0_) | copy-start | bytes 393220
  163.3 12.0 %collective-permute-start.8 = (bf16[512,128]{1,0:T(8,128)(2,1)S(1)}, bf16[512,128]{1,0:T(8,128)(2,1)S(1)}, u32[]{:S(2)}, u32[]{:S(2)}) collective-permute-start(bf16[512,128]{1,0:T(8,128)(2,1)S(1)} %get-tuple-element.53), channel_id=1, source_target_pairs={{0,4},{1,5},{2,6},{3,7},{4,8},{5,9},{6,10},{7,11},{8,12},{9,13},{1... | collective-permute-start | bytes 393224 | tf_op jit(solution)/shard_map/ppermute | solution.py:264
  165.3 10.3 %collective-permute-start.9 = (bf16[512,128]{1,0:T(8,128)(2,1)S(1)}, bf16[512,128]{1,0:T(8,128)(2,1)S(1)}, u32[]{:S(2)}, u32[]{:S(2)}) collective-permute-start(bf16[512,128]{1,0:T(8,128)(2,1)S(1)} %get-tuple-element.54), channel_id=1, source_target_pairs={{0,12},{1,13},{2,14},{3,15},{4,0},{5,1},{6,2},{7,3},{8,4},{9,5},{1... | collective-permute-start | bytes 393224 | tf_op jit(solution)/shard_map/ppermute | solution.py:264
  170.7 10.1 %collective-permute-start.10 = (bf16[512,128]{1,0:T(8,128)(2,1)S(1)}, bf16[512,128]{1,0:T(8,128)(2,1)S(1)}, u32[]{:S(2)}, u32[]{:S(2)}) collective-permute-start(bf16[512,128]{1,0:T(8,128)(2,1)S(1)} %get-tuple-element.55), channel_id=1, source_target_pairs={{0,8},{1,9},{2,10},{3,11},{4,12},{5,13},{6,14},{7,15},{8,0},{9,1},... | collective-permute-start | bytes 393224 | tf_op jit(solution)/shard_map/ppermute | solution.py:264
  175.2 5.6 %copy-start.13 = (bf16[512,128]{1,0:T(8,128)(2,1)}, bf16[512,128]{1,0:T(8,128)(2,1)S(1)}, u32[]{:S(2)}) copy-start(bf16[512,128]{1,0:T(8,128)(2,1)S(1)} %collective-permute-done.8.refs_1_) | copy-start | bytes 393220
  175.6 5.2 %copy-start.14 = (bf16[512,128]{1,0:T(8,128)(2,1)}, bf16[512,128]{1,0:T(8,128)(2,1)S(1)}, u32[]{:S(2)}) copy-start(bf16[512,128]{1,0:T(8,128)(2,1)S(1)} %collective-permute-done.9.refs_2_) | copy-start | bytes 393220
  180.8 0.6 copy-start.15

commit v5 on v3

--- a/solution.py
+++ b/solution.py
@@ -12,10 +12,11 @@
 bf16 = jnp.bfloat16
 SMEM = pl.BlockSpec(memory_space=pltpu.SMEM)
 VMEM = pl.BlockSpec(memory_space=pltpu.VMEM)
-VMEM_LIMIT = 40 * 1024 * 1024
-
-
-def local_call(body, out_shape, specs, scratch=(), flops=0, moved=0):
+VMEM_LIMIT = 16 * 1024 * 1024
+HBM_LIMIT = 60 * 1024 * 1024
+
+
+def local_call(body, out_shape, specs, scratch=(), flops=0, moved=0, limit=VMEM_LIMIT):
     multiple = isinstance(out_shape, (tuple, list))
     return pl.pallas_call(
         body,
@@ -23,7 +24,7 @@
         in_specs=specs,
         out_specs=(VMEM,) * len(out_shape) if multiple else VMEM,
         scratch_shapes=list(scratch),
-        compiler_params=pltpu.CompilerParams(vmem_limit_bytes=VMEM_LIMIT),
+        compiler_params=pltpu.CompilerParams(vmem_limit_bytes=limit),
         cost_estimate=pl.CostEstimate(flops=flops, bytes_accessed=moved, transcendentals=0),
     )
 
@@ -228,6 +229,7 @@
         shape(slots, length, width),
         [SMEM, SMEM, SMEM, VMEM, VMEM],
         moved=3 * slots * length * width,
+        limit=HBM_LIMIT,
     )(place, sequence_index, storage_row, tokens, cotangent)
     arrived = exchange(spread, "dp")
 
@@ -244,12 +246,13 @@
     across = [(t, t ^ 2) for t in range(tensor_count)]
     quarter = chips // 2
     cot = after(cotangent, spread)
+    opposite = moved_along(cot, quarter)
     near = local_call(
         pack_body,
         shape(quarter, rows, out_block),
         [VMEM] * quarter,
         moved=4 * quarter * rows * out_block,
-    )(cot, moved_along(cot, -2), moved_along(cot, 2), moved_along(cot, quarter))
+    )(cot, moved_along(cot, -2), moved_along(cot, 2), opposite)
     far = lax.ppermute(near, "tensor", across)
     near_other = lax.ppermute(near, "tensor", swap)
     far_other = lax.ppermute(far, "tensor", swap)
@@ -260,22 +263,11 @@
         [SMEM, VMEM, VMEM],
         flops=2 * rows * block * tensor_count * out_block,
         moved=2 * (rows * block + 2 * block * tensor_count * out_block),
-    )(after(place, spread), tokens, weight)
+    )(after(place, near), tokens, weight)
     came = lax.ppermute(send, "tensor", swap)
-    keep, give = local_call(
-        pair_body,
-        (shape(quarter, rows, out_block),) * 2,
-        [VMEM, VMEM],
-        moved=6 * chips * rows * out_block,
-    )(own, came)
-    base = local_call(
-        base_body,
-        shape(rows, block, dtype=f32),
-        [SMEM, VMEM, VMEM, VMEM, VMEM, VMEM],
-        flops=2 * rows * block * tensor_count * out_block,
-        moved=2 * (2 * rows * tensor_count * out_block),
-    )(place, near, near_other, far, far_other, weight)
-    arrived, base, keep, give = lax.optimization_barrier((arrived, base, keep, give))
+    arrived, near_other, far_other, own, came = lax.optimization_barrier(
+        (arrived, near_other, far_other, own, came)
+    )
 
     half = slots * length // 2
     part = local_call(
@@ -308,16 +300,28 @@
     )(pick, ranks, down, up)
     returned = exchange(contributions, "dp")
 
-    crossed = lax.ppermute(after(give, contributions), "tensor", across)
+    keep, give = local_call(
+        pair_body,
+        (shape(quarter, rows, out_block),) * 2,
+        [VMEM, VMEM],
+        moved=6 * chips * rows * out_block,
+    )(after(own, contributions), came)
+    crossed = lax.ppermute(give, "tensor", across)
+    base = local_call(
+        base_body,
+        shape(rows, block, dtype=f32),
+        [SMEM, VMEM, VMEM, VMEM, VMEM, VMEM],
+        flops=2 * rows * block * tensor_count * out_block,
+        moved=2 * (2 * rows * tensor_count * out_block),
+    )(after(place, give), near, near_other, far, far_other, weight)
     summed = local_call(
         neighbour_body,
         (shape(rows, out_block),) * quarter,
         [VMEM, VMEM],
         moved=6 * quarter * rows * out_block,
     )(keep, crossed)
-    parts = [summed[0]]
-    for value, distance in zip(summed[1:], (2, -2, quarter)):
-        parts.append(moved_along(value, distance))
+    opposite = moved_along(summed[3], quarter)
+    parts = [summed[0], moved_along(summed[1], 2), moved_along(summed[2], -2), opposite]
 
     grad_down, grad_up = local_call(
         gradient_body,
@@ -332,6 +336,7 @@
         (shape(rows, block), shape(rows, out_block)),
         [SMEM, SMEM, SMEM, VMEM, VMEM] + [VMEM] * quarter,
         moved=2 * (3 * rows * block + slots * length * width),
+        limit=HBM_LIMIT,
     )(place, sequence_index, storage_row, base, returned, *parts)
     return (key_value_output, token_gradient, grad_down, grad_up)
 

time: 154 us -> 145 us (0.942)
  the two profiles are of different devices: /device:TPU:1 before, /device:TPU:4 now
where the time goes in v5:
time: 145 us
  starting transfers between devices  60.7 us (42%)
  blocking collectives  31 us (21%)
  waiting for transfers between devices  23.4 us (16%)
  Pallas kernels  20.7 us (14%)
  local copies, waits for them, and re-layouts  6.78 us (5%)
    all_to_all x2, blocking collectives, exchange(): lax.all_to_all(value, axis, split_axis=0, concat_axis=0, axis_index_group...  26.9 us
    ppermute x6, starting transfers between devices, moved_along(): return lax.ppermute(value, 'tensor', perm)  26.1 us
    all_to_all x2, starting transfers between devices, exchange(): lax.all_to_all(value, axis, split_axis=0, concat_axis=0, axis_index_group...  23.5 us
    ppermute x1, waiting for transfers between devices, on_device(): crossed = lax.ppermute(give, 'tensor', across)  12.7 us
    ppermute x6, waiting for transfers between devices, moved_along(): return lax.ppermute(value, 'tensor', perm)  8.01 us
    unnamed x36, local copies, waits for them, and re-layouts  6.7 us
    pallas_call x1, Pallas kernels, on_device(): local_call(projection_body, (shape(chips, rows, out_block), shape(chips,...  5.12 us
  transfers between devices with their start and end apart: 13, of which 7 were waited for; matrix products, arithmetic and copies ran while one was open for 0% of the time, Pallas kernels for 8%

profile of v5, /device:TPU:4, one launch (start us, length us, event | category | flops | bytes accessed | tf_op | source)
XLA Modules:
  0.0 144.6 jit_solution(7890140068451546867)
XLA Ops:
  0.6 0.7 pad_add_fusion.place_ref
  1.3 2.3 %shard_map.102 = bf16[32,32,640]{2,1,0:T(8,128)(2,1)} custom-call(s32[4]{0:T(128)} %pad_add_fusion.place_ref, s32[512]{0:T(512)} %index_ref.3, s32[96]{0:T(128)} %storage_ref.3, bf16[512,512]{1,0:T(8,128)(2,1)} %tokens_ref.3, bf16[512,128]{1,0:T(8,128)(2,1)} %refs_0_), custom_call_target="tpu_custom_call" | custom-call | bytes 1966080 | tf_op jit(solution)/shard_map/pallas_call | solution.py:227
  3.6 13.6 %all-to-all-start = ((bf16[32,32,640]{2,1,0:T(8,128)(2,1)}), bf16[32,32,640]{2,1,0:T(8,128)(2,1)S(1)}, u32[]{:S(2)}, u32[]{:S(2)}) async-start(bf16[32,32,640]{2,1,0:T(8,128)(2,1)} %shard_map.102), calls=%async_computation | async-start | bytes 2621440 | tf_op jit(solution)/shard_map/all_to_all | solution.py:192
  17.2 0.0 copy-done.9
  17.2 7.7 %collective-permute-start.2 = (bf16[512,128]{1,0:T(8,128)(2,1)S(1)}, bf16[512,128]{1,0:T(8,128)(2,1)S(1)}, u32[]{:S(2)}, u32[]{:S(2)}) collective-permute-start(bf16[512,128]{1,0:T(8,128)(2,1)S(1)} %copy-done.9), channel_id=1, source_target_pairs={{0,8},{1,9},{2,10},{3,11},{4,12},{5,13},{6,14},{7,15},{8,0},{9,1},... | collective-permute-start | bytes 393224 | tf_op jit(solution)/shard_map/ppermute | solution.py:225
  24.9 2.7 %collective-permute-start.1 = (bf16[512,128]{1,0:T(8,128)(2,1)S(1)}, bf16[512,128]{1,0:T(8,128)(2,1)S(1)}, u32[]{:S(2)}, u32[]{:S(2)}) collective-permute-start(bf16[512,128]{1,0:T(8,128)(2,1)S(1)} %copy-done.9), channel_id=1, source_target_pairs={{0,4},{1,5},{2,6},{3,7},{4,8},{5,9},{6,10},{7,11},{8,12},{9,13},{1... | collective-permute-start | bytes 393224 | tf_op jit(solution)/shard_map/ppermute | solution.py:225
  27.7 5.3 %collective-permute-start = (bf16[512,128]{1,0:T(8,128)(2,1)S(1)}, bf16[512,128]{1,0:T(8,128)(2,1)S(1)}, u32[]{:S(2)}, u32[]{:S(2)}) collective-permute-start(bf16[512,128]{1,0:T(8,128)(2,1)S(1)} %copy-done.9), channel_id=1, source_target_pairs={{0,12},{1,13},{2,14},{3,15},{4,0},{5,1},{6,2},{7,3},{8,4},{9,5},{1... | collective-permute-start | bytes 393224 | tf_op jit(solution)/shard_map/ppermute | solution.py:225
  32.9 0.0 collective-permute-done.2.refs_3_
  32.9 2.9 %collective-permute-done.1.refs_2_ = bf16[512,128]{1,0:T(8,128)(2,1)S(1)} collective-permute-done((bf16[512,128]{1,0:T(8,128)(2,1)S(1)}, bf16[512,128]{1,0:T(8,128)(2,1)S(1)}, u32[]{:S(2)}, u32[]{:S(2)}) %collective-permute-start.1) | collective-permute-done | bytes 131104 | tf_op jit(solution)/shard_map/ppermute | solution.py:225
  35.8 1.7 %collective-permute-done.refs_1_ = bf16[512,128]{1,0:T(8,128)(2,1)S(1)} collective-permute-done((bf16[512,128]{1,0:T(8,128)(2,1)S(1)}, bf16[512,128]{1,0:T(8,128)(2,1)S(1)}, u32[]{:S(2)}, u32[]{:S(2)}) %collective-permute-start) | collective-permute-done | bytes 131104 | tf_op jit(solution)/shard_map/ppermute | solution.py:225
  37.5 0.8 shard_map.103.near_ref
  38.3 2.4 %collective-permute-start.4 = (bf16[4,512,128]{2,1,0:T(8,128)(2,1)}, bf16[4,512,128]{2,1,0:T(8,128)(2,1)}, u32[]{:S(2)}, u32[]{:S(2)}) collective-permute-start(bf16[4,512,128]{2,1,0:T(8,128)(2,1)} %shard_map.103.near_ref), channel_id=1, source_target_pairs={{0,2},{1,3},{2,0},{3,1},{4,6},{5,7},{6,4},{7,5},{8,10},{9,11},{10,... | collective-permute-start | bytes 1572872 | tf_op jit(solution)/shard_map/ppermute | solution.py:256
  40.7 0.0 copy-done.1
  40.7 0.0 copy-done.12
  40.7 0.0 copy-start.8
  40.7 1.0 copy-done.8
  41.8 5.1 %shard_map.104 = (bf16[8,512,128]{2,1,0:T(8,128)(2,1)S(1)}, bf16[8,512,128]{2,1,0:T(8,128)(2,1)}) custom-call(s32[4]{0:T(128)S(1)} %copy-done.12, bf16[512,512]{1,0:T(8,128)(2,1)S(1)} %copy-done.8, bf16[512,2048]{1,0:T(8,128)(2,1)S(1)} %copy-done.1), custom_call_target="tpu_custom_call" | custom-call | flops 1073741824 | bytes 4718592 | tf_op jit(solution)/shard_map/pallas_call | solution.py:260
  46.9 1.0 copy-done.3
  47.9 1.9 %collective-permute-start.6 = (bf16[8,512,128]{2,1,0:T(8,128)(2,1)}, bf16[8,512,128]{2,1,0:T(8,128)(2,1)S(1)}, u32[]{:S(2)}, u32[]{:S(2)}) collective-permute-start(bf16[8,512,128]{2,1,0:T(8,128)(2,1)} %get-tuple-element.28), channel_id=1, source_target_pairs={{0,1},{1,0},{2,3},{3,2},{4,5},{5,4},{6,7},{7,6},{8,9},{9,8},{10,11... | collective-permute-start | bytes 3145736 | tf_op jit(solution)/shard_map/ppermute | solution.py:267
  49.8 2.4 %collective-permute-start.3 = (bf16[4,512,128]{2,1,0:T(8,128)(2,1)}, bf16[4,512,128]{2,1,0:T(8,128)(2,1)S(1)}, u32[]{:S(2)}, u32[]{:S(2)}) collective-permute-start(bf16[4,512,128]{2,1,0:T(8,128)(2,1)} %shard_map.103.near_ref), channel_id=1, source_target_pairs={{0,1},{1,0},{2,3},{3,2},{4,5},{5,4},{6,7},{7,6},{8,9},{9,8},{10,11... | collective-permute-start | bytes 1572872 | tf_op jit(solution)/shard_map/ppermute | solution.py:257
  52.2 0.8 collective-permute-done.4.far_ref
  53.0 1.9 %collective-permute-start.5 = (bf16[4,512,128]{2,1,0:T(8,128)(2,1)}, bf16[4,512,128]{2,1,0:T(8,128)(2,1)}, u32[]{:S(2)}, u32[]{:S(2)}) collective-permute-start(bf16[4,512,128]{2,1,0:T(8,128)(2,1)} %collective-permute-done.4.far_ref), channel_id=1, source_target_pairs={{0,1},{1,0},{2,3},{3,2},{4,5},{5,4},{6,7},{7,6},{8,9},{9,8},{10,11... | collective-permute-start | bytes 1572872 | tf_op jit(solution)/shard_map/ppermute | solution.py:258
  54.9 0.0 copy-done.16
  54.9 0.0 copy-done.17
  54.9 0.1 select_reduce_fusion
  55.1 0.1 sub.12
  55.1 0.1 select_reduce_fusion.1.pick_ref
  55.3 0.0 collective-permute-done.3.near_other_ref
  55.3 1.9 %collective-permute-done.5.far_other_ref = bf16[4,512,128]{2,1,0:T(8,128)(2,1)} collective-permute-done((bf16[4,512,128]{2,1,0:T(8,128)(2,1)}, bf16[4,512,128]{2,1,0:T(8,128)(2,1)}, u32[]{:S(2)}, u32[]{:S(2)}) %collective-permute-start.5) | collective-permute-done | bytes 524320 | tf_op jit(solution)/shard_map/ppermute | solution.py:258
  57.1 0.0 collective-permute-done.6.came_ref
  57.1 0.0 all-to-all-done.rows_ref
  57.1 0.0 copy-done.10
  57.1 0.0 copy-start.7
  57.2 1.2 copy-done.7
  58.3 1.8 %shard_map.105 = bf16[1024,128]{1,0:T(8,128)(2,1)S(1)} custom-call(s32[32]{0:T(128)S(1)} %select_reduce_fusion.1.pick_ref, bf16[32,32,640]{2,1,0:T(8,128)(2,1)S(1)} %all-to-all-done.rows_ref, bf16[3,64,512]{2,1,0:T(8,128)(2,1)S(1)} %copy-done.7, bf16[3,64,128]{2,1,0:T(8,128)(2,1)S(1)} %copy-done.10), custom_call_target="tpu_custom_call" | custom-call | flops 251658240 | bytes 1310720 | tf_op jit(solution)/shard_map/pallas_call | solution.py:273
  60.1 2.2 %all-gather = bf16[2048,128]{1,0:T(8,128)(2,1)S(1)} all-gather(bf16[1024,128]{1,0:T(8,128)(2,1)S(1)} %shard_map.105), channel_id=2, replica_groups={{0,1},{2,3},{4,5},{6,7},{8,9},{10,11},{12,13},{14,15},{16,17},{18,19},{..., dimensions={0}, use_global_device_ids=true | all-gather | bytes 786432 | tf_op jit(solution)/shard_map/all_gather | solution.py:280
  62.3 0.0 copy-done.5
  62.3 15.4 %all_to_all.20.parts_ref = bf16[8,64,128]{2,1,0:T(8,128)(2,1)S(1)} all-to-all(bf16[8,64,128]{2,1,0:T(8,128)(2,1)S(1)} %bitcast.12), channel_id=1, replica_groups={{0,2,4,6,8,10,12,14},{1,3,5,7,9,11,13,15},{16,18,20,22,24,26,28,30},{17..., dimensions={0} | all-to-all | bytes 262144 | tf_op jit(solution)/shard_map/all_to_all | solution.py:192
  77.8 11.5 %all_to_all.21 = bf16[8,64,128]{2,1,0:T(8,128)(2,1)S(1)} all-to-all(bf16[8,64,128]{2,1,0:T(8,128)(2,1)S(1)} %shard_map.106), channel_id=1, replica_groups={{0,2,4,6,8,10,12,14},{1,3,5,7,9,11,13,15},{16,18,20,22,24,26,28,30},{17..., dimensions={0} | all-to-all | bytes 262144 | tf_op jit(solution)/shard_map/all_to_all | solution.py:192
  89.2 2.0 %all_gather.11 = bf16[2,512,128]{2,1,0:T(8,128)(2,1)S(1)} all-gather(bf16[1,512,128]{2,1,0:T(8,128)(2,1)S(1)} %bitcast.11), channel_id=1, replica_groups={{0,1},{2,3},{4,5},{6,7},{8,9},{10,11},{12,13},{14,15},{16,17},{18,19},{..., dimensions={0}, use_global_device_ids=true | all-gather | bytes 393216 | tf_op jit(solution)/shard_map/all_gather | solution.py:290
  91.2 2.4 %shard_map.107 = bf16[32,32,640]{2,1,0:T(8,128)(2,1)} custom-call(s32[32]{0:T(128)S(1)} %select_reduce_fusion.1.pick_ref, bf16[1024,128]{1,0:T(8,128)(2,1)S(1)} %bitcast.8, bf16[3,64,512]{2,1,0:T(8,128)(2,1)S(1)} %copy-done.7, bf16[3,64,128]{2,1,0:T(8,128)(2,1)S(1)} %copy-done.10), custom_call_target="tpu_custom_call" | custom-call | flops 251658240 | bytes 1310720 | tf_op jit(solution)/shard_map/pallas_call | solution.py:293
  93.7 10.0 %all-to-all-start.3 = ((bf16[32,32,640]{2,1,0:T(8,128)(2,1)}), bf16[32,32,640]{2,1,0:T(8,128)(2,1)}, u32[]{:S(2)}, u32[]{:S(2)}) async-start(bf16[32,32,640]{2,1,0:T(8,128)(2,1)} %shard_map.107), calls=%async_computation.3 | async-start | bytes 2621440 | tf_op jit(solution)/shard_map/all_to_all | solution.py:192
  103.6 0.0 copy-done.4
  103.6 0.0 copy-start.6
  103.7 1.2 copy-done.6
  104.9 0.2 shard_map.108
  105.1 2.5 %collective-permute-start.7 = (bf16[4,512,128]{2,1,0:T(8,128)(2,1)S(1)}, bf16[4,512,128]{2,1,0:T(8,128)(2,1)S(1)}, u32[]{:S(2)}, u32[]{:S(2)}) collective-permute-start(bf16[4,512,128]{2,1,0:T(8,128)(2,1)S(1)} %get-tuple-element.33), channel_id=1, source_target_pairs={{0,2},{1,3},{2,0},{3,1},{4,6},{5,7},{6,4},{7,5},{8,10},{9,11},{10,... | collective-permute-start | bytes 1572872 | tf_op jit(solution)/shard_map/ppermute | solution.py:309
  107.6 0.1 convert_reduce_fusion
  107.7 12.7 %collective-permute-done.7.came_ref = bf16[4,512,128]{2,1,0:T(8,128)(2,1)S(1)} collective-permute-done((bf16[4,512,128]{2,1,0:T(8,128)(2,1)S(1)}, bf16[4,512,128]{2,1,0:T(8,128)(2,1)S(1)}, u32[]{:S(2)}, u32[]{:S(2)}) %collective-permute-start.7) | collective-permute-done | bytes 524320 | tf_op jit(solution)/shard_map/ppermute | solution.py:309
  120.4 0.1 shard_map.110
  120.6 0.0 copy-start.11
  120.6 0.6 copy-done.11
  121.2 1.9 %collective-permute-start.8 = (bf16[512,128]{1,0:T(8,128)(2,1)S(1)}, bf16[512,128]{1,0:T(8,128)(2,1)S(1)}, u32[]{:S(2)}, u32[]{:S(2)}) collective-permute-start(bf16[512,128]{1,0:T(8,128)(2,1)S(1)} %get-tuple-element.39), channel_id=1, source_target_pairs={{0,4},{1,5},{2,6},{3,7},{4,8},{5,9},{6,10},{7,11},{8,12},{9,13},{1... | collective-permute-start | bytes 393224 | tf_op jit(solution)/shard_map/ppermute | solution.py:225
  123.2 6.0 %collective-permute-start.9 = (bf16[512,128]{1,0:T(8,128)(2,1)S(1)}, bf16[512,128]{1,0:T(8,128)(2,1)S(1)}, u32[]{:S(2)}, u32[]{:S(2)}) collective-permute-start(bf16[512,128]{1,0:T(8,128)(2,1)S(1)} %get-tuple-element.40), channel_id=1, source_target_pairs={{0,12},{1,13},{2,14},{3,15},{4,0},{5,1},{6,2},{7,3},{8,4},{9,5},{1... | collective-permute-start | bytes 393224 | tf_op jit(solution)/shard_map/ppermute | solution.py:225
  129.2 2.5 %collective-permute-start.10 = (bf16[512,128]{1,0:T(8,128)(2,1)S(1)}, bf16[512,128]{1,0:T(8,128)(2,1)S(1)}, u32[]{:S(2)}, u32[]{:S(2)}) collective-permute-start(bf16[512,128]{1,0:T(8,128)(2,1)S(1)} %get-tuple-element.41), channel_id=1, source_target_pairs={{0,8},{1,9},{2,10},{3,11},{4,12},{5,13},{6,14},{7,15},{8,0},{9,1},... | collective-permute-start | bytes 393224 | tf_op jit(solution)/shard_map/ppermute | solution.py:225
  131.7 2.4 %shard_map.112 = (f32[3,64,512]{2,1,0:T(8,128)}, f32[3,64,128]{2,1,0:T(8,128)}) custom-call(s32[32]{0:T(128)S(1)} %select_reduce_fusion.1.pick_ref, f32[3]{0:T(128)S(1)} %maximum_divide_fusion.scale_ref, bf16[1024,128]{1,0:T(8,128)(2,1)S(1)} %bitcast.9, bf16[32,32,640]{2,1,0:T(8,128)(2,1)S(1)} %all-to-all-done.rows_ref), custom_call_target="tpu_custom_call" | custom-call | flops 251658240 | bytes 1310720 | tf_op jit(solution)/shard_map/pallas_call | solution.py:326
  134.0 2.7 %shard_map.109.base_ref = f32[512,512]{1,0:T(8,128)S(1)} custom-call(s32[4]{0:T(128)S(1)} %copy-done.12, bf16[4,512,128]{2,1,0:T(8,128)(2,1)} %shard_map.103.near_ref, bf16[4,512,128]{2,1,0:T(8,128)(2,1)S(1)} %collective-permute-done.3.near_other_ref, bf16[4,512,128]{2,1,0:T(8,128)(2,1)} %collective-permute-done.4.far_ref, ...), custom_call_target="tpu_custom_call" | custom-call | flops 1073741824 | bytes 4194304 | tf_op jit(solution)/shard_map/pallas_call | solution.py:310
  136.7 1.0 copy-done
  137.7 0.0 collective-permute-done.8.refs_1_
  137.7 1.4 collective-permute-done.9.refs_2_
  139.0 2.1 %collective-permute-done.10.refs_3_ = bf16[512,128]{1,0:T(8,128)(2,1)S(1)} collective-permute-done((bf16[512,128]{1,0:T(8,128)(2,1)S(1)}, bf16[512,128]{1,0:T(8,128)(2,1)S(1)}, u32[]{:S(2)}, u32[]{:S(2)}) %collective-permute-start.10) | collective-permute-done | bytes 131104 | tf_op jit(solution)/shard_map/ppermute | solution.py:225
  141.1 0.0 all-to-all-done.3.came_ref
  141.2 0.6 copy-done.15
  141.8 2.8 %shard_map.111 = (bf16[512,512]{1,0:T(8,128)(2,1)}, bf16[512,128]{1,0:T(8,128)(2,1)}) custom-call(s32[4]{0:T(128)} %pad_add_fusion.place_ref, s32[512]{0:T(512)} %index_ref.3, s32[96]{0:T(128)} %storage_ref.3, f32[512,512]{1,0:T(8,128)} %copy-done, bf16[32,32,640]{2,1,0:T(8,128)(2,1)} %all-to-all-done.3.came_ref, bf16[512,128]{1,0:T(8,128)(2,1)} %copy-done.11, ...), custom_call_target="tpu_custom_call" | custom-call | bytes 2883584 | tf_op jit(solution)/shard_map/pallas_call | solution.py:334
  (21 shorter events, 0.1 us)
Async XLA Ops:
  3.6 13.6 %copy-start.9 = (bf16[512,128]{1,0:T(8,128)(2,1)S(1)}, bf16[512,128]{1,0:T(8,128)(2,1)}, u32[]{:S(2)}) copy-start(bf16[512,128]{1,0:T(8,128)(2,1)} %refs_0_) | copy-start | bytes 393220
  3.6 37.1 %copy-start.1 = (bf16[512,2048]{1,0:T(8,128)(2,1)S(1)}, bf16[512,2048]{1,0:T(8,128)(2,1)}, u32[]{:S(2)}) copy-start(bf16[512,2048]{1,0:T(8,128)(2,1)} %weight_ref.3) | copy-start | bytes 6291460
  3.6 37.1 %copy-start.12 = (s32[4]{0:T(128)S(1)}, s32[4]{0:T(128)}, u32[]{:S(2)}) copy-start(s32[4]{0:T(128)} %pad_add_fusion.place_ref) | copy-start | bytes 52
  3.6 53.5 %all-to-all-start = ((bf16[32,32,640]{2,1,0:T(8,128)(2,1)}), bf16[32,32,640]{2,1,0:T(8,128)(2,1)S(1)}, u32[]{:S(2)}, u32[]{:S(2)}) async-start(bf16[32,32,640]{2,1,0:T(8,128)(2,1)} %shard_map.102), calls=%async_computation | async-start | bytes 2621440 | tf_op jit(solution)/shard_map/all_to_all | solution.py:192
  17.2 15.7 %collective-permute-start.2 = (bf16[512,128]{1,0:T(8,128)(2,1)S(1)}, bf16[512,128]{1,0:T(8,128)(2,1)S(1)}, u32[]{:S(2)}, u32[]{:S(2)}) collective-permute-start(bf16[512,128]{1,0:T(8,128)(2,1)S(1)} %copy-done.9), channel_id=1, source_target_pairs={{0,8},{1,9},{2,10},{3,11},{4,12},{5,13},{6,14},{7,15},{8,0},{9,1},... | collective-permute-start | bytes 393224 | tf_op jit(solution)/shard_map/ppermute | solution.py:225
  24.9 10.9 %collective-permute-start.1 = (bf16[512,128]{1,0:T(8,128)(2,1)S(1)}, bf16[512,128]{1,0:T(8,128)(2,1)S(1)}, u32[]{:S(2)}, u32[]{:S(2)}) collective-permute-start(bf16[512,128]{1,0:T(8,128)(2,1)S(1)} %copy-done.9), channel_id=1, source_target_pairs={{0,4},{1,5},{2,6},{3,7},{4,8},{5,9},{6,10},{7,11},{8,12},{9,13},{1... | collective-permute-start | bytes 393224 | tf_op jit(solution)/shard_map/ppermute | solution.py:225
  27.7 9.8 %collective-permute-start = (bf16[512,128]{1,0:T(8,128)(2,1)S(1)}, bf16[512,128]{1,0:T(8,128)(2,1)S(1)}, u32[]{:S(2)}, u32[]{:S(2)}) collective-permute-start(bf16[512,128]{1,0:T(8,128)(2,1)S(1)} %copy-done.9), channel_id=1, source_target_pairs={{0,12},{1,13},{2,14},{3,15},{4,0},{5,1},{6,2},{7,3},{8,4},{9,5},{1... | collective-permute-start | bytes 393224 | tf_op jit(solution)/shard_map/ppermute | solution.py:225
  38.3 14.7 %collective-permute-start.4 = (bf16[4,512,128]{2,1,0:T(8,128)(2,1)}, bf16[4,512,128]{2,1,0:T(8,128)(2,1)}, u32[]{:S(2)}, u32[]{:S(2)}) collective-permute-start(bf16[4,512,128]{2,1,0:T(8,128)(2,1)} %shard_map.103.near_ref), channel_id=1, source_target_pairs={{0,2},{1,3},{2,0},{3,1},{4,6},{5,7},{6,4},{7,5},{8,10},{9,11},{10,... | collective-permute-start | bytes 1572872 | tf_op jit(solution)/shard_map/ppermute | solution.py:256
  40.7 1.0 copy-start.8
  41.8 13.2 %copy-start.16 = (s32[512]{0:T(512)S(1)}, s32[512]{0:T(512)}, u32[]{:S(2)}) copy-start(s32[512]{0:T(512)} %index_ref.3) | copy-start | bytes 6148
  41.8 13.2 %copy-start.17 = (s32[96]{0:T(128)S(1)}, s32[96]{0:T(128)}, u32[]{:S(2)}) copy-start(s32[96]{0:T(128)} %storage_ref.3) | copy-start | bytes 1156
  41.8 15.4 %copy-start.10 = (bf16[3,64,128]{2,1,0:T(8,128)(2,1)S(1)}, bf16[3,64,128]{2,1,0:T(8,128)(2,1)}, u32[]{:S(2)}) copy-start(bf16[3,64,128]{2,1,0:T(8,128)(2,1)} %up_ref.3) | copy-start | bytes 147460
  46.9 1.0 copy-start.3
  47.9 9.3 %collective-permute-start.6 = (bf16[8,512,128]{2,1,0:T(8,128)(2,1)}, bf16[8,512,128]{2,1,0:T(8,128)(2,1)S(1)}, u32[]{:S(2)}, u32[]{:S(2)}) collective-permute-start(bf16[8,512,128]{2,1,0:T(8,128)(2,1)} %get-tuple-element.28), channel_id=1, source_target_pairs={{0,1},{1,0},{2,3},{3,2},{4,5},{5,4},{6,7},{7,6},{8,9},{9,8},{10,11... | collective-permute-start | bytes 3145736 | tf_op jit(solution)/shard_map/ppermute | solution.py:267
  49.8 5.5 %collective-permute-start.3 = (bf16[4,512,128]{2,1,0:T(8,128)(2,1)}, bf16[4,512,128]{2,1,0:T(8,128)(2,1)S(1)}, u32[]{:S(2)}, u32[]{:S(2)}) collective-permute-start(bf16[4,512,128]{2,1,0:T(8,128)(2,1)} %shard_map.103.near_ref), channel_id=1, source_target_pairs={{0,1},{1,0},{2,3},{3,2},{4,5},{5,4},{6,7},{7,6},{8,9},{9,8},{10,11... | collective-permute-start | bytes 1572872 | tf_op jit(solution)/shard_map/ppermute | solution.py:257
  53.0 4.1 %collective-permute-start.5 = (bf16[4,512,128]{2,1,0:T(8,128)(2,1)}, bf16[4,512,128]{2,1,0:T(8,128)(2,1)}, u32[]{:S(2)}, u32[]{:S(2)}) collective-permute-start(bf16[4,512,128]{2,1,0:T(8,128)(2,1)} %collective-permute-done.4.far_ref), channel_id=1, source_target_pairs={{0,1},{1,0},{2,3},{3,2},{4,5},{5,4},{6,7},{7,6},{8,9},{9,8},{10,11... | collective-permute-start | bytes 1572872 | tf_op jit(solution)/shard_map/ppermute | solution.py:258
  57.1 5.2 %copy-start.5 = (bf16[8,512,128]{2,1,0:T(8,128)(2,1)}, bf16[8,512,128]{2,1,0:T(8,128)(2,1)S(1)}, u32[]{:S(2)}) copy-start(bf16[8,512,128]{2,1,0:T(8,128)(2,1)S(1)} %collective-permute-done.6.came_ref) | copy-start | bytes 3145732
  57.1 1.2 copy-start.7
  93.7 10.0 %copy-start.4 = (bf16[8,512,128]{2,1,0:T(8,128)(2,1)S(1)}, bf16[8,512,128]{2,1,0:T(8,128)(2,1)}, u32[]{:S(2)}) copy-start(bf16[8,512,128]{2,1,0:T(8,128)(2,1)} %copy-done.3) | copy-start | bytes 3145732
  93.7 47.5 %all-to-all-start.3 = ((bf16[32,32,640]{2,1,0:T(8,128)(2,1)}), bf16[32,32,640]{2,1,0:T(8,128)(2,1)}, u32[]{:S(2)}, u32[]{:S(2)}) async-start(bf16[32,32,640]{2,1,0:T(8,128)(2,1)} %shard_map.107), calls=%async_computation.3 | async-start | bytes 2621440 | tf_op jit(solution)/shard_map/all_to_all | solution.py:192
  103.6 1.2 copy-start.6
  105.1 15.3 %collective-permute-start.7 = (bf16[4,512,128]{2,1,0:T(8,128)(2,1)S(1)}, bf16[4,512,128]{2,1,0:T(8,128)(2,1)S(1)}, u32[]{:S(2)}, u32[]{:S(2)}) collective-permute-start(bf16[4,512,128]{2,1,0:T(8,128)(2,1)S(1)} %get-tuple-element.33), channel_id=1, source_target_pairs={{0,2},{1,3},{2,0},{3,1},{4,6},{5,7},{6,4},{7,5},{8,10},{9,11},{10,... | collective-permute-start | bytes 1572872 | tf_op jit(solution)/shard_map/ppermute | solution.py:309
  120.4 13.6 %copy-start.2 = (bf16[512,2048]{1,0:T(8,128)(2,1)S(1)}, bf16[512,2048]{1,0:T(8,128)(2,1)}, u32[]{:S(2)}) copy-start(bf16[512,2048]{1,0:T(8,128)(2,1)} %weight_ref.3) | copy-start | bytes 6291460
  120.6 0.7 copy-start.11
  121.2 16.5 %collective-permute-start.8 = (bf16[512,128]{1,0:T(8,128)(2,1)S(1)}, bf16[512,128]{1,0:T(8,128)(2,1)S(1)}, u32[]{:S(2)}, u32[]{:S(2)}) collective-permute-start(bf16[512,128]{1,0:T(8,128)(2,1)S(1)} %get-tuple-element.39), channel_id=1, source_target_pairs={{0,4},{1,5},{2,6},{3,7},{4,8},{5,9},{6,10},{7,11},{8,12},{9,13},{1... | collective-permute-start | bytes 393224 | tf_op jit(solution)/shard_map/ppermute | solution.py:225
  123.2 15.9 %collective-permute-start.9 = (bf16[512,128]{1,0:T(8,128)(2,1)S(1)}, bf16[512,128]{1,0:T(8,128)(2,1)S(1)}, u32[]{:S(2)}, u32[]{:S(2)}) collective-permute-start(bf16[512,128]{1,0:T(8,128)(2,1)S(1)} %get-tuple-element.40), channel_id=1, source_target_pairs={{0,12},{1,13},{2,14},{3,15},{4,0},{5,1},{6,2},{7,3},{8,4},{9,5},{1... | collective-permute-start | bytes 393224 | tf_op jit(solution)/shard_map/ppermute | solution.py:225
  129.2 12.0 %collective-permute-start.10 = (bf16[512,128]{1,0:T(8,128)(2,1)S(1)}, bf16[512,128]{1,0:T(8,128)(2,1)S(1)}, u32[]{:S(2)}, u32[]{:S(2)}) collective-permute-start(bf16[512,128]{1,0:T(8,128)(2,1)S(1)} %get-tuple-element.41), channel_id=1, source_target_pairs={{0,8},{1,9},{2,10},{3,11},{4,12},{5,13},{6,14},{7,15},{8,0},{9,1},... | collective-permute-start | bytes 393224 | tf_op jit(solution)/shard_map/ppermute | solution.py:225
  136.7 1.0 copy-start
  137.7 3.5 %copy-start.13 = (bf16[512,128]{1,0:T(8,128)(2,1)}, bf16[512,128]{1,0:T(8,128)(2,1)S(1)}, u32[]{:S(2)}) copy-start(bf16[512,128]{1,0:T(8,128)(2,1)S(1)} %collective-permute-done.8.refs_1_) | copy-start | bytes 393220
  139.0 2.1 %copy-start.14 = (bf16[512,128]{1,0:T(8,128)(2,1)}, bf16[512,128]{1,0:T(8,128)(2,1)S(1)}, u32[]{:S(2)}) copy-start(bf16[512,128]{1,0:T(8,128)(2,1)S(1)} %collective-permute-done.9.refs_2_) | copy-start | bytes 393220
  141.1 0.7 copy-start.15

commit v6 on v5

--- a/solution.py
+++ b/solution.py
@@ -71,22 +71,21 @@
             send_ref[b] = low
 
 
-def pair_body(own_ref, came_ref, keep_ref, give_ref):
-    half = keep_ref.shape[0]
-    for b in range(half):
-        keep_ref[b] = (own_ref[b].astype(f32) + came_ref[b].astype(f32)).astype(bf16)
-        other = own_ref[half + b].astype(f32) + came_ref[half + b].astype(f32)
-        give_ref[b] = other.astype(bf16)
-
-
-def neighbour_body(keep_ref, came_ref, *out_refs):
-    for b, out_ref in enumerate(out_refs):
-        out_ref[...] = (keep_ref[b].astype(f32) + came_ref[b].astype(f32)).astype(bf16)
-
-
-def pack_body(*refs):
-    for b, ref in enumerate(refs[:-1]):
-        refs[-1][b] = ref[...]
+def pair_body(own_ref, came_ref, *out_refs):
+    count = len(out_refs)
+    for k, out_ref in enumerate(out_refs):
+        for b in range(2):
+            at = k + b * count
+            out_ref[b] = (own_ref[at].astype(f32) + came_ref[at].astype(f32)).astype(bf16)
+
+
+def meet_body(*refs):
+    part_refs, (mine_ref, other_ref) = refs[:-2], refs[-2:]
+    for b, out_ref in enumerate((mine_ref, other_ref)):
+        total = part_refs[0][b].astype(f32)
+        for part_ref in part_refs[1:]:
+            total = total + part_ref[b].astype(f32)
+        out_ref[...] = total.astype(bf16)
 
 
 def rank_body(pick_ref, rows_ref, down_ref, up_ref, out_ref):
@@ -168,7 +167,9 @@
         low = jnp.where(first_core, own, other)
         high = jnp.where(first_core, other, own)
         pair = jnp.concatenate([low, high], axis=1)
-        columns = chip_columns(place_ref, k, 2 * blocks, 2 * width)
+        odd = lax.rem(place_ref[2] + k // blocks, 2)
+        chip = 2 * (k % blocks) + odd
+        columns = pl.ds(pl.multiple_of(chip * 2 * width, 2 * width), 2 * width)
         part = lax.dot_general(pair, weight_ref[:, columns], dims, preferred_element_type=f32)
         out_ref[...] = part if k == 0 else out_ref[...] + part
 
@@ -245,14 +246,8 @@
     swap = [(t, t ^ 1) for t in range(tensor_count)]
     across = [(t, t ^ 2) for t in range(tensor_count)]
     quarter = chips // 2
-    cot = after(cotangent, spread)
-    opposite = moved_along(cot, quarter)
-    near = local_call(
-        pack_body,
-        shape(quarter, rows, out_block),
-        [VMEM] * quarter,
-        moved=4 * quarter * rows * out_block,
-    )(cot, moved_along(cot, -2), moved_along(cot, 2), opposite)
+    alternate = [list(range(p, tensor_count, 4)) for p in range(4)]
+    near = lax.all_gather(after(cotangent, spread), "tensor", axis_index_groups=alternate)
     far = lax.ppermute(near, "tensor", across)
     near_other = lax.ppermute(near, "tensor", swap)
     far_other = lax.ppermute(far, "tensor", swap)
@@ -300,29 +295,21 @@
     )(pick, ranks, down, up)
     returned = exchange(contributions, "dp")
 
-    keep, give = local_call(
+    paired = local_call(
         pair_body,
-        (shape(quarter, rows, out_block),) * 2,
+        (shape(2, rows, out_block),) * quarter,
         [VMEM, VMEM],
         moved=6 * chips * rows * out_block,
     )(after(own, contributions), came)
-    crossed = lax.ppermute(give, "tensor", across)
+    sums = [paired[0], moved_along(paired[3], quarter)]
+    sums += [moved_along(paired[1], 2), moved_along(paired[2], -2)]
     base = local_call(
         base_body,
         shape(rows, block, dtype=f32),
         [SMEM, VMEM, VMEM, VMEM, VMEM, VMEM],
         flops=2 * rows * block * tensor_count * out_block,
         moved=2 * (2 * rows * tensor_count * out_block),
-    )(after(place, give), near, near_other, far, far_other, weight)
-    summed = local_call(
-        neighbour_body,
-        (shape(rows, out_block),) * quarter,
-        [VMEM, VMEM],
-        moved=6 * quarter * rows * out_block,
-    )(keep, crossed)
-    opposite = moved_along(summed[3], quarter)
-    parts = [summed[0], moved_along(summed[1], 2), moved_along(summed[2], -2), opposite]
-
+    )(after(place, paired[0]), near, near_other, far, far_other, weight)
     grad_down, grad_up = local_call(
         gradient_body,
         (shape(held, rank, block, dtype=f32), shape(held, rank, out_block, dtype=f32)),
@@ -331,12 +318,20 @@
         flops=2 * slots * length * width * held * rank,
         moved=2 * slots * length * width,
     )(pick, scale, ranks, arrived)
+    sums, base, grad_down, grad_up = lax.optimization_barrier((sums, base, grad_down, grad_up))
+    mine_sum, other_sum = local_call(
+        meet_body,
+        (shape(rows, out_block),) * 2,
+        [VMEM] * quarter,
+        moved=2 * 10 * rows * out_block,
+    )(*sums)
+    parts = [mine_sum, lax.ppermute(other_sum, "tensor", across)]
+
     token_gradient, key_value_output = local_call(
         functools.partial(final_body, held),
         (shape(rows, block), shape(rows, out_block)),
-        [SMEM, SMEM, SMEM, VMEM, VMEM] + [VMEM] * quarter,
+        [SMEM, SMEM, SMEM, VMEM, VMEM, VMEM, VMEM],
         moved=2 * (3 * rows * block + slots * length * width),
-        limit=HBM_LIMIT,
     )(place, sequence_index, storage_row, base, returned, *parts)
     return (key_value_output, token_gradient, grad_down, grad_up)
 

time: 145 us -> 143 us (0.986)
  the two profiles are of different devices: /device:TPU:4 before, /device:TPU:1 now
where the time goes in v6:
time: 143 us; the launch traced here: 142 us
  starting transfers between devices  47.7 us (33%)
  blocking collectives  47.3 us (33%)
  waiting for transfers between devices  18.1 us (13%)
  Pallas kernels  17.4 us (12%)
  local copies, waits for them, and re-layouts  9.78 us (7%)
    all_to_all x2, starting transfers between devices, exchange(): lax.all_to_all(value, axis, split_axis=0, concat_axis=0, axis_index_group...  23.3 us
    all_to_all x2, blocking collectives, exchange(): lax.all_to_all(value, axis, split_axis=0, concat_axis=0, axis_index_group...  23.2 us
    all_gather x1, blocking collectives, on_device(): lax.all_gather(after(cotangent, spread), 'tensor', axis_index_groups=alte...  17 us
    ppermute x3, waiting for transfers between devices, moved_along(): return lax.ppermute(value, 'tensor', perm)  13.2 us
    ppermute x3, starting transfers between devices, moved_along(): return lax.ppermute(value, 'tensor', perm)  9.72 us
    unnamed x36, local copies, waits for them, and re-layouts  9.71 us
    ppermute x1, starting transfers between devices, on_device(): came = lax.ppermute(send, 'tensor', swap)  5.5 us
    pallas_call x1, Pallas kernels, on_device(): local_call(projection_body, (shape(chips, rows, out_block), shape(chips,...  5.13 us
  transfers between devices with their start and end apart: 10, of which 5 were waited for; matrix products, arithmetic and copies ran while one was open for 0% of the time, Pallas kernels for 7%

profile of v6, /device:TPU:1, one launch (start us, length us, event | category | flops | bytes accessed | tf_op | source)
XLA Modules:
  0.0 142.2 jit_solution(2961880459129327265)
XLA Ops:
  0.6 0.6 pad_add_fusion.place_ref
  1.3 2.3 %shard_map.102 = bf16[32,32,640]{2,1,0:T(8,128)(2,1)} custom-call(s32[4]{0:T(128)} %pad_add_fusion.place_ref, s32[512]{0:T(512)} %index_ref.3, s32[96]{0:T(128)} %storage_ref.3, bf16[512,512]{1,0:T(8,128)(2,1)} %tokens_ref.3, bf16[512,128]{1,0:T(8,128)(2,1)} %cot_ref.1), custom_call_target="tpu_custom_call" | custom-call | bytes 1966080 | tf_op jit(solution)/shard_map/pallas_call | solution.py:228
  3.6 0.0 copy-start.3
  3.6 13.8 %all-to-all-start = ((bf16[32,32,640]{2,1,0:T(8,128)(2,1)}), bf16[32,32,640]{2,1,0:T(8,128)(2,1)S(1)}, u32[]{:S(2)}, u32[]{:S(2)}) async-start(bf16[32,32,640]{2,1,0:T(8,128)(2,1)} %shard_map.102), calls=%async_computation | async-start | bytes 2621440 | tf_op jit(solution)/shard_map/all_to_all | solution.py:193
  17.4 17.0 %all-gather = bf16[2048,128]{1,0:T(8,128)(2,1)} all-gather(bf16[512,128]{1,0:T(8,128)(2,1)} %cot_ref.1), channel_id=2, replica_groups={{0,4,8,12},{1,5,9,13},{2,6,10,14},{3,7,11,15},{16,20,24,28},{17,21,25,2..., dimensions={0}, use_global_device_ids=true | all-gather | bytes 655360 | tf_op jit(solution)/shard_map/all_gather | solution.py:250
  34.4 1.9 %collective-permute-start.1 = (bf16[4,512,128]{2,1,0:T(8,128)(2,1)}, bf16[4,512,128]{2,1,0:T(8,128)(2,1)}, u32[]{:S(2)}, u32[]{:S(2)}) collective-permute-start(bf16[4,512,128]{2,1,0:T(8,128)(2,1)} %bitcast.4.near_ref), channel_id=1, source_target_pairs={{0,2},{1,3},{2,0},{3,1},{4,6},{5,7},{6,4},{7,5},{8,10},{9,11},{10,... | collective-permute-start | bytes 1572872 | tf_op jit(solution)/shard_map/ppermute | solution.py:251
  36.3 0.0 copy-done.3
  36.3 0.0 copy-done.16
  36.3 0.0 copy-start.11
  36.3 1.0 copy-done.11
  37.4 5.1 %shard_map.103 = (bf16[8,512,128]{2,1,0:T(8,128)(2,1)S(1)}, bf16[8,512,128]{2,1,0:T(8,128)(2,1)}) custom-call(s32[4]{0:T(128)S(1)} %copy-done.16, bf16[512,512]{1,0:T(8,128)(2,1)S(1)} %copy-done.11, bf16[512,2048]{1,0:T(8,128)(2,1)S(1)} %copy-done.3), custom_call_target="tpu_custom_call" | custom-call | flops 1073741824 | bytes 4718592 | tf_op jit(solution)/shard_map/pallas_call | solution.py:255
  42.5 1.0 copy-done.5
  43.5 5.5 %collective-permute-start.3 = (bf16[8,512,128]{2,1,0:T(8,128)(2,1)}, bf16[8,512,128]{2,1,0:T(8,128)(2,1)S(1)}, u32[]{:S(2)}, u32[]{:S(2)}) collective-permute-start(bf16[8,512,128]{2,1,0:T(8,128)(2,1)} %get-tuple-element.35), channel_id=1, source_target_pairs={{0,1},{1,0},{2,3},{3,2},{4,5},{5,4},{6,7},{7,6},{8,9},{9,8},{10,11... | collective-permute-start | bytes 3145736 | tf_op jit(solution)/shard_map/ppermute | solution.py:262
  49.0 1.9 %collective-permute-start = (bf16[4,512,128]{2,1,0:T(8,128)(2,1)}, bf16[4,512,128]{2,1,0:T(8,128)(2,1)S(1)}, u32[]{:S(2)}, u32[]{:S(2)}) collective-permute-start(bf16[4,512,128]{2,1,0:T(8,128)(2,1)} %bitcast.4.near_ref), channel_id=1, source_target_pairs={{0,1},{1,0},{2,3},{3,2},{4,5},{5,4},{6,7},{7,6},{8,9},{9,8},{10,11... | collective-permute-start | bytes 1572872 | tf_op jit(solution)/shard_map/ppermute | solution.py:252
  50.9 0.0 collective-permute-done.1.far_ref
  50.9 2.4 %collective-permute-start.2 = (bf16[4,512,128]{2,1,0:T(8,128)(2,1)}, bf16[4,512,128]{2,1,0:T(8,128)(2,1)S(1)}, u32[]{:S(2)}, u32[]{:S(2)}) collective-permute-start(bf16[4,512,128]{2,1,0:T(8,128)(2,1)} %collective-permute-done.1.far_ref), channel_id=1, source_target_pairs={{0,1},{1,0},{2,3},{3,2},{4,5},{5,4},{6,7},{7,6},{8,9},{9,8},{10,11... | collective-permute-start | bytes 1572872 | tf_op jit(solution)/shard_map/ppermute | solution.py:253
  53.4 0.0 copy-done.15
  53.4 0.0 copy-done.17
  53.4 0.1 select_reduce_fusion
  53.5 0.1 sub.12
  53.6 0.1 select_reduce_fusion.1.pick_ref
  53.7 0.0 collective-permute-done.near_other_ref
  53.7 1.4 collective-permute-done.2.far_other_ref
  55.1 0.8 copy-done.12
  55.9 0.0 collective-permute-done.3.came_ref
  55.9 0.0 all-to-all-done.rows_ref
  55.9 0.0 copy-done.14
  55.9 0.0 copy-start.9
  55.9 1.2 copy-done.9
  57.1 1.8 %shard_map.104 = bf16[1024,128]{1,0:T(8,128)(2,1)S(1)} custom-call(s32[32]{0:T(128)S(1)} %select_reduce_fusion.1.pick_ref, bf16[32,32,640]{2,1,0:T(8,128)(2,1)S(1)} %all-to-all-done.rows_ref, bf16[3,64,512]{2,1,0:T(8,128)(2,1)S(1)} %copy-done.9, bf16[3,64,128]{2,1,0:T(8,128)(2,1)S(1)} %copy-done.14), custom_call_target="tpu_custom_call" | custom-call | flops 251658240 | bytes 1310720 | tf_op jit(solution)/shard_map/pallas_call | solution.py:268
  58.9 0.0 copy-start.10
  58.9 2.3 %all-gather.1 = bf16[2048,128]{1,0:T(8,128)(2,1)S(1)} all-gather(bf16[1024,128]{1,0:T(8,128)(2,1)S(1)} %shard_map.104), channel_id=3, replica_groups={{0,1},{2,3},{4,5},{6,7},{8,9},{10,11},{12,13},{14,15},{16,17},{18,19},{..., dimensions={0}, use_global_device_ids=true | all-gather | bytes 786432 | tf_op jit(solution)/shard_map/all_gather | solution.py:275
  61.2 0.0 copy-done.7
  61.2 12.8 %all_to_all.20.parts_ref = bf16[8,64,128]{2,1,0:T(8,128)(2,1)S(1)} all-to-all(bf16[8,64,128]{2,1,0:T(8,128)(2,1)S(1)} %bitcast.13), channel_id=1, replica_groups={{0,2,4,6,8,10,12,14},{1,3,5,7,9,11,13,15},{16,18,20,22,24,26,28,30},{17..., dimensions={0} | all-to-all | bytes 262144 | tf_op jit(solution)/shard_map/all_to_all | solution.py:193
  74.1 10.4 %all_to_all.21 = bf16[8,64,128]{2,1,0:T(8,128)(2,1)S(1)} all-to-all(bf16[8,64,128]{2,1,0:T(8,128)(2,1)S(1)} %shard_map.105), channel_id=1, replica_groups={{0,2,4,6,8,10,12,14},{1,3,5,7,9,11,13,15},{16,18,20,22,24,26,28,30},{17..., dimensions={0} | all-to-all | bytes 262144 | tf_op jit(solution)/shard_map/all_to_all | solution.py:193
  84.5 4.8 %all_gather.19 = bf16[2,512,128]{2,1,0:T(8,128)(2,1)S(1)} all-gather(bf16[1,512,128]{2,1,0:T(8,128)(2,1)S(1)} %bitcast.12), channel_id=1, replica_groups={{0,1},{2,3},{4,5},{6,7},{8,9},{10,11},{12,13},{14,15},{16,17},{18,19},{..., dimensions={0}, use_global_device_ids=true | all-gather | bytes 393216 | tf_op jit(solution)/shard_map/all_gather | solution.py:285
  89.3 0.0 copy-done.10
  89.3 1.4 shard_map.106
  90.7 0.0 copy-start
  90.7 1.1 copy-done
  91.7 9.4 %all-to-all-start.3 = ((bf16[32,32,640]{2,1,0:T(8,128)(2,1)}), bf16[32,32,640]{2,1,0:T(8,128)(2,1)S(1)}, u32[]{:S(2)}, u32[]{:S(2)}) async-start(bf16[32,32,640]{2,1,0:T(8,128)(2,1)} %copy-done), calls=%async_computation.3 | async-start | bytes 2621440 | tf_op jit(solution)/shard_map/all_to_all | solution.py:193
  101.2 0.1 convert_reduce_fusion
  101.3 1.2 copy-done.6
  102.5 1.2 copy-done.8
  103.7 0.2 shard_map.107
  104.0 0.0 copy-start.13
  104.0 2.3 %collective-permute-start.4 = (bf16[2,512,128]{2,1,0:T(8,128)(2,1)S(1)}, bf16[2,512,128]{2,1,0:T(8,128)(2,1)S(1)}, u32[]{:S(2)}, u32[]{:S(2)}) collective-permute-start(bf16[2,512,128]{2,1,0:T(8,128)(2,1)S(1)} %get-tuple-element.41), channel_id=1, source_target_pairs={{0,8},{1,9},{2,10},{3,11},{4,12},{5,13},{6,14},{7,15},{8,0},{9,1},... | collective-permute-start | bytes 786440 | tf_op jit(solution)/shard_map/ppermute | solution.py:226
  106.3 3.8 %collective-permute-start.5 = (bf16[2,512,128]{2,1,0:T(8,128)(2,1)S(1)}, bf16[2,512,128]{2,1,0:T(8,128)(2,1)S(1)}, u32[]{:S(2)}, u32[]{:S(2)}) collective-permute-start(bf16[2,512,128]{2,1,0:T(8,128)(2,1)S(1)} %get-tuple-element.42), channel_id=1, source_target_pairs={{0,4},{1,5},{2,6},{3,7},{4,8},{5,9},{6,10},{7,11},{8,12},{9,13},{1... | collective-permute-start | bytes 786440 | tf_op jit(solution)/shard_map/ppermute | solution.py:226
  110.2 3.6 %collective-permute-start.6 = (bf16[2,512,128]{2,1,0:T(8,128)(2,1)S(1)}, bf16[2,512,128]{2,1,0:T(8,128)(2,1)S(1)}, u32[]{:S(2)}, u32[]{:S(2)}) collective-permute-start(bf16[2,512,128]{2,1,0:T(8,128)(2,1)S(1)} %get-tuple-element.43), channel_id=1, source_target_pairs={{0,12},{1,13},{2,14},{3,15},{4,0},{5,1},{6,2},{7,3},{8,4},{9,5},{1... | collective-permute-start | bytes 786440 | tf_op jit(solution)/shard_map/ppermute | solution.py:226
  113.7 2.4 %shard_map.109 = (f32[3,64,512]{2,1,0:T(8,128)}, f32[3,64,128]{2,1,0:T(8,128)}) custom-call(s32[32]{0:T(128)S(1)} %select_reduce_fusion.1.pick_ref, f32[3]{0:T(128)S(1)} %maximum_divide_fusion.scale_ref, bf16[1024,128]{1,0:T(8,128)(2,1)S(1)} %bitcast.10, bf16[32,32,640]{2,1,0:T(8,128)(2,1)S(1)} %all-to-all-done.rows_ref), custom_call_target="tpu_custom_call" | custom-call | flops 251658240 | bytes 1310720 | tf_op jit(solution)/shard_map/pallas_call | solution.py:313
  116.1 0.0 copy-done.4
  116.1 0.0 copy-done.13
  116.1 2.5 %shard_map.108.base_ref = f32[512,512]{1,0:T(8,128)S(1)} custom-call(s32[4]{0:T(128)S(1)} %copy-done.16, bf16[4,512,128]{2,1,0:T(8,128)(2,1)} %bitcast.4.near_ref, bf16[4,512,128]{2,1,0:T(8,128)(2,1)S(1)} %collective-permute-done.near_other_ref, bf16[4,512,128]{2,1,0:T(8,128)(2,1)} %collective-permute-done.1.far_ref, bf16[4,512,128]{2,1,0:T(8,128)(2,1)S(1)} %copy-done.13, ...), custom_call_target="tpu_custom_call" | custom-call | flops 1073741824 | bytes 4194304 | tf_op jit(solution)/shard_map/pallas_call | solution.py:306
  118.6 0.0 copy-start.1
  118.6 1.0 copy-done.1
  119.6 0.3 collective-permute-done.4.refs_1_
  119.9 6.3 %collective-permute-done.5.refs_2_ = bf16[2,512,128]{2,1,0:T(8,128)(2,1)S(1)} collective-permute-done((bf16[2,512,128]{2,1,0:T(8,128)(2,1)S(1)}, bf16[2,512,128]{2,1,0:T(8,128)(2,1)S(1)}, u32[]{:S(2)}, u32[]{:S(2)}) %collective-permute-start.5) | collective-permute-done | bytes 262176 | tf_op jit(solution)/shard_map/ppermute | solution.py:226
  126.2 6.7 %collective-permute-done.6.refs_3_ = bf16[2,512,128]{2,1,0:T(8,128)(2,1)S(1)} collective-permute-done((bf16[2,512,128]{2,1,0:T(8,128)(2,1)S(1)}, bf16[2,512,128]{2,1,0:T(8,128)(2,1)S(1)}, u32[]{:S(2)}, u32[]{:S(2)}) %collective-permute-start.6) | collective-permute-done | bytes 262176 | tf_op jit(solution)/shard_map/ppermute | solution.py:226
  132.9 0.1 shard_map.110
  133.0 3.0 %collective-permute-start.7 = (bf16[512,128]{1,0:T(8,128)(2,1)S(1)}, bf16[512,128]{1,0:T(8,128)(2,1)S(1)}, u32[]{:S(2)}, u32[]{:S(2)}) collective-permute-start(bf16[512,128]{1,0:T(8,128)(2,1)S(1)} %get-tuple-element.55), channel_id=1, source_target_pairs={{0,2},{1,3},{2,0},{3,1},{4,6},{5,7},{6,4},{7,5},{8,10},{9,11},{10,... | collective-permute-start | bytes 393224 | tf_op jit(solution)/shard_map/ppermute | solution.py:328
  136.0 3.5 %collective-permute-done.7.refs_1_ = bf16[512,128]{1,0:T(8,128)(2,1)S(1)} collective-permute-done((bf16[512,128]{1,0:T(8,128)(2,1)S(1)}, bf16[512,128]{1,0:T(8,128)(2,1)S(1)}, u32[]{:S(2)}, u32[]{:S(2)}) %collective-permute-start.7) | collective-permute-done | bytes 131104 | tf_op jit(solution)/shard_map/ppermute | solution.py:328
  139.5 0.0 all-to-all-done.3.came_ref
  139.5 1.2 copy-done.2
  140.7 1.6 %shard_map.111 = (bf16[512,512]{1,0:T(8,128)(2,1)}, bf16[512,128]{1,0:T(8,128)(2,1)}) custom-call(s32[4]{0:T(128)S(1)} %copy-done.16, s32[512]{0:T(512)S(1)} %copy-done.15, s32[96]{0:T(128)S(1)} %copy-done.17, f32[512,512]{1,0:T(8,128)S(1)} %copy-done.2, bf16[32,32,640]{2,1,0:T(8,128)(2,1)S(1)} %all-to-all-done.3.came_ref, ...), custom_call_target="tpu_custom_call" | custom-call | bytes 2883584 | tf_op jit(solution)/shard_map/pallas_call | solution.py:330
  (15 shorter events, 0.1 us)
Async XLA Ops:
  3.6 32.8 %copy-start.3 = (bf16[512,2048]{1,0:T(8,128)(2,1)S(1)}, bf16[512,2048]{1,0:T(8,128)(2,1)}, u32[]{:S(2)}) copy-start(bf16[512,2048]{1,0:T(8,128)(2,1)} %weight_ref.3) | copy-start | bytes 6291460
  3.6 32.8 %copy-start.16 = (s32[4]{0:T(128)S(1)}, s32[4]{0:T(128)}, u32[]{:S(2)}) copy-start(s32[4]{0:T(128)} %pad_add_fusion.place_ref) | copy-start | bytes 52
  3.6 52.3 %all-to-all-start = ((bf16[32,32,640]{2,1,0:T(8,128)(2,1)}), bf16[32,32,640]{2,1,0:T(8,128)(2,1)S(1)}, u32[]{:S(2)}, u32[]{:S(2)}) async-start(bf16[32,32,640]{2,1,0:T(8,128)(2,1)} %shard_map.102), calls=%async_computation | async-start | bytes 2621440 | tf_op jit(solution)/shard_map/all_to_all | solution.py:193
  34.4 16.5 %collective-permute-start.1 = (bf16[4,512,128]{2,1,0:T(8,128)(2,1)}, bf16[4,512,128]{2,1,0:T(8,128)(2,1)}, u32[]{:S(2)}, u32[]{:S(2)}) collective-permute-start(bf16[4,512,128]{2,1,0:T(8,128)(2,1)} %bitcast.4.near_ref), channel_id=1, source_target_pairs={{0,2},{1,3},{2,0},{3,1},{4,6},{5,7},{6,4},{7,5},{8,10},{9,11},{10,... | collective-permute-start | bytes 1572872 | tf_op jit(solution)/shard_map/ppermute | solution.py:251
  36.3 1.0 copy-start.11
  37.4 16.0 %copy-start.15 = (s32[512]{0:T(512)S(1)}, s32[512]{0:T(512)}, u32[]{:S(2)}) copy-start(s32[512]{0:T(512)} %index_ref.3) | copy-start | bytes 6148
  37.4 16.0 %copy-start.17 = (s32[96]{0:T(128)S(1)}, s32[96]{0:T(128)}, u32[]{:S(2)}) copy-start(s32[96]{0:T(128)} %storage_ref.3) | copy-start | bytes 1156
  37.4 18.5 %copy-start.14 = (bf16[3,64,128]{2,1,0:T(8,128)(2,1)S(1)}, bf16[3,64,128]{2,1,0:T(8,128)(2,1)}, u32[]{:S(2)}) copy-start(bf16[3,64,128]{2,1,0:T(8,128)(2,1)} %up_ref.3) | copy-start | bytes 147460
  42.5 1.0 copy-start.5
  43.5 12.4 %collective-permute-start.3 = (bf16[8,512,128]{2,1,0:T(8,128)(2,1)}, bf16[8,512,128]{2,1,0:T(8,128)(2,1)S(1)}, u32[]{:S(2)}, u32[]{:S(2)}) collective-permute-start(bf16[8,512,128]{2,1,0:T(8,128)(2,1)} %get-tuple-element.35), channel_id=1, source_target_pairs={{0,1},{1,0},{2,3},{3,2},{4,5},{5,4},{6,7},{7,6},{8,9},{9,8},{10,11... | collective-permute-start | bytes 3145736 | tf_op jit(solution)/shard_map/ppermute | solution.py:262
  49.0 4.7 %collective-permute-start = (bf16[4,512,128]{2,1,0:T(8,128)(2,1)}, bf16[4,512,128]{2,1,0:T(8,128)(2,1)S(1)}, u32[]{:S(2)}, u32[]{:S(2)}) collective-permute-start(bf16[4,512,128]{2,1,0:T(8,128)(2,1)} %bitcast.4.near_ref), channel_id=1, source_target_pairs={{0,1},{1,0},{2,3},{3,2},{4,5},{5,4},{6,7},{7,6},{8,9},{9,8},{10,11... | collective-permute-start | bytes 1572872 | tf_op jit(solution)/shard_map/ppermute | solution.py:252
  50.9 4.1 %collective-permute-start.2 = (bf16[4,512,128]{2,1,0:T(8,128)(2,1)}, bf16[4,512,128]{2,1,0:T(8,128)(2,1)S(1)}, u32[]{:S(2)}, u32[]{:S(2)}) collective-permute-start(bf16[4,512,128]{2,1,0:T(8,128)(2,1)} %collective-permute-done.1.far_ref), channel_id=1, source_target_pairs={{0,1},{1,0},{2,3},{3,2},{4,5},{5,4},{6,7},{7,6},{8,9},{9,8},{10,11... | collective-permute-start | bytes 1572872 | tf_op jit(solution)/shard_map/ppermute | solution.py:253
  55.1 0.8 copy-start.12
  55.9 5.3 %copy-start.7 = (bf16[8,512,128]{2,1,0:T(8,128)(2,1)}, bf16[8,512,128]{2,1,0:T(8,128)(2,1)S(1)}, u32[]{:S(2)}) copy-start(bf16[8,512,128]{2,1,0:T(8,128)(2,1)S(1)} %collective-permute-done.3.came_ref) | copy-start | bytes 3145732
  55.9 1.2 copy-start.9
  58.9 30.4 %copy-start.10 = (bf16[3,64,512]{2,1,0:T(8,128)(2,1)S(1)}, bf16[3,64,512]{2,1,0:T(8,128)(2,1)}, u32[]{:S(2)}) copy-start(bf16[3,64,512]{2,1,0:T(8,128)(2,1)} %down_ref.3) | copy-start | bytes 589828
  90.7 1.1 copy-start
  91.7 47.7 %all-to-all-start.3 = ((bf16[32,32,640]{2,1,0:T(8,128)(2,1)}), bf16[32,32,640]{2,1,0:T(8,128)(2,1)S(1)}, u32[]{:S(2)}, u32[]{:S(2)}) async-start(bf16[32,32,640]{2,1,0:T(8,128)(2,1)} %copy-done), calls=%async_computation.3 | async-start | bytes 2621440 | tf_op jit(solution)/shard_map/all_to_all | solution.py:193
  101.3 1.2 copy-start.6
  102.5 1.2 copy-start.8
  103.7 12.4 %copy-start.4 = (bf16[512,2048]{1,0:T(8,128)(2,1)S(1)}, bf16[512,2048]{1,0:T(8,128)(2,1)}, u32[]{:S(2)}) copy-start(bf16[512,2048]{1,0:T(8,128)(2,1)} %weight_ref.3) | copy-start | bytes 6291460
  104.0 12.1 %copy-start.13 = (bf16[4,512,128]{2,1,0:T(8,128)(2,1)S(1)}, bf16[4,512,128]{2,1,0:T(8,128)(2,1)}, u32[]{:S(2)}) copy-start(bf16[4,512,128]{2,1,0:T(8,128)(2,1)} %copy-done.12) | copy-start | bytes 1572868
  104.0 15.9 %collective-permute-start.4 = (bf16[2,512,128]{2,1,0:T(8,128)(2,1)S(1)}, bf16[2,512,128]{2,1,0:T(8,128)(2,1)S(1)}, u32[]{:S(2)}, u32[]{:S(2)}) collective-permute-start(bf16[2,512,128]{2,1,0:T(8,128)(2,1)S(1)} %get-tuple-element.41), channel_id=1, source_target_pairs={{0,8},{1,9},{2,10},{3,11},{4,12},{5,13},{6,14},{7,15},{8,0},{9,1},... | collective-permute-start | bytes 786440 | tf_op jit(solution)/shard_map/ppermute | solution.py:226
  106.3 19.9 %collective-permute-start.5 = (bf16[2,512,128]{2,1,0:T(8,128)(2,1)S(1)}, bf16[2,512,128]{2,1,0:T(8,128)(2,1)S(1)}, u32[]{:S(2)}, u32[]{:S(2)}) collective-permute-start(bf16[2,512,128]{2,1,0:T(8,128)(2,1)S(1)} %get-tuple-element.42), channel_id=1, source_target_pairs={{0,4},{1,5},{2,6},{3,7},{4,8},{5,9},{6,10},{7,11},{8,12},{9,13},{1... | collective-permute-start | bytes 786440 | tf_op jit(solution)/shard_map/ppermute | solution.py:226
  110.2 22.7 %collective-permute-start.6 = (bf16[2,512,128]{2,1,0:T(8,128)(2,1)S(1)}, bf16[2,512,128]{2,1,0:T(8,128)(2,1)S(1)}, u32[]{:S(2)}, u32[]{:S(2)}) collective-permute-start(bf16[2,512,128]{2,1,0:T(8,128)(2,1)S(1)} %get-tuple-element.43), channel_id=1, source_target_pairs={{0,12},{1,13},{2,14},{3,15},{4,0},{5,1},{6,2},{7,3},{8,4},{9,5},{1... | collective-permute-start | bytes 786440 | tf_op jit(solution)/shard_map/ppermute | solution.py:226
  118.6 1.0 copy-start.1
  133.0 6.5 %collective-permute-start.7 = (bf16[512,128]{1,0:T(8,128)(2,1)S(1)}, bf16[512,128]{1,0:T(8,128)(2,1)S(1)}, u32[]{:S(2)}, u32[]{:S(2)}) collective-permute-start(bf16[512,128]{1,0:T(8,128)(2,1)S(1)} %get-tuple-element.55), channel_id=1, source_target_pairs={{0,2},{1,3},{2,0},{3,1},{4,6},{5,7},{6,4},{7,5},{8,10},{9,11},{10,... | collective-permute-start | bytes 393224 | tf_op jit(solution)/shard_map/ppermute | solution.py:328
  139.5 1.2 copy-start.2

commit v7 on v5

--- a/solution.py
+++ b/solution.py
@@ -82,11 +82,6 @@
 def neighbour_body(keep_ref, came_ref, *out_refs):
     for b, out_ref in enumerate(out_refs):
         out_ref[...] = (keep_ref[b].astype(f32) + came_ref[b].astype(f32)).astype(bf16)
-
-
-def pack_body(*refs):
-    for b, ref in enumerate(refs[:-1]):
-        refs[-1][b] = ref[...]
 
 
 def rank_body(pick_ref, rows_ref, down_ref, up_ref, out_ref):
@@ -168,7 +163,9 @@
         low = jnp.where(first_core, own, other)
         high = jnp.where(first_core, other, own)
         pair = jnp.concatenate([low, high], axis=1)
-        columns = chip_columns(place_ref, k, 2 * blocks, 2 * width)
+        odd = lax.rem(place_ref[2] + k // blocks, 2)
+        chip = 2 * (k % blocks) + odd
+        columns = pl.ds(pl.multiple_of(chip * 2 * width, 2 * width), 2 * width)
         part = lax.dot_general(pair, weight_ref[:, columns], dims, preferred_element_type=f32)
         out_ref[...] = part if k == 0 else out_ref[...] + part
 
@@ -245,17 +242,9 @@
     swap = [(t, t ^ 1) for t in range(tensor_count)]
     across = [(t, t ^ 2) for t in range(tensor_count)]
     quarter = chips // 2
-    cot = after(cotangent, spread)
-    opposite = moved_along(cot, quarter)
-    near = local_call(
-        pack_body,
-        shape(quarter, rows, out_block),
-        [VMEM] * quarter,
-        moved=4 * quarter * rows * out_block,
-    )(cot, moved_along(cot, -2), moved_along(cot, 2), opposite)
+    alternate = [list(range(p, tensor_count, 4)) for p in range(4)]
+    near = lax.all_gather(after(cotangent, spread), "tensor", axis_index_groups=alternate)
     far = lax.ppermute(near, "tensor", across)
-    near_other = lax.ppermute(near, "tensor", swap)
-    far_other = lax.ppermute(far, "tensor", swap)
 
     own, send = local_call(
         projection_body,
@@ -264,10 +253,8 @@
         flops=2 * rows * block * tensor_count * out_block,
         moved=2 * (rows * block + 2 * block * tensor_count * out_block),
     )(after(place, near), tokens, weight)
+    arrived, far, own, send = lax.optimization_barrier((arrived, far, own, send))
     came = lax.ppermute(send, "tensor", swap)
-    arrived, near_other, far_other, own, came = lax.optimization_barrier(
-        (arrived, near_other, far_other, own, came)
-    )
 
     half = slots * length // 2
     part = local_call(
@@ -280,12 +267,13 @@
     both = lax.all_gather(part, "tensor", axis_index_groups=pairs)
     mine = lax.dynamic_slice_in_dim(both, core * half, half, axis=1)
     mine = mine.astype(f32).sum(0).astype(bf16).reshape(chips, half // chips, 2 * rank)
+    pieces, came = lax.optimization_barrier((exchange(mine, "tensor", same_core), came))
     totals = local_call(
         total_body,
         shape(*mine.shape),
         [VMEM],
         moved=4 * half * 2 * rank,
-    )(exchange(mine, "tensor", same_core))
+    )(pieces)
     shared = exchange(totals, "tensor", same_core).reshape(half, 2 * rank)
     ranks = lax.all_gather(shared, "tensor", axis_index_groups=pairs).reshape(part.shape)
 
@@ -306,7 +294,17 @@
         [VMEM, VMEM],
         moved=6 * chips * rows * out_block,
     )(after(own, contributions), came)
+    far_other = lax.ppermute(after(far, give), "tensor", swap)
+    near_other = lax.ppermute(after(near, give), "tensor", swap)
     crossed = lax.ppermute(give, "tensor", across)
+    grad_down, grad_up = local_call(
+        gradient_body,
+        (shape(held, rank, block, dtype=f32), shape(held, rank, out_block, dtype=f32)),
+        [SMEM, SMEM, VMEM, VMEM],
+        [masked, masked],
+        flops=2 * slots * length * width * held * rank,
+        moved=2 * slots * length * width,
+    )(pick, after(scale, give), ranks, arrived)
     base = local_call(
         base_body,
         shape(rows, block, dtype=f32),
@@ -314,29 +312,23 @@
         flops=2 * rows * block * tensor_count * out_block,
         moved=2 * (2 * rows * tensor_count * out_block),
     )(after(place, give), near, near_other, far, far_other, weight)
+    crossed, keep, base, grad_down, grad_up = lax.optimization_barrier(
+        (crossed, keep, base, grad_down, grad_up)
+    )
     summed = local_call(
         neighbour_body,
         (shape(rows, out_block),) * quarter,
         [VMEM, VMEM],
         moved=6 * quarter * rows * out_block,
     )(keep, crossed)
-    opposite = moved_along(summed[3], quarter)
-    parts = [summed[0], moved_along(summed[1], 2), moved_along(summed[2], -2), opposite]
-
-    grad_down, grad_up = local_call(
-        gradient_body,
-        (shape(held, rank, block, dtype=f32), shape(held, rank, out_block, dtype=f32)),
-        [SMEM, SMEM, VMEM, VMEM],
-        [masked, masked],
-        flops=2 * slots * length * width * held * rank,
-        moved=2 * slots * length * width,
-    )(pick, scale, ranks, arrived)
+    parts = [summed[0], moved_along(summed[3], quarter)]
+    parts += [moved_along(summed[1], 2), moved_along(summed[2], -2)]
+
     token_gradient, key_value_output = local_call(
         functools.partial(final_body, held),
         (shape(rows, block), shape(rows, out_block)),
         [SMEM, SMEM, SMEM, VMEM, VMEM] + [VMEM] * quarter,
         moved=2 * (3 * rows * block + slots * length * width),
-        limit=HBM_LIMIT,
     )(place, sequence_index, storage_row, base, returned, *parts)
     return (key_value_output, token_gradient, grad_down, grad_up)
 

time: 145 us -> 141 us (0.972)
  the two profiles are of different devices: /device:TPU:4 before, /device:TPU:1 now
where the time goes in v7:
time: 141 us; the launch traced here: 140 us
  blocking collectives  48.1 us (34%)
  starting transfers between devices  43 us (30%)
  waiting for transfers between devices  23.4 us (17%)
  Pallas kernels  16.3 us (12%)
  local copies, waits for them, and re-layouts  7.54 us (5%)
    all_to_all x2, blocking collectives, exchange(): lax.all_to_all(value, axis, split_axis=0, concat_axis=0, axis_index_group...  25.3 us
    all_to_all x2, starting transfers between devices, exchange(): lax.all_to_all(value, axis, split_axis=0, concat_axis=0, axis_index_group...  19.4 us
    all_gather x1, blocking collectives, on_device(): lax.all_gather(after(cotangent, spread), 'tensor', axis_index_groups=alte...  16.1 us
    ppermute x3, waiting for transfers between devices, moved_along(): return lax.ppermute(value, 'tensor', perm)  9.68 us
    ppermute x3, starting transfers between devices, moved_along(): return lax.ppermute(value, 'tensor', perm)  9.57 us
    ppermute x1, waiting for transfers between devices, on_device(): crossed = lax.ppermute(give, 'tensor', across)  7.81 us
    unnamed x34, local copies, waits for them, and re-layouts  7.46 us
    all_to_all x2, waiting for transfers between devices, exchange(): lax.all_to_all(value, axis, split_axis=0, concat_axis=0, axis_index_group...  4.73 us
  transfers between devices with their start and end apart: 10, of which 6 were waited for; matrix products, arithmetic and copies ran while one was open for 0% of the time, Pallas kernels for 8%

profile of v7, /device:TPU:1, one launch (start us, length us, event | category | flops | bytes accessed | tf_op | source)
XLA Modules:
  0.0 140.3 jit_solution(18054817903526373265)
XLA Ops:
  0.6 0.7 pad_add_fusion.place_ref
  1.3 2.3 %shard_map.102 = bf16[32,32,640]{2,1,0:T(8,128)(2,1)} custom-call(s32[4]{0:T(128)} %pad_add_fusion.place_ref, s32[512]{0:T(512)} %index_ref.3, s32[96]{0:T(128)} %storage_ref.3, bf16[512,512]{1,0:T(8,128)(2,1)} %tokens_ref.3, bf16[512,128]{1,0:T(8,128)(2,1)} %cot_ref.1), custom_call_target="tpu_custom_call" | custom-call | bytes 1966080 | tf_op jit(solution)/shard_map/pallas_call | solution.py:224
  3.6 0.0 copy-start.1
  3.6 0.0 copy-start.14
  3.6 13.8 %all-to-all-start = ((bf16[32,32,640]{2,1,0:T(8,128)(2,1)}), bf16[32,32,640]{2,1,0:T(8,128)(2,1)S(1)}, u32[]{:S(2)}, u32[]{:S(2)}) async-start(bf16[32,32,640]{2,1,0:T(8,128)(2,1)} %shard_map.102), calls=%async_computation | async-start | bytes 2621440 | tf_op jit(solution)/shard_map/all_to_all | solution.py:189
  17.5 16.1 %all-gather = bf16[2048,128]{1,0:T(8,128)(2,1)S(1)} all-gather(bf16[512,128]{1,0:T(8,128)(2,1)} %cot_ref.1), channel_id=2, replica_groups={{0,4,8,12},{1,5,9,13},{2,6,10,14},{3,7,11,15},{16,20,24,28},{17,21,25,2..., dimensions={0}, use_global_device_ids=true | all-gather | bytes 655360 | tf_op jit(solution)/shard_map/all_gather | solution.py:246
  33.5 2.6 %collective-permute-start = (bf16[4,512,128]{2,1,0:T(8,128)(2,1)S(1)}, bf16[4,512,128]{2,1,0:T(8,128)(2,1)}, u32[]{:S(2)}, u32[]{:S(2)}) collective-permute-start(bf16[4,512,128]{2,1,0:T(8,128)(2,1)S(1)} %bitcast.11), channel_id=1, source_target_pairs={{0,2},{1,3},{2,0},{3,1},{4,6},{5,7},{6,4},{7,5},{8,10},{9,11},{10,... | collective-permute-start | bytes 1572872 | tf_op jit(solution)/shard_map/ppermute | solution.py:247
  36.2 0.0 copy-done.1
  36.2 0.0 copy-done.14
  36.2 0.0 copy-start.11
  36.2 1.0 copy-done.11
  37.2 4.1 %shard_map.103 = (bf16[8,512,128]{2,1,0:T(8,128)(2,1)S(1)}, bf16[8,512,128]{2,1,0:T(8,128)(2,1)S(1)}) custom-call(s32[4]{0:T(128)S(1)} %copy-done.14, bf16[512,512]{1,0:T(8,128)(2,1)S(1)} %copy-done.11, bf16[512,2048]{1,0:T(8,128)(2,1)S(1)} %copy-done.1), custom_call_target="tpu_custom_call" | custom-call | flops 1073741824 | bytes 4718592 | tf_op jit(solution)/shard_map/pallas_call | solution.py:249
  41.4 0.0 copy-done.3
  41.4 0.0 copy-start.5
  41.4 1.0 copy-done.5
  42.4 1.0 copy-done.16
  43.3 1.2 collective-permute-done.far_ref
  44.6 4.7 %all-to-all-done.rows_ref = bf16[32,32,640]{2,1,0:T(8,128)(2,1)S(1)} async-done(((bf16[32,32,640]{2,1,0:T(8,128)(2,1)}), bf16[32,32,640]{2,1,0:T(8,128)(2,1)S(1)}, u32[]{:S(2)}, u32[]{:S(2)}) %all-to-all-start) | async-done | bytes 1310752 | tf_op jit(solution)/shard_map/all_to_all | solution.py:189
  49.3 4.6 %collective-permute-start.1 = (bf16[8,512,128]{2,1,0:T(8,128)(2,1)}, bf16[8,512,128]{2,1,0:T(8,128)(2,1)S(1)}, u32[]{:S(2)}, u32[]{:S(2)}) collective-permute-start(bf16[8,512,128]{2,1,0:T(8,128)(2,1)} %copy-done.16), channel_id=1, source_target_pairs={{0,1},{1,0},{2,3},{3,2},{4,5},{5,4},{6,7},{7,6},{8,9},{9,8},{10,11... | collective-permute-start | bytes 3145736 | tf_op jit(solution)/shard_map/ppermute | solution.py:257
  53.9 0.0 copy-done.13
  53.9 0.0 copy-done.15
  53.9 0.1 select_reduce_fusion
  54.0 0.1 sub.12
  54.1 0.1 select_reduce_fusion.1.pick_ref
  54.2 0.0 copy-done.12
  54.2 0.0 copy-start.9
  54.2 0.9 copy-done.9
  55.2 1.8 %shard_map.104 = bf16[1024,128]{1,0:T(8,128)(2,1)S(1)} custom-call(s32[32]{0:T(128)S(1)} %select_reduce_fusion.1.pick_ref, bf16[32,32,640]{2,1,0:T(8,128)(2,1)S(1)} %all-to-all-done.rows_ref, bf16[3,64,512]{2,1,0:T(8,128)(2,1)S(1)} %copy-done.9, bf16[3,64,128]{2,1,0:T(8,128)(2,1)S(1)} %copy-done.12), custom_call_target="tpu_custom_call" | custom-call | flops 251658240 | bytes 1310720 | tf_op jit(solution)/shard_map/pallas_call | solution.py:260
  57.0 0.0 copy-start.10
  57.0 2.3 %all-gather.1 = bf16[2048,128]{1,0:T(8,128)(2,1)S(1)} all-gather(bf16[1024,128]{1,0:T(8,128)(2,1)S(1)} %shard_map.104), channel_id=3, replica_groups={{0,1},{2,3},{4,5},{6,7},{8,9},{10,11},{12,13},{14,15},{16,17},{18,19},{..., dimensions={0}, use_global_device_ids=true | all-gather | bytes 786432 | tf_op jit(solution)/shard_map/all_gather | solution.py:267
  59.3 15.0 %all_to_all.20.parts_ref = bf16[8,64,128]{2,1,0:T(8,128)(2,1)S(1)} all-to-all(bf16[8,64,128]{2,1,0:T(8,128)(2,1)S(1)} %bitcast.16), channel_id=1, replica_groups={{0,2,4,6,8,10,12,14},{1,3,5,7,9,11,13,15},{16,18,20,22,24,26,28,30},{17..., dimensions={0} | all-to-all | bytes 262144 | tf_op jit(solution)/shard_map/all_to_all | solution.py:189
  74.3 0.0 collective-permute-done.1.came_ref
  74.3 10.3 %all_to_all.21 = bf16[8,64,128]{2,1,0:T(8,128)(2,1)S(1)} all-to-all(bf16[8,64,128]{2,1,0:T(8,128)(2,1)S(1)} %shard_map.105), channel_id=1, replica_groups={{0,2,4,6,8,10,12,14},{1,3,5,7,9,11,13,15},{16,18,20,22,24,26,28,30},{17..., dimensions={0} | all-to-all | bytes 262144 | tf_op jit(solution)/shard_map/all_to_all | solution.py:189
  84.7 4.4 %all_gather.19 = bf16[2,512,128]{2,1,0:T(8,128)(2,1)S(1)} all-gather(bf16[1,512,128]{2,1,0:T(8,128)(2,1)S(1)} %bitcast.15), channel_id=1, replica_groups={{0,1},{2,3},{4,5},{6,7},{8,9},{10,11},{12,13},{14,15},{16,17},{18,19},{..., dimensions={0}, use_global_device_ids=true | all-gather | bytes 393216 | tf_op jit(solution)/shard_map/all_gather | solution.py:278
  89.1 0.0 copy-done.10
  89.1 1.4 shard_map.106
  90.5 0.0 copy-done.7
  90.5 0.0 copy-start
  90.5 1.1 copy-done
  91.6 5.5 %all-to-all-start.3 = ((bf16[32,32,640]{2,1,0:T(8,128)(2,1)}), bf16[32,32,640]{2,1,0:T(8,128)(2,1)S(1)}, u32[]{:S(2)}, u32[]{:S(2)}) async-start(bf16[32,32,640]{2,1,0:T(8,128)(2,1)} %copy-done), calls=%async_computation.3 | async-start | bytes 2621440 | tf_op jit(solution)/shard_map/all_to_all | solution.py:189
  97.1 0.0 copy-start.6
  97.1 1.2 copy-done.6
  98.3 1.2 copy-done.8
  99.6 0.2 shard_map.107
  99.8 2.7 %collective-permute-start.4 = (bf16[4,512,128]{2,1,0:T(8,128)(2,1)}, bf16[4,512,128]{2,1,0:T(8,128)(2,1)S(1)}, u32[]{:S(2)}, u32[]{:S(2)}) collective-permute-start(bf16[4,512,128]{2,1,0:T(8,128)(2,1)} %collective-permute-done.far_ref), channel_id=1, source_target_pairs={{0,1},{1,0},{2,3},{3,2},{4,5},{5,4},{6,7},{7,6},{8,9},{9,8},{10,11... | collective-permute-start | bytes 1572872 | tf_op jit(solution)/shard_map/ppermute | solution.py:297
  102.5 0.0 copy-done.4
  102.5 1.9 %collective-permute-start.3 = (bf16[4,512,128]{2,1,0:T(8,128)(2,1)S(1)}, bf16[4,512,128]{2,1,0:T(8,128)(2,1)S(1)}, u32[]{:S(2)}, u32[]{:S(2)}) collective-permute-start(bf16[4,512,128]{2,1,0:T(8,128)(2,1)S(1)} %bitcast.12), channel_id=1, source_target_pairs={{0,1},{1,0},{2,3},{3,2},{4,5},{5,4},{6,7},{7,6},{8,9},{9,8},{10,11... | collective-permute-start | bytes 1572872 | tf_op jit(solution)/shard_map/ppermute | solution.py:298
  104.4 2.2 %collective-permute-start.2 = (bf16[4,512,128]{2,1,0:T(8,128)(2,1)S(1)}, bf16[4,512,128]{2,1,0:T(8,128)(2,1)S(1)}, u32[]{:S(2)}, u32[]{:S(2)}) collective-permute-start(bf16[4,512,128]{2,1,0:T(8,128)(2,1)S(1)} %get-tuple-element.44), channel_id=1, source_target_pairs={{0,2},{1,3},{2,0},{3,1},{4,6},{5,7},{6,4},{7,5},{8,10},{9,11},{10,... | collective-permute-start | bytes 1572872 | tf_op jit(solution)/shard_map/ppermute | solution.py:299
  106.6 0.1 convert_reduce_fusion
  106.8 2.4 %shard_map.109 = (f32[3,64,512]{2,1,0:T(8,128)}, f32[3,64,128]{2,1,0:T(8,128)}) custom-call(s32[32]{0:T(128)S(1)} %select_reduce_fusion.1.pick_ref, f32[3]{0:T(128)S(1)} %maximum_divide_fusion.scale_ref, bf16[1024,128]{1,0:T(8,128)(2,1)S(1)} %bitcast.10, bf16[32,32,640]{2,1,0:T(8,128)(2,1)S(1)} %all-to-all-done.rows_ref), custom_call_target="tpu_custom_call" | custom-call | flops 251658240 | bytes 1310720 | tf_op jit(solution)/shard_map/pallas_call | solution.py:300
  109.1 0.0 collective-permute-done.4.far_other_ref
  109.1 0.0 collective-permute-done.3.near_other_ref
  109.1 0.0 copy-done.2
  109.1 2.4 %shard_map.108.base_ref = f32[512,512]{1,0:T(8,128)S(1)} custom-call(s32[4]{0:T(128)S(1)} %copy-done.14, bf16[4,512,128]{2,1,0:T(8,128)(2,1)S(1)} %bitcast.13, bf16[4,512,128]{2,1,0:T(8,128)(2,1)S(1)} %collective-permute-done.3.near_other_ref, bf16[4,512,128]{2,1,0:T(8,128)(2,1)} %collective-permute-done.far_ref, ...), custom_call_target="tpu_custom_call" | custom-call | flops 1073741824 | bytes 4194304 | tf_op jit(solution)/shard_map/pallas_call | solution.py:308
  111.5 7.8 %collective-permute-done.2.came_ref = bf16[4,512,128]{2,1,0:T(8,128)(2,1)S(1)} collective-permute-done((bf16[4,512,128]{2,1,0:T(8,128)(2,1)S(1)}, bf16[4,512,128]{2,1,0:T(8,128)(2,1)S(1)}, u32[]{:S(2)}, u32[]{:S(2)}) %collective-permute-start.2) | collective-permute-done | bytes 524320 | tf_op jit(solution)/shard_map/ppermute | solution.py:299
  119.3 0.1 shard_map.110
  119.4 2.2 %collective-permute-start.5 = (bf16[512,128]{1,0:T(8,128)(2,1)S(1)}, bf16[512,128]{1,0:T(8,128)(2,1)S(1)}, u32[]{:S(2)}, u32[]{:S(2)}) collective-permute-start(bf16[512,128]{1,0:T(8,128)(2,1)S(1)} %get-tuple-element.57), channel_id=1, source_target_pairs={{0,8},{1,9},{2,10},{3,11},{4,12},{5,13},{6,14},{7,15},{8,0},{9,1},... | collective-permute-start | bytes 393224 | tf_op jit(solution)/shard_map/ppermute | solution.py:222
  121.6 3.8 %collective-permute-start.6 = (bf16[512,128]{1,0:T(8,128)(2,1)S(1)}, bf16[512,128]{1,0:T(8,128)(2,1)S(1)}, u32[]{:S(2)}, u32[]{:S(2)}) collective-permute-start(bf16[512,128]{1,0:T(8,128)(2,1)S(1)} %get-tuple-element.58), channel_id=1, source_target_pairs={{0,4},{1,5},{2,6},{3,7},{4,8},{5,9},{6,10},{7,11},{8,12},{9,13},{1... | collective-permute-start | bytes 393224 | tf_op jit(solution)/shard_map/ppermute | solution.py:222
  125.5 3.6 %collective-permute-start.7 = (bf16[512,128]{1,0:T(8,128)(2,1)S(1)}, bf16[512,128]{1,0:T(8,128)(2,1)S(1)}, u32[]{:S(2)}, u32[]{:S(2)}) collective-permute-start(bf16[512,128]{1,0:T(8,128)(2,1)S(1)} %get-tuple-element.59), channel_id=1, source_target_pairs={{0,12},{1,13},{2,14},{3,15},{4,0},{5,1},{6,2},{7,3},{8,4},{9,5},{1... | collective-permute-start | bytes 393224 | tf_op jit(solution)/shard_map/ppermute | solution.py:222
  129.0 0.4 collective-permute-done.5.refs_1_
  129.5 3.8 %collective-permute-done.6.refs_2_ = bf16[512,128]{1,0:T(8,128)(2,1)S(1)} collective-permute-done((bf16[512,128]{1,0:T(8,128)(2,1)S(1)}, bf16[512,128]{1,0:T(8,128)(2,1)S(1)}, u32[]{:S(2)}, u32[]{:S(2)}) %collective-permute-start.6) | collective-permute-done | bytes 131104 | tf_op jit(solution)/shard_map/ppermute | solution.py:222
  133.2 5.5 %collective-permute-done.7.refs_3_ = bf16[512,128]{1,0:T(8,128)(2,1)S(1)} collective-permute-done((bf16[512,128]{1,0:T(8,128)(2,1)S(1)}, bf16[512,128]{1,0:T(8,128)(2,1)S(1)}, u32[]{:S(2)}, u32[]{:S(2)}) %collective-permute-start.7) | collective-permute-done | bytes 131104 | tf_op jit(solution)/shard_map/ppermute | solution.py:222
  138.7 0.0 all-to-all-done.3.came_ref
  138.7 1.6 %shard_map.111 = (bf16[512,512]{1,0:T(8,128)(2,1)}, bf16[512,128]{1,0:T(8,128)(2,1)}) custom-call(s32[4]{0:T(128)S(1)} %copy-done.14, s32[512]{0:T(512)S(1)} %copy-done.13, s32[96]{0:T(128)S(1)} %copy-done.15, f32[512,512]{1,0:T(8,128)S(1)} %shard_map.108.base_ref, bf16[32,32,640]{2,1,0:T(8,128)(2,1)S(1)} %all-to-all-done.3.came_ref, ...), custom_call_target="tpu_custom_call" | custom-call | bytes 2883584 | tf_op jit(solution)/shard_map/pallas_call | solution.py:327
  (13 shorter events, 0.1 us)
Async XLA Ops:
  3.6 32.6 %copy-start.1 = (bf16[512,2048]{1,0:T(8,128)(2,1)S(1)}, bf16[512,2048]{1,0:T(8,128)(2,1)}, u32[]{:S(2)}) copy-start(bf16[512,2048]{1,0:T(8,128)(2,1)} %weight_ref.3) | copy-start | bytes 6291460
  3.6 32.6 %copy-start.14 = (s32[4]{0:T(128)S(1)}, s32[4]{0:T(128)}, u32[]{:S(2)}) copy-start(s32[4]{0:T(128)} %pad_add_fusion.place_ref) | copy-start | bytes 52
  3.6 45.7 %all-to-all-start = ((bf16[32,32,640]{2,1,0:T(8,128)(2,1)}), bf16[32,32,640]{2,1,0:T(8,128)(2,1)S(1)}, u32[]{:S(2)}, u32[]{:S(2)}) async-start(bf16[32,32,640]{2,1,0:T(8,128)(2,1)} %shard_map.102), calls=%async_computation | async-start | bytes 2621440 | tf_op jit(solution)/shard_map/all_to_all | solution.py:189
  33.5 7.8 %copy-start.3 = (bf16[2048,128]{1,0:T(8,128)(2,1)}, bf16[2048,128]{1,0:T(8,128)(2,1)S(1)}, u32[]{:S(2)}) copy-start(bf16[2048,128]{1,0:T(8,128)(2,1)S(1)} %all-gather) | copy-start | bytes 1572868
  33.5 11.0 %collective-permute-start = (bf16[4,512,128]{2,1,0:T(8,128)(2,1)S(1)}, bf16[4,512,128]{2,1,0:T(8,128)(2,1)}, u32[]{:S(2)}, u32[]{:S(2)}) collective-permute-start(bf16[4,512,128]{2,1,0:T(8,128)(2,1)S(1)} %bitcast.11), channel_id=1, source_target_pairs={{0,2},{1,3},{2,0},{3,1},{4,6},{5,7},{6,4},{7,5},{8,10},{9,11},{10,... | collective-permute-start | bytes 1572872 | tf_op jit(solution)/shard_map/ppermute | solution.py:247
  36.2 1.0 copy-start.11
  37.2 16.7 %copy-start.13 = (s32[512]{0:T(512)S(1)}, s32[512]{0:T(512)}, u32[]{:S(2)}) copy-start(s32[512]{0:T(512)} %index_ref.3) | copy-start | bytes 6148
  37.2 16.7 %copy-start.15 = (s32[96]{0:T(128)S(1)}, s32[96]{0:T(128)}, u32[]{:S(2)}) copy-start(s32[96]{0:T(128)} %storage_ref.3) | copy-start | bytes 1156
  37.2 17.0 %copy-start.12 = (bf16[3,64,128]{2,1,0:T(8,128)(2,1)S(1)}, bf16[3,64,128]{2,1,0:T(8,128)(2,1)}, u32[]{:S(2)}) copy-start(bf16[3,64,128]{2,1,0:T(8,128)(2,1)} %up_ref.3) | copy-start | bytes 147460
  41.4 1.0 copy-start.5
  42.4 1.0 copy-start.16
  49.3 25.0 %collective-permute-start.1 = (bf16[8,512,128]{2,1,0:T(8,128)(2,1)}, bf16[8,512,128]{2,1,0:T(8,128)(2,1)S(1)}, u32[]{:S(2)}, u32[]{:S(2)}) collective-permute-start(bf16[8,512,128]{2,1,0:T(8,128)(2,1)} %copy-done.16), channel_id=1, source_target_pairs={{0,1},{1,0},{2,3},{3,2},{4,5},{5,4},{6,7},{7,6},{8,9},{9,8},{10,11... | collective-permute-start | bytes 3145736 | tf_op jit(solution)/shard_map/ppermute | solution.py:257
  54.2 0.9 copy-start.9
  57.0 32.1 %copy-start.10 = (bf16[3,64,512]{2,1,0:T(8,128)(2,1)S(1)}, bf16[3,64,512]{2,1,0:T(8,128)(2,1)}, u32[]{:S(2)}) copy-start(bf16[3,64,512]{2,1,0:T(8,128)(2,1)} %down_ref.3) | copy-start | bytes 589828
  74.3 16.2 %copy-start.7 = (bf16[8,512,128]{2,1,0:T(8,128)(2,1)}, bf16[8,512,128]{2,1,0:T(8,128)(2,1)S(1)}, u32[]{:S(2)}) copy-start(bf16[8,512,128]{2,1,0:T(8,128)(2,1)S(1)} %collective-permute-done.1.came_ref) | copy-start | bytes 3145732
  90.5 1.1 copy-start
  91.6 10.9 %copy-start.4 = (bf16[2048,128]{1,0:T(8,128)(2,1)S(1)}, bf16[2048,128]{1,0:T(8,128)(2,1)}, u32[]{:S(2)}) copy-start(bf16[2048,128]{1,0:T(8,128)(2,1)} %copy-done.3) | copy-start | bytes 1572868
  91.6 47.1 %all-to-all-start.3 = ((bf16[32,32,640]{2,1,0:T(8,128)(2,1)}), bf16[32,32,640]{2,1,0:T(8,128)(2,1)S(1)}, u32[]{:S(2)}, u32[]{:S(2)}) async-start(bf16[32,32,640]{2,1,0:T(8,128)(2,1)} %copy-done), calls=%async_computation.3 | async-start | bytes 2621440 | tf_op jit(solution)/shard_map/all_to_all | solution.py:189
  97.1 1.2 copy-start.6
  98.3 1.2 copy-start.8
  99.6 9.6 %copy-start.2 = (bf16[512,2048]{1,0:T(8,128)(2,1)S(1)}, bf16[512,2048]{1,0:T(8,128)(2,1)}, u32[]{:S(2)}) copy-start(bf16[512,2048]{1,0:T(8,128)(2,1)} %weight_ref.3) | copy-start | bytes 6291460
  99.8 9.3 %collective-permute-start.4 = (bf16[4,512,128]{2,1,0:T(8,128)(2,1)}, bf16[4,512,128]{2,1,0:T(8,128)(2,1)S(1)}, u32[]{:S(2)}, u32[]{:S(2)}) collective-permute-start(bf16[4,512,128]{2,1,0:T(8,128)(2,1)} %collective-permute-done.far_ref), channel_id=1, source_target_pairs={{0,1},{1,0},{2,3},{3,2},{4,5},{5,4},{6,7},{7,6},{8,9},{9,8},{10,11... | collective-permute-start | bytes 1572872 | tf_op jit(solution)/shard_map/ppermute | solution.py:297
  102.5 6.6 %collective-permute-start.3 = (bf16[4,512,128]{2,1,0:T(8,128)(2,1)S(1)}, bf16[4,512,128]{2,1,0:T(8,128)(2,1)S(1)}, u32[]{:S(2)}, u32[]{:S(2)}) collective-permute-start(bf16[4,512,128]{2,1,0:T(8,128)(2,1)S(1)} %bitcast.12), channel_id=1, source_target_pairs={{0,1},{1,0},{2,3},{3,2},{4,5},{5,4},{6,7},{7,6},{8,9},{9,8},{10,11... | collective-permute-start | bytes 1572872 | tf_op jit(solution)/shard_map/ppermute | solution.py:298
  104.4 14.9 %collective-permute-start.2 = (bf16[4,512,128]{2,1,0:T(8,128)(2,1)S(1)}, bf16[4,512,128]{2,1,0:T(8,128)(2,1)S(1)}, u32[]{:S(2)}, u32[]{:S(2)}) collective-permute-start(bf16[4,512,128]{2,1,0:T(8,128)(2,1)S(1)} %get-tuple-element.44), channel_id=1, source_target_pairs={{0,2},{1,3},{2,0},{3,1},{4,6},{5,7},{6,4},{7,5},{8,10},{9,11},{10,... | collective-permute-start | bytes 1572872 | tf_op jit(solution)/shard_map/ppermute | solution.py:299
  119.4 10.0 %collective-permute-start.5 = (bf16[512,128]{1,0:T(8,128)(2,1)S(1)}, bf16[512,128]{1,0:T(8,128)(2,1)S(1)}, u32[]{:S(2)}, u32[]{:S(2)}) collective-permute-start(bf16[512,128]{1,0:T(8,128)(2,1)S(1)} %get-tuple-element.57), channel_id=1, source_target_pairs={{0,8},{1,9},{2,10},{3,11},{4,12},{5,13},{6,14},{7,15},{8,0},{9,1},... | collective-permute-start | bytes 393224 | tf_op jit(solution)/shard_map/ppermute | solution.py:222
  121.6 11.6 %collective-permute-start.6 = (bf16[512,128]{1,0:T(8,128)(2,1)S(1)}, bf16[512,128]{1,0:T(8,128)(2,1)S(1)}, u32[]{:S(2)}, u32[]{:S(2)}) collective-permute-start(bf16[512,128]{1,0:T(8,128)(2,1)S(1)} %get-tuple-element.58), channel_id=1, source_target_pairs={{0,4},{1,5},{2,6},{3,7},{4,8},{5,9},{6,10},{7,11},{8,12},{9,13},{1... | collective-permute-start | bytes 393224 | tf_op jit(solution)/shard_map/ppermute | solution.py:222
  125.5 13.2 %collective-permute-start.7 = (bf16[512,128]{1,0:T(8,128)(2,1)S(1)}, bf16[512,128]{1,0:T(8,128)(2,1)S(1)}, u32[]{:S(2)}, u32[]{:S(2)}) collective-permute-start(bf16[512,128]{1,0:T(8,128)(2,1)S(1)} %get-tuple-element.59), channel_id=1, source_target_pairs={{0,12},{1,13},{2,14},{3,15},{4,0},{5,1},{6,2},{7,3},{8,4},{9,5},{1... | collective-permute-start | bytes 393224 | tf_op jit(solution)/shard_map/ppermute | solution.py:222

commit v8 on v7

--- a/solution.py
+++ b/solution.py
@@ -274,7 +274,16 @@
         [VMEM],
         moved=4 * half * 2 * rank,
     )(pieces)
-    shared = exchange(totals, "tensor", same_core).reshape(half, 2 * rank)
+    keep, give = local_call(
+        pair_body,
+        (shape(quarter, rows, out_block),) * 2,
+        [VMEM, VMEM],
+        moved=6 * chips * rows * out_block,
+    )(after(own, totals), came)
+    shared, keep, give = lax.optimization_barrier(
+        (exchange(totals, "tensor", same_core), keep, give)
+    )
+    shared = shared.reshape(half, 2 * rank)
     ranks = lax.all_gather(shared, "tensor", axis_index_groups=pairs).reshape(part.shape)
 
     masked = pltpu.VMEM((slots * length, held * rank), bf16)
@@ -288,12 +297,7 @@
     )(pick, ranks, down, up)
     returned = exchange(contributions, "dp")
 
-    keep, give = local_call(
-        pair_body,
-        (shape(quarter, rows, out_block),) * 2,
-        [VMEM, VMEM],
-        moved=6 * chips * rows * out_block,
-    )(after(own, contributions), came)
+    keep, give, _ = lax.optimization_barrier((keep, give, contributions))
     far_other = lax.ppermute(after(far, give), "tensor", swap)
     near_other = lax.ppermute(after(near, give), "tensor", swap)
     crossed = lax.ppermute(give, "tensor", across)

time: 141 us -> 142 us (level)
  blocking collectives: 48.1 us -> 38 us
  waiting for transfers between devices: 23.4 us -> 28.1 us
  starting transfers between devices: 43 us -> 46.8 us
  local copies, waits for them, and re-layouts: 7.54 us -> 9.18 us
    all_to_all x2 -> x1, blocking collectives: 25.3 us -> 15 us  [exchange(): lax.all_to_all(value, axis, split_axis=0, concat_axis=0, axis_index_group...]
    all_to_all x2 -> x3, waiting for transfers between devices: 4.73 us -> 10.8 us  [exchange(): lax.all_to_all(value, axis, split_axis=0, concat_axis=0, axis_index_group...]
    all_to_all x2 -> x3, starting transfers between devices: 19.4 us -> 23.4 us  [exchange(): lax.all_to_all(value, axis, split_axis=0, concat_axis=0, axis_index_group...]
    unnamed x34 -> x36, local copies, waits for them, and re-layouts: 7.46 us -> 9.1 us
  transfers between devices with their start and end apart: 10 -> 11, of which waited for: 6 -> 7; matrix products, arithmetic and copies ran while one was open for 0% -> 0% of each run, Pallas kernels for 8% -> 8%
where the time goes in v8:
time: 142 us; the launch traced here: 141 us
  starting transfers between devices  46.8 us (33%)
  blocking collectives  38 us (27%)
  waiting for transfers between devices  28.1 us (20%)
  Pallas kernels  17 us (12%)
  local copies, waits for them, and re-layouts  9.18 us (6%)
    all_to_all x3, starting transfers between devices, exchange(): lax.all_to_all(value, axis, split_axis=0, concat_axis=0, axis_index_group...  23.4 us
    all_gather x1, blocking collectives, on_device(): lax.all_gather(after(cotangent, spread), 'tensor', axis_index_groups=alte...  16.1 us
    all_to_all x1, blocking collectives, exchange(): lax.all_to_all(value, axis, split_axis=0, concat_axis=0, axis_index_group...  15 us
    all_to_all x3, waiting for transfers between devices, exchange(): lax.all_to_all(value, axis, split_axis=0, concat_axis=0, axis_index_group...  10.8 us
    ppermute x3, waiting for transfers between devices, moved_along(): return lax.ppermute(value, 'tensor', perm)  9.69 us
    ppermute x3, starting transfers between devices, moved_along(): return lax.ppermute(value, 'tensor', perm)  9.56 us
    unnamed x36, local copies, waits for them, and re-layouts  9.1 us
    ppermute x1, waiting for transfers between devices, on_device(): crossed = lax.ppermute(give, 'tensor', across)  6.42 us
  transfers between devices with their start and end apart: 11, of which 7 were waited for; matrix products, arithmetic and copies ran while one was open for 0% of the time, Pallas kernels for 8%

profile of v8, /device:TPU:1, one launch (start us, length us, event | category | flops | bytes accessed | tf_op | source)
XLA Modules:
  0.0 141.1 jit_solution(17357607670942885571)
XLA Ops:
  0.6 0.7 pad_add_fusion.place_ref
  1.3 2.3 %shard_map.102 = bf16[32,32,640]{2,1,0:T(8,128)(2,1)} custom-call(s32[4]{0:T(128)} %pad_add_fusion.place_ref, s32[512]{0:T(512)} %index_ref.3, s32[96]{0:T(128)} %storage_ref.3, bf16[512,512]{1,0:T(8,128)(2,1)} %tokens_ref.3, bf16[512,128]{1,0:T(8,128)(2,1)} %cot_ref.1), custom_call_target="tpu_custom_call" | custom-call | bytes 1966080 | tf_op jit(solution)/shard_map/pallas_call | solution.py:224
  3.6 13.8 %all-to-all-start = ((bf16[32,32,640]{2,1,0:T(8,128)(2,1)}), bf16[32,32,640]{2,1,0:T(8,128)(2,1)S(1)}, u32[]{:S(2)}, u32[]{:S(2)}) async-start(bf16[32,32,640]{2,1,0:T(8,128)(2,1)} %shard_map.102), calls=%async_computation | async-start | bytes 2621440 | tf_op jit(solution)/shard_map/all_to_all | solution.py:189
  17.4 16.1 %all-gather = bf16[2048,128]{1,0:T(8,128)(2,1)S(1)} all-gather(bf16[512,128]{1,0:T(8,128)(2,1)} %cot_ref.1), channel_id=2, replica_groups={{0,4,8,12},{1,5,9,13},{2,6,10,14},{3,7,11,15},{16,20,24,28},{17,21,25,2..., dimensions={0}, use_global_device_ids=true | all-gather | bytes 655360 | tf_op jit(solution)/shard_map/all_gather | solution.py:246
  33.5 2.6 %collective-permute-start = (bf16[4,512,128]{2,1,0:T(8,128)(2,1)S(1)}, bf16[4,512,128]{2,1,0:T(8,128)(2,1)}, u32[]{:S(2)}, u32[]{:S(2)}) collective-permute-start(bf16[4,512,128]{2,1,0:T(8,128)(2,1)S(1)} %bitcast.11), channel_id=1, source_target_pairs={{0,2},{1,3},{2,0},{3,1},{4,6},{5,7},{6,4},{7,5},{8,10},{9,11},{10,... | collective-permute-start | bytes 1572872 | tf_op jit(solution)/shard_map/ppermute | solution.py:247
  36.1 0.0 copy-done.1
  36.2 0.0 copy-done.14
  36.2 0.0 copy-start.11
  36.2 1.0 copy-done.11
  37.2 4.1 %shard_map.103 = (bf16[8,512,128]{2,1,0:T(8,128)(2,1)S(1)}, bf16[8,512,128]{2,1,0:T(8,128)(2,1)S(1)}) custom-call(s32[4]{0:T(128)S(1)} %copy-done.14, bf16[512,512]{1,0:T(8,128)(2,1)S(1)} %copy-done.11, bf16[512,2048]{1,0:T(8,128)(2,1)S(1)} %copy-done.1), custom_call_target="tpu_custom_call" | custom-call | flops 1073741824 | bytes 4718592 | tf_op jit(solution)/shard_map/pallas_call | solution.py:249
  41.4 0.0 copy-done.3
  41.4 0.0 copy-start.5
  41.4 1.0 copy-done.5
  42.3 1.0 copy-done.16
  43.3 1.2 collective-permute-done.far_ref
  44.6 4.7 %all-to-all-done.rows_ref = bf16[32,32,640]{2,1,0:T(8,128)(2,1)S(1)} async-done(((bf16[32,32,640]{2,1,0:T(8,128)(2,1)}), bf16[32,32,640]{2,1,0:T(8,128)(2,1)S(1)}, u32[]{:S(2)}, u32[]{:S(2)}) %all-to-all-start) | async-done | bytes 1310752 | tf_op jit(solution)/shard_map/all_to_all | solution.py:189
  49.3 4.6 %collective-permute-start.1 = (bf16[8,512,128]{2,1,0:T(8,128)(2,1)}, bf16[8,512,128]{2,1,0:T(8,128)(2,1)S(1)}, u32[]{:S(2)}, u32[]{:S(2)}) collective-permute-start(bf16[8,512,128]{2,1,0:T(8,128)(2,1)} %copy-done.16), channel_id=1, source_target_pairs={{0,1},{1,0},{2,3},{3,2},{4,5},{5,4},{6,7},{7,6},{8,9},{9,8},{10,11... | collective-permute-start | bytes 3145736 | tf_op jit(solution)/shard_map/ppermute | solution.py:257
  53.9 0.0 copy-done.13
  53.9 0.0 copy-done.15
  53.9 0.1 select_reduce_fusion
  54.0 0.1 sub.12
  54.1 0.1 select_reduce_fusion.1.pick_ref
  54.2 0.0 copy-done.12
  54.2 0.0 copy-start.7
  54.2 0.9 copy-done.7
  55.2 1.8 %shard_map.104 = bf16[1024,128]{1,0:T(8,128)(2,1)S(1)} custom-call(s32[32]{0:T(128)S(1)} %select_reduce_fusion.1.pick_ref, bf16[32,32,640]{2,1,0:T(8,128)(2,1)S(1)} %all-to-all-done.rows_ref, bf16[3,64,512]{2,1,0:T(8,128)(2,1)S(1)} %copy-done.7, bf16[3,64,128]{2,1,0:T(8,128)(2,1)S(1)} %copy-done.12), custom_call_target="tpu_custom_call" | custom-call | flops 251658240 | bytes 1310720 | tf_op jit(solution)/shard_map/pallas_call | solution.py:260
  57.0 0.0 copy-start.6
  57.0 2.3 %all-gather.1 = bf16[2048,128]{1,0:T(8,128)(2,1)S(1)} all-gather(bf16[1024,128]{1,0:T(8,128)(2,1)S(1)} %shard_map.104), channel_id=3, replica_groups={{0,1},{2,3},{4,5},{6,7},{8,9},{10,11},{12,13},{14,15},{16,17},{18,19},{..., dimensions={0}, use_global_device_ids=true | all-gather | bytes 786432 | tf_op jit(solution)/shard_map/all_gather | solution.py:267
  59.3 15.0 %all_to_all.20.parts_ref = bf16[8,64,128]{2,1,0:T(8,128)(2,1)S(1)} all-to-all(bf16[8,64,128]{2,1,0:T(8,128)(2,1)S(1)} %bitcast.15), channel_id=1, replica_groups={{0,2,4,6,8,10,12,14},{1,3,5,7,9,11,13,15},{16,18,20,22,24,26,28,30},{17..., dimensions={0} | all-to-all | bytes 262144 | tf_op jit(solution)/shard_map/all_to_all | solution.py:189
  74.3 0.0 collective-permute-done.1.came_ref
  74.3 0.7 shard_map.105
  75.0 4.0 %all-to-all-start.2 = ((bf16[8,64,128]{2,1,0:T(8,128)(2,1)}), bf16[8,64,128]{2,1,0:T(8,128)(2,1)}, u32[]{:S(2)}, u32[]{:S(2)}) async-start(bf16[8,64,128]{2,1,0:T(8,128)(2,1)} %shard_map.105), calls=%async_computation.2 | async-start | bytes 262144 | tf_op jit(solution)/shard_map/all_to_all | solution.py:189
  79.0 0.0 copy-done.6
  79.0 0.2 shard_map.106
  79.3 0.0 copy-start.9
  79.3 0.8 copy-done.9
  80.0 0.8 copy-done.17
  80.9 6.1 %all-to-all-done.2 = bf16[8,64,128]{2,1,0:T(8,128)(2,1)} async-done(((bf16[8,64,128]{2,1,0:T(8,128)(2,1)}), bf16[8,64,128]{2,1,0:T(8,128)(2,1)}, u32[]{:S(2)}, u32[]{:S(2)}) %all-to-all-start.2) | async-done | bytes 131104 | tf_op jit(solution)/shard_map/all_to_all | solution.py:189
  86.9 4.6 %all_gather.19 = bf16[2,512,128]{2,1,0:T(8,128)(2,1)S(1)} all-gather(bf16[1,512,128]{2,1,0:T(8,128)(2,1)} %bitcast.7), channel_id=1, replica_groups={{0,1},{2,3},{4,5},{6,7},{8,9},{10,11},{12,13},{14,15},{16,17},{18,19},{..., dimensions={0}, use_global_device_ids=true | all-gather | bytes 393216 | tf_op jit(solution)/shard_map/all_gather | solution.py:287
  91.6 0.9 copy-done.8
  92.5 1.4 shard_map.107
  93.9 0.0 copy-start
  93.9 1.1 copy-done
  95.0 5.5 %all-to-all-start.3 = ((bf16[32,32,640]{2,1,0:T(8,128)(2,1)}), bf16[32,32,640]{2,1,0:T(8,128)(2,1)S(1)}, u32[]{:S(2)}, u32[]{:S(2)}) async-start(bf16[32,32,640]{2,1,0:T(8,128)(2,1)} %copy-done), calls=%async_computation.3 | async-start | bytes 2621440 | tf_op jit(solution)/shard_map/all_to_all | solution.py:189
  100.5 0.0 copy-done.4
  100.5 2.5 %collective-permute-start.3 = (bf16[4,512,128]{2,1,0:T(8,128)(2,1)S(1)}, bf16[4,512,128]{2,1,0:T(8,128)(2,1)S(1)}, u32[]{:S(2)}, u32[]{:S(2)}) collective-permute-start(bf16[4,512,128]{2,1,0:T(8,128)(2,1)S(1)} %bitcast.12), channel_id=1, source_target_pairs={{0,1},{1,0},{2,3},{3,2},{4,5},{5,4},{6,7},{7,6},{8,9},{9,8},{10,11... | collective-permute-start | bytes 1572872 | tf_op jit(solution)/shard_map/ppermute | solution.py:302
  103.1 1.9 %collective-permute-start.4 = (bf16[4,512,128]{2,1,0:T(8,128)(2,1)}, bf16[4,512,128]{2,1,0:T(8,128)(2,1)S(1)}, u32[]{:S(2)}, u32[]{:S(2)}) collective-permute-start(bf16[4,512,128]{2,1,0:T(8,128)(2,1)} %collective-permute-done.far_ref), channel_id=1, source_target_pairs={{0,1},{1,0},{2,3},{3,2},{4,5},{5,4},{6,7},{7,6},{8,9},{9,8},{10,11... | collective-permute-start | bytes 1572872 | tf_op jit(solution)/shard_map/ppermute | solution.py:301
  105.0 2.2 %collective-permute-start.2 = (bf16[4,512,128]{2,1,0:T(8,128)(2,1)}, bf16[4,512,128]{2,1,0:T(8,128)(2,1)S(1)}, u32[]{:S(2)}, u32[]{:S(2)}) collective-permute-start(bf16[4,512,128]{2,1,0:T(8,128)(2,1)} %copy-done.17), channel_id=1, source_target_pairs={{0,2},{1,3},{2,0},{3,1},{4,6},{5,7},{6,4},{7,5},{8,10},{9,11},{10,... | collective-permute-start | bytes 1572872 | tf_op jit(solution)/shard_map/ppermute | solution.py:303
  107.2 0.1 convert_reduce_fusion
  107.3 2.4 %shard_map.109 = (f32[3,64,512]{2,1,0:T(8,128)}, f32[3,64,128]{2,1,0:T(8,128)}) custom-call(s32[32]{0:T(128)S(1)} %select_reduce_fusion.1.pick_ref, f32[3]{0:T(128)S(1)} %maximum_divide_fusion.scale_ref, bf16[1024,128]{1,0:T(8,128)(2,1)S(1)} %bitcast.10, bf16[32,32,640]{2,1,0:T(8,128)(2,1)S(1)} %all-to-all-done.rows_ref), custom_call_target="tpu_custom_call" | custom-call | flops 251658240 | bytes 1310720 | tf_op jit(solution)/shard_map/pallas_call | solution.py:304
  109.7 0.0 collective-permute-done.3.near_other_ref
  109.7 0.0 collective-permute-done.4.far_other_ref
  109.7 1.6 %copy-done.2 = bf16[512,2048]{1,0:T(8,128)(2,1)S(1)} copy-done((bf16[512,2048]{1,0:T(8,128)(2,1)S(1)}, bf16[512,2048]{1,0:T(8,128)(2,1)}, u32[]{:S(2)}) %copy-start.2) | copy-done | bytes 2097176
  111.3 2.4 %shard_map.108.base_ref = f32[512,512]{1,0:T(8,128)S(1)} custom-call(s32[4]{0:T(128)S(1)} %copy-done.14, bf16[4,512,128]{2,1,0:T(8,128)(2,1)S(1)} %bitcast.13, bf16[4,512,128]{2,1,0:T(8,128)(2,1)S(1)} %collective-permute-done.3.near_other_ref, bf16[4,512,128]{2,1,0:T(8,128)(2,1)} %collective-permute-done.far_ref, ...), custom_call_target="tpu_custom_call" | custom-call | flops 1073741824 | bytes 4194304 | tf_op jit(solution)/shard_map/pallas_call | solution.py:312
  113.7 6.4 %collective-permute-done.2.came_ref = bf16[4,512,128]{2,1,0:T(8,128)(2,1)S(1)} collective-permute-done((bf16[4,512,128]{2,1,0:T(8,128)(2,1)}, bf16[4,512,128]{2,1,0:T(8,128)(2,1)S(1)}, u32[]{:S(2)}, u32[]{:S(2)}) %collective-permute-start.2) | collective-permute-done | bytes 524320 | tf_op jit(solution)/shard_map/ppermute | solution.py:303
  120.1 0.1 shard_map.110
  120.2 2.2 %collective-permute-start.5 = (bf16[512,128]{1,0:T(8,128)(2,1)S(1)}, bf16[512,128]{1,0:T(8,128)(2,1)S(1)}, u32[]{:S(2)}, u32[]{:S(2)}) collective-permute-start(bf16[512,128]{1,0:T(8,128)(2,1)S(1)} %get-tuple-element.67), channel_id=1, source_target_pairs={{0,8},{1,9},{2,10},{3,11},{4,12},{5,13},{6,14},{7,15},{8,0},{9,1},... | collective-permute-start | bytes 393224 | tf_op jit(solution)/shard_map/ppermute | solution.py:222
  122.4 3.8 %collective-permute-start.6 = (bf16[512,128]{1,0:T(8,128)(2,1)S(1)}, bf16[512,128]{1,0:T(8,128)(2,1)S(1)}, u32[]{:S(2)}, u32[]{:S(2)}) collective-permute-start(bf16[512,128]{1,0:T(8,128)(2,1)S(1)} %get-tuple-element.68), channel_id=1, source_target_pairs={{0,4},{1,5},{2,6},{3,7},{4,8},{5,9},{6,10},{7,11},{8,12},{9,13},{1... | collective-permute-start | bytes 393224 | tf_op jit(solution)/shard_map/ppermute | solution.py:222
  126.3 3.6 %collective-permute-start.7 = (bf16[512,128]{1,0:T(8,128)(2,1)S(1)}, bf16[512,128]{1,0:T(8,128)(2,1)S(1)}, u32[]{:S(2)}, u32[]{:S(2)}) collective-permute-start(bf16[512,128]{1,0:T(8,128)(2,1)S(1)} %get-tuple-element.69), channel_id=1, source_target_pairs={{0,12},{1,13},{2,14},{3,15},{4,0},{5,1},{6,2},{7,3},{8,4},{9,5},{1... | collective-permute-start | bytes 393224 | tf_op jit(solution)/shard_map/ppermute | solution.py:222
  129.8 0.4 collective-permute-done.5.refs_1_
  130.2 3.7 %collective-permute-done.6.refs_2_ = bf16[512,128]{1,0:T(8,128)(2,1)S(1)} collective-permute-done((bf16[512,128]{1,0:T(8,128)(2,1)S(1)}, bf16[512,128]{1,0:T(8,128)(2,1)S(1)}, u32[]{:S(2)}, u32[]{:S(2)}) %collective-permute-start.6) | collective-permute-done | bytes 131104 | tf_op jit(solution)/shard_map/ppermute | solution.py:222
  134.0 5.5 %collective-permute-done.7.refs_3_ = bf16[512,128]{1,0:T(8,128)(2,1)S(1)} collective-permute-done((bf16[512,128]{1,0:T(8,128)(2,1)S(1)}, bf16[512,128]{1,0:T(8,128)(2,1)S(1)}, u32[]{:S(2)}, u32[]{:S(2)}) %collective-permute-start.7) | collective-permute-done | bytes 131104 | tf_op jit(solution)/shard_map/ppermute | solution.py:222
  139.5 0.0 all-to-all-done.3.came_ref
  139.5 1.6 %shard_map.111 = (bf16[512,512]{1,0:T(8,128)(2,1)}, bf16[512,128]{1,0:T(8,128)(2,1)}) custom-call(s32[4]{0:T(128)S(1)} %copy-done.14, s32[512]{0:T(512)S(1)} %copy-done.13, s32[96]{0:T(128)S(1)} %copy-done.15, f32[512,512]{1,0:T(8,128)S(1)} %shard_map.108.base_ref, bf16[32,32,640]{2,1,0:T(8,128)(2,1)S(1)} %all-to-all-done.3.came_ref, ...), custom_call_target="tpu_custom_call" | custom-call | bytes 2883584 | tf_op jit(solution)/shard_map/pallas_call | solution.py:331
  (16 shorter events, 0.1 us)
Async XLA Ops:
  3.6 32.6 %copy-start.1 = (bf16[512,2048]{1,0:T(8,128)(2,1)S(1)}, bf16[512,2048]{1,0:T(8,128)(2,1)}, u32[]{:S(2)}) copy-start(bf16[512,2048]{1,0:T(8,128)(2,1)} %weight_ref.3) | copy-start | bytes 6291460
  3.6 32.6 %copy-start.14 = (s32[4]{0:T(128)S(1)}, s32[4]{0:T(128)}, u32[]{:S(2)}) copy-start(s32[4]{0:T(128)} %pad_add_fusion.place_ref) | copy-start | bytes 52
  3.6 45.7 %all-to-all-start = ((bf16[32,32,640]{2,1,0:T(8,128)(2,1)}), bf16[32,32,640]{2,1,0:T(8,128)(2,1)S(1)}, u32[]{:S(2)}, u32[]{:S(2)}) async-start(bf16[32,32,640]{2,1,0:T(8,128)(2,1)} %shard_map.102), calls=%async_computation | async-start | bytes 2621440 | tf_op jit(solution)/shard_map/all_to_all | solution.py:189
  33.5 7.8 %copy-start.3 = (bf16[2048,128]{1,0:T(8,128)(2,1)}, bf16[2048,128]{1,0:T(8,128)(2,1)S(1)}, u32[]{:S(2)}) copy-start(bf16[2048,128]{1,0:T(8,128)(2,1)S(1)} %all-gather) | copy-start | bytes 1572868
  33.5 11.0 %collective-permute-start = (bf16[4,512,128]{2,1,0:T(8,128)(2,1)S(1)}, bf16[4,512,128]{2,1,0:T(8,128)(2,1)}, u32[]{:S(2)}, u32[]{:S(2)}) collective-permute-start(bf16[4,512,128]{2,1,0:T(8,128)(2,1)S(1)} %bitcast.11), channel_id=1, source_target_pairs={{0,2},{1,3},{2,0},{3,1},{4,6},{5,7},{6,4},{7,5},{8,10},{9,11},{10,... | collective-permute-start | bytes 1572872 | tf_op jit(solution)/shard_map/ppermute | solution.py:247
  36.2 1.0 copy-start.11
  37.2 16.7 %copy-start.13 = (s32[512]{0:T(512)S(1)}, s32[512]{0:T(512)}, u32[]{:S(2)}) copy-start(s32[512]{0:T(512)} %index_ref.3) | copy-start | bytes 6148
  37.2 16.7 %copy-start.15 = (s32[96]{0:T(128)S(1)}, s32[96]{0:T(128)}, u32[]{:S(2)}) copy-start(s32[96]{0:T(128)} %storage_ref.3) | copy-start | bytes 1156
  37.2 17.0 %copy-start.12 = (bf16[3,64,128]{2,1,0:T(8,128)(2,1)S(1)}, bf16[3,64,128]{2,1,0:T(8,128)(2,1)}, u32[]{:S(2)}) copy-start(bf16[3,64,128]{2,1,0:T(8,128)(2,1)} %up_ref.3) | copy-start | bytes 147460
  41.4 1.0 copy-start.5
  42.3 1.0 copy-start.16
  49.3 25.0 %collective-permute-start.1 = (bf16[8,512,128]{2,1,0:T(8,128)(2,1)}, bf16[8,512,128]{2,1,0:T(8,128)(2,1)S(1)}, u32[]{:S(2)}, u32[]{:S(2)}) collective-permute-start(bf16[8,512,128]{2,1,0:T(8,128)(2,1)} %copy-done.16), channel_id=1, source_target_pairs={{0,1},{1,0},{2,3},{3,2},{4,5},{5,4},{6,7},{7,6},{8,9},{9,8},{10,11... | collective-permute-start | bytes 3145736 | tf_op jit(solution)/shard_map/ppermute | solution.py:257
  54.2 0.9 copy-start.7
  57.0 22.0 %copy-start.6 = (bf16[8,512,128]{2,1,0:T(8,128)(2,1)S(1)}, bf16[8,512,128]{2,1,0:T(8,128)(2,1)}, u32[]{:S(2)}) copy-start(bf16[8,512,128]{2,1,0:T(8,128)(2,1)} %copy-done.5) | copy-start | bytes 3145732
  75.0 11.9 %all-to-all-start.2 = ((bf16[8,64,128]{2,1,0:T(8,128)(2,1)}), bf16[8,64,128]{2,1,0:T(8,128)(2,1)}, u32[]{:S(2)}, u32[]{:S(2)}) async-start(bf16[8,64,128]{2,1,0:T(8,128)(2,1)} %shard_map.105), calls=%async_computation.2 | async-start | bytes 262144 | tf_op jit(solution)/shard_map/all_to_all | solution.py:189
  79.3 0.8 copy-start.9
  80.0 0.8 copy-start.17
  91.6 0.9 copy-start.8
  93.9 1.1 copy-start
  95.0 5.5 %copy-start.4 = (bf16[2048,128]{1,0:T(8,128)(2,1)S(1)}, bf16[2048,128]{1,0:T(8,128)(2,1)}, u32[]{:S(2)}) copy-start(bf16[2048,128]{1,0:T(8,128)(2,1)} %copy-done.3) | copy-start | bytes 1572868
  95.0 44.5 %all-to-all-start.3 = ((bf16[32,32,640]{2,1,0:T(8,128)(2,1)}), bf16[32,32,640]{2,1,0:T(8,128)(2,1)S(1)}, u32[]{:S(2)}, u32[]{:S(2)}) async-start(bf16[32,32,640]{2,1,0:T(8,128)(2,1)} %copy-done), calls=%async_computation.3 | async-start | bytes 2621440 | tf_op jit(solution)/shard_map/all_to_all | solution.py:189
  100.5 9.2 %collective-permute-start.3 = (bf16[4,512,128]{2,1,0:T(8,128)(2,1)S(1)}, bf16[4,512,128]{2,1,0:T(8,128)(2,1)S(1)}, u32[]{:S(2)}, u32[]{:S(2)}) collective-permute-start(bf16[4,512,128]{2,1,0:T(8,128)(2,1)S(1)} %bitcast.12), channel_id=1, source_target_pairs={{0,1},{1,0},{2,3},{3,2},{4,5},{5,4},{6,7},{7,6},{8,9},{9,8},{10,11... | collective-permute-start | bytes 1572872 | tf_op jit(solution)/shard_map/ppermute | solution.py:302
  103.1 6.6 %collective-permute-start.4 = (bf16[4,512,128]{2,1,0:T(8,128)(2,1)}, bf16[4,512,128]{2,1,0:T(8,128)(2,1)S(1)}, u32[]{:S(2)}, u32[]{:S(2)}) collective-permute-start(bf16[4,512,128]{2,1,0:T(8,128)(2,1)} %collective-permute-done.far_ref), channel_id=1, source_target_pairs={{0,1},{1,0},{2,3},{3,2},{4,5},{5,4},{6,7},{7,6},{8,9},{9,8},{10,11... | collective-permute-start | bytes 1572872 | tf_op jit(solution)/shard_map/ppermute | solution.py:301
  105.0 15.1 %collective-permute-start.2 = (bf16[4,512,128]{2,1,0:T(8,128)(2,1)}, bf16[4,512,128]{2,1,0:T(8,128)(2,1)S(1)}, u32[]{:S(2)}, u32[]{:S(2)}) collective-permute-start(bf16[4,512,128]{2,1,0:T(8,128)(2,1)} %copy-done.17), channel_id=1, source_target_pairs={{0,2},{1,3},{2,0},{3,1},{4,6},{5,7},{6,4},{7,5},{8,10},{9,11},{10,... | collective-permute-start | bytes 1572872 | tf_op jit(solution)/shard_map/ppermute | solution.py:303
  107.3 12.8 %copy-start.10 = (bf16[4,512,128]{2,1,0:T(8,128)(2,1)S(1)}, bf16[4,512,128]{2,1,0:T(8,128)(2,1)}, u32[]{:S(2)}) copy-start(bf16[4,512,128]{2,1,0:T(8,128)(2,1)} %copy-done.9) | copy-start | bytes 1572868
  109.7 1.6 %copy-start.2 = (bf16[512,2048]{1,0:T(8,128)(2,1)S(1)}, bf16[512,2048]{1,0:T(8,128)(2,1)}, u32[]{:S(2)}) copy-start(bf16[512,2048]{1,0:T(8,128)(2,1)} %weight_ref.3) | copy-start | bytes 6291460
  120.2 10.0 %collective-permute-start.5 = (bf16[512,128]{1,0:T(8,128)(2,1)S(1)}, bf16[512,128]{1,0:T(8,128)(2,1)S(1)}, u32[]{:S(2)}, u32[]{:S(2)}) collective-permute-start(bf16[512,128]{1,0:T(8,128)(2,1)S(1)} %get-tuple-element.67), channel_id=1, source_target_pairs={{0,8},{1,9},{2,10},{3,11},{4,12},{5,13},{6,14},{7,15},{8,0},{9,1},... | collective-permute-start | bytes 393224 | tf_op jit(solution)/shard_map/ppermute | solution.py:222
  122.4 11.6 %collective-permute-start.6 = (bf16[512,128]{1,0:T(8,128)(2,1)S(1)}, bf16[512,128]{1,0:T(8,128)(2,1)S(1)}, u32[]{:S(2)}, u32[]{:S(2)}) collective-permute-start(bf16[512,128]{1,0:T(8,128)(2,1)S(1)} %get-tuple-element.68), channel_id=1, source_target_pairs={{0,4},{1,5},{2,6},{3,7},{4,8},{5,9},{6,10},{7,11},{8,12},{9,13},{1... | collective-permute-start | bytes 393224 | tf_op jit(solution)/shard_map/ppermute | solution.py:222
  126.3 13.2 %collective-permute-start.7 = (bf16[512,128]{1,0:T(8,128)(2,1)S(1)}, bf16[512,128]{1,0:T(8,128)(2,1)S(1)}, u32[]{:S(2)}, u32[]{:S(2)}) collective-permute-start(bf16[512,128]{1,0:T(8,128)(2,1)S(1)} %get-tuple-element.69), channel_id=1, source_target_pairs={{0,12},{1,13},{2,14},{3,15},{4,0},{5,1},{6,2},{7,3},{8,4},{9,5},{1... | collective-permute-start | bytes 393224 | tf_op jit(solution)/shard_map/ppermute | solution.py:222
